TPU v7x, 32 devices: a whole 2x2x4 slice. The times are simulated.
32 devices in a mesh: pb: 4 (over y, x), pa: 4 (over z), ma: 2 (over core).
Axes of the slice: x: 2, y: 2, z: 4, core: 2. Of those that a mesh axis runs over, the one named last changes fastest.
Arguments:
- encoded: bfloat16 [4, 8, 256, 4096], P('pb', 'pa'), may hold values from -6 to 6
- key_weight: bfloat16 [4096, 2048], P('pa', 'ma'), may hold values from -0.09375 to 0.09375
- value_weight: bfloat16 [4096, 2048], P('pa', 'ma'), may hold values from -0.09375 to 0.09375
- queries: bfloat16 [4, 32, 2048], P('pb', None, 'ma')
- key_len: int32 [4, 8], P('pb', 'pa'), may hold values from 64 to 256, as said below
- retr_query: float32 [4, 768], P('pb')
- passage_ids: int32 [4, 8], P('pb'), may hold values from 0 to 3
- placement_perm: int32 [4, 4], P('pb'), may hold values from 0 to 3, each once within a row
- pool_in: bfloat16 [16, 256, 768], P(('pb', 'pa')), may hold values from -6 to 6
- pool_pre: bfloat16 [16, 256, 768], P(('pb', 'pa')), may hold values from -6 to 6
- pool_len: int32 [16], P(('pb', 'pa')), may hold values from 64 to 256, as said below
- up_weight: bfloat16 [768, 3072], P(None, 'ma'), may hold values from -0.21875 to 0.21875
- up_bias: float32 [3072], P('ma'), may hold values from -3 to 3
- down_weight: bfloat16 [768, 3072], P(None, 'ma'), may hold values from -0.109375 to 0.109375
- norm_gain: float32 [768], replicated, may hold values from 0.1 to 1.9
Outputs:
- attn_out: bfloat16 [4, 32, 2048], P('pb', None, 'ma')
- pool_grad: bfloat16 [16, 256, 768], P(('pb', 'pa'))
- up_grad: float32 [768, 3072], P(('pb', 'pa'), 'ma')
- down_grad: float32 [768, 3072], P(('pb', 'pa'), 'ma')
Inputs may be any that keep to these rules, and one draw needn't show every extreme that they name: `key_len`: at least one passage of every question has 256 tokens. `pool_len`: at least one pool passage has 256 tokens. `passage_ids`: indices into the pool of the question's own group; several reads may name the same pool passage. Each row is a permutation: pool passage k of group g is stored at position g * 4 + placement_perm[g, k].
All inputs are finite; a program needn't handle non-finite values.
Results may differ from a plain program's by a relative error of at most 0.0049.
Values may be sent and summed in bfloat16 or wider, within the bound.
No kernel may reach another device: no remote copies, remote signals or barrier semaphores. Data moves between devices by JAX's collectives and lax.ppermute only.
A program may use at most 128 MiB of HBM per device.

v0:
```python
import jax
import jax.numpy as jnp
from jax import lax
from jax.sharding import PartitionSpec as P

HEADS = 32
HDIM = 64
ANS = 32
DR = 768


loss_scale = 16384.0
highest = lax.Precision.HIGHEST


def gelu_exact(upper):
    return 0.5 * upper * (1.0 + lax.erf(upper * 0.7071067811865476))


def gelu_slope(upper):
    return (
        0.5 * (1.0 + lax.erf(upper * 0.7071067811865476))
        + upper * jnp.exp(-0.5 * upper * upper) * 0.3989422804014327
    )


def local(
    encoded,
    key_weight,
    value_weight,
    queries,
    key_len,
    retr_query,
    passage_ids,
    placement_perm,
    pool_in,
    pool_pre,
    pool_len,
    up_weight,
    up_bias,
    down_weight,
    norm_gain,
):
    q_here, p_here, tokens, width = encoded.shape
    heads_here = HEADS // lax.axis_size("ma")
    cols_here = key_weight.shape[1]
    token_rows = encoded.reshape(q_here * p_here * tokens, width)

    def add_one(piece):
        return jnp.dot(token_rows, piece, preferred_element_type=jnp.float32)

    keys = add_one(lax.all_gather(key_weight, "pa", axis=0, tiled=True))
    values = add_one(lax.all_gather(value_weight, "pa", axis=0, tiled=True))
    keys = keys.reshape(q_here, p_here * tokens, heads_here, HDIM)
    values = values.reshape(q_here, p_here * tokens, heads_here, HDIM)
    query_f = queries.astype(jnp.float32).reshape(q_here, ANS, heads_here, HDIM)
    scores = jnp.einsum("bahj,bthj->baht", query_f, keys, precision=highest)
    positions = jnp.arange(tokens, dtype=jnp.int32)
    valid = (positions[None, None, :] < key_len[:, :, None]).reshape(q_here, 1, 1, p_here * tokens)
    masked = jnp.where(valid, scores, -1e30)
    local_top = jnp.max(masked, axis=-1)
    global_top = lax.pmax(local_top, "pa")
    weights = jnp.where(valid, jnp.exp(masked - global_top[..., None]), 0.0)
    local_total = jnp.sum(weights, axis=-1)
    local_summed = jnp.einsum("baht,bthj->bahj", weights, values, precision=highest)
    totals, summed = lax.psum((local_total, local_summed), "pa")
    attn_out = (summed / totals[..., None]).astype(jnp.bfloat16).reshape(q_here, ANS, cols_here)
    shares = (weights / totals[..., None]).reshape(q_here, ANS, heads_here, p_here, tokens)
    mass_part = jnp.sum(shares, axis=(1, 2, 4)) / (ANS * HEADS)
    pre_f = pool_pre.astype(jnp.float32)
    centre = pre_f - jnp.mean(pre_f, axis=-1, keepdims=True)
    spread = jnp.mean(centre * centre, axis=-1, keepdims=True)
    inverse = 1.0 / jnp.sqrt(spread + 1e-05)
    normed = centre * inverse
    live = (positions[None, :] < pool_len[:, None]).astype(jnp.float32)
    lengths = pool_len.astype(jnp.float32)
    embed = jnp.sum(normed * norm_gain * live[..., None], axis=1) / lengths[:, None]
    ma_count = lax.axis_size("ma")
    pa_count = lax.axis_size("pa")
    pool_here = pool_in.shape[0]
    feat_half = DR // ma_count
    embed_half = lax.dynamic_slice_in_dim(embed, lax.axis_index("ma") * feat_half, feat_half, 1)
    mass_all, embed_all = (
        lax.all_gather(mass_part.T, ("pa", "ma"), axis=0, tiled=True),
        lax.all_gather(embed_half, ("pa", "ma"), axis=0, tiled=True),
    )
    mass_all = jnp.sum(mass_all.reshape(pa_count, ma_count, p_here, q_here), axis=1)
    mass_all = jnp.transpose(mass_all, (2, 0, 1)).reshape(q_here, pa_count * p_here)
    embed_all = embed_all.reshape(pa_count, ma_count, pool_here, feat_half)
    embed_all = jnp.transpose(embed_all, (0, 2, 1, 3)).reshape(pa_count * pool_here, DR)
    where_at = placement_perm[0][passage_ids]
    chosen = embed_all[where_at]
    sim = jnp.einsum("bd,bpd->bp", retr_query, chosen, precision=highest)
    p_ret = jax.nn.softmax(sim, axis=-1)
    coef = loss_scale * (p_ret - mass_all)
    owned = lax.axis_index("pa") * pool_here + jnp.arange(pool_here, dtype=jnp.int32)
    onehot = (where_at[..., None] == owned[None, None, :]).astype(jnp.float32)
    weighted = jnp.sum(onehot * coef[..., None], axis=1)
    signal = jnp.einsum("br,bd->rd", weighted, retr_query, precision=highest)
    dnorm = signal[:, None, :] * live[..., None] * norm_gain / lengths[:, None, None]
    dpre = (
        dnorm
        - jnp.mean(dnorm, axis=-1, keepdims=True)
        - normed * jnp.mean(dnorm * normed, axis=-1, keepdims=True)
    ) * inverse
    input_rows = pool_in.reshape(pool_here * tokens, DR)
    dpre_rows = dpre.reshape(pool_here * tokens, DR)
    dpre_b = dpre_rows.astype(jnp.bfloat16)
    upper = jnp.dot(input_rows, up_weight, preferred_element_type=jnp.float32) + up_bias
    act_b = gelu_exact(upper).astype(jnp.bfloat16)
    dact = jnp.dot(dpre_b, down_weight, preferred_element_type=jnp.float32)
    dup_b = (dact * gelu_slope(upper)).astype(jnp.bfloat16)
    grad_up = jnp.einsum("rd,rf->df", input_rows, dup_b, preferred_element_type=jnp.float32)
    grad_down = jnp.einsum("rd,rf->df", dpre_b, act_b, preferred_element_type=jnp.float32)
    partial_back = jnp.einsum("rf,df->rd", dup_b, up_weight, preferred_element_type=jnp.float32)
    back = lax.psum(partial_back, "ma")
    pool_grad = (dpre_rows + back).astype(jnp.bfloat16).reshape(pool_here, tokens, DR)
    up_grad, down_grad = (
        lax.psum_scatter(grad_up, ("pb", "pa"), scatter_dimension=0, tiled=True),
        lax.psum_scatter(grad_down, ("pb", "pa"), scatter_dimension=0, tiled=True),
    )
    return (attn_out, pool_grad, up_grad, down_grad)


def solution(mesh):
    return jax.shard_map(
        local,
        mesh=mesh,
        in_specs=(
            P("pb", "pa", None, None),
            P("pa", "ma"),
            P("pa", "ma"),
            P("pb", None, "ma"),
            P("pb", "pa"),
            P("pb", None),
            P("pb", None),
            P("pb", None),
            P(("pb", "pa"), None, None),
            P(("pb", "pa"), None, None),
            P(("pb", "pa")),
            P(None, "ma"),
            P("ma"),
            P(None, "ma"),
            P(),
        ),
        out_specs=(
            P("pb", None, "ma"),
            P(("pb", "pa"), None, None),
            P(("pb", "pa"), "ma"),
            P(("pb", "pa"), "ma"),
        ),
        check_vma=False,
    )
```

profile of v0, /device:TPU:0, one launch (start us, length us, event | category | flops | bytes accessed | tf_op | source)
XLA Modules:
  0.0 674.2 jit_solution(8622942334240299472)
XLA Ops:
  7.2 4.1 copy.32
  11.4 4.0 copy.31
  17.2 14.4 %all-gather.2 = f32[8,1,384]{2,1,0:T(1,128)S(1)} all-gather(f32[1,1,384]{2,1,0:T(1,128)S(1)} %reshape.459), channel_id=2, replica_groups=mesh['pb'=4,'pa'=4,'ma'=2] {'pa','ma'}, dimensions={0}, use_global_device_ids=true | all-gather | bytes 13824 | tf_op jit(solution)/shard_map/all_gather | solution.py:85
  31.9 0.6 reduce.20
  32.5 0.6 gather_fusion
  35.6 0.8 fusion.43
  36.4 1.3 fusion.39
  37.7 2.0 convolution_add_fusion
  39.6 124.3 %all-gather.8.cloned.1.call-done = bf16[4096,1024]{0,1:T(8,128)(2,1)} async-done(((bf16[1024,1024]{0,1:T(8,128)(2,1)}), bf16[4096,1024]{0,1:T(8,128)(2,1)}) %all-gather.8.cloned.1.call-update) | async-done | bytes 8388624 | tf_op jit(solution)/shard_map/all_gather | solution.py:52
  163.9 8.2 %fusion.45 = f32[512,16,64]{0,2,1:T(8,128)S(1)} fusion(bf16[512,4096,1]{1,0,2:T(8,128)(2,1)} %bitcast.87, bf16[16,64,4096]{2,1,0:T(8,128)(2,1)} %bitcast.86), kind=kOutput, calls=%fused_computation.77 | convolution fusion | flops 4294967296 | bytes 14680064 | tf_op jit(solution)/shard_map/dot_general | solution.py:50
  172.1 1.0 fusion.42
  173.2 9.3 %pmax.7 = f32[32,16]{0,1:T(8,128)S(1)} all-reduce(f32[32,16]{0,1:T(8,128)S(1)} %get-tuple-element.22), channel_id=1, replica_groups=mesh['pb'=4,'pa'=4,'ma'=2] {'pa'}, use_global_device_ids=true, to_apply=%region_1.2 | all-reduce | flops 512 | bytes 4096 | tf_op jit(solution)/shard_map/pmax | solution.py:62
  182.8 18.9 %psum.22 = f32[32,16]{0,1:T(8,128)S(1)} all-reduce(f32[32,16]{0,1:T(8,128)S(1)} %fusion.22), channel_id=1, replica_groups=mesh['pb'=4,'pa'=4,'ma'=2] {'pa'}, use_global_device_ids=true, to_apply=%region_4.5 | all-reduce | flops 512 | bytes 4096 | tf_op jit(solution)/shard_map/psum | solution.py:66
  202.2 14.2 %all-reduce = f32[16]{0:T(128)S(1)} all-reduce(f32[16]{0:T(128)S(1)} %multiply_dynamic-update-slice_fusion), channel_id=3, replica_groups=mesh['pb'=4,'pa'=4,'ma'=2] {'pa','ma'}, use_global_device_ids=true, to_apply=%add | all-reduce | flops 16 | bytes 128
  216.6 1.9 fusion.34
  218.5 0.6 broadcast_multiply_fusion
  219.2 1.4 fusion.26
  220.6 93.9 %all-gather.6.cloned.1.call-done = bf16[4096,1024]{0,1:T(8,128)(2,1)} async-done(((bf16[1024,1024]{0,1:T(8,128)(2,1)}), bf16[4096,1024]{0,1:T(8,128)(2,1)}) %all-gather.6.cloned.1.call-update) | async-done | bytes 8388624 | tf_op jit(solution)/shard_map/all_gather | solution.py:53
  314.5 8.2 %fusion.44 = f32[512,16,64]{0,2,1:T(8,128)S(1)} fusion(bf16[512,4096,1]{1,0,2:T(8,128)(2,1)} %bitcast.88, bf16[16,64,4096]{2,1,0:T(8,128)(2,1)} %bitcast.85), kind=kOutput, calls=%fused_computation.76 | convolution fusion | flops 4294967296 | bytes 14680064 | tf_op jit(solution)/shard_map/dot_general | solution.py:50
  322.7 2.8 convolution_bitcast_fusion.2
  325.8 3.4 fusion
  329.2 1.7 fusion.46
  331.0 4.7 fusion.20
  335.8 4.1 convolution_bitcast_fusion
  339.9 6.1 copy.36
  346.1 13.3 %all-reduce.4.cloned.1.call-done = f32[1,32,16,64]{3,1,2,0:T(8,128)} async-done(((f32[1,32,16,64]{3,1,2,0:T(8,128)}), f32[1,32,16,64]{3,1,2,0:T(8,128)}) %all-reduce.4.cloned.1.call-update) | async-done | bytes 131088 | tf_op jit(solution)/shard_map/psum | solution.py:66
  359.4 1.1 divide_convert_fusion
  360.5 0.8 reshape.421
  361.3 19.4 %all-reduce.6.cloned.1.call-done = f32[256,768]{1,0:T(8,128)} async-done(((f32[256,768]{1,0:T(8,128)}), f32[256,768]{1,0:T(8,128)}) %all-reduce.6.cloned.1.call-update) | async-done | bytes 786448 | tf_op jit(solution)/shard_map/psum | solution.py:116
  380.7 2.3 fusion.27
  382.9 142.2 %reduce-scatter.5.cloned.1.call-done = f32[48,1536]{1,0:T(8,128)} async-done(((f32[768,1536]{1,0:T(8,128)}), f32[48,1536]{1,0:T(8,128)}) %reduce-scatter.5.cloned.1.call-update) | async-done | bytes 294928 | tf_op jit(solution)/shard_map/reduce_scatter | solution.py:120
  525.2 142.2 %reduce-scatter.7.cloned.1.call-done = f32[48,1536]{1,0:T(8,128)} async-done(((f32[768,1536]{1,0:T(8,128)}), f32[48,1536]{1,0:T(8,128)}) %reduce-scatter.7.cloned.1.call-update) | async-done | bytes 294928
  (109 shorter events, 4.5 us)
Async XLA Ops:
  7.2 30.5 %copy-start = (bf16[768,1536]{1,0:T(8,128)(2,1)S(1)}, bf16[768,1536]{1,0:T(8,128)(2,1)}, u32[]{:S(2)}) copy-start(bf16[768,1536]{1,0:T(8,128)(2,1)} %param.26) | copy-start | bytes 7077892
  7.2 156.7 %all-gather.8.cloned.1.call-start = ((), (), s32[]{:S(2)}) async-start(), calls=%async_computation.3 | async-start | bytes 10485760 | tf_op jit(solution)/shard_map/all_gather | solution.py:52
  11.4 303.1 %all-gather.6.cloned.1.call-start = ((), (), s32[]{:S(2)}) async-start(), calls=%async_computation.2 | async-start | bytes 10485760 | tf_op jit(solution)/shard_map/all_gather | solution.py:53
  15.4 16.3 %copy-start.5 = (bf16[1,32,1024]{2,1,0:T(8,128)(2,1)S(1)}, bf16[1,32,1024]{2,1,0:T(8,128)(2,1)}, u32[]{:S(2)}) copy-start(bf16[1,32,1024]{2,1,0:T(8,128)(2,1)} %param.18) | copy-start | bytes 196612
  15.4 16.5 %copy-start.16 = (f32[1,768]{1,0:T(1,128)S(1)}, f32[1,768]{1,0:T(1,128)}, u32[]{:S(2)}) copy-start(f32[1,768]{1,0:T(1,128)} %param.20) | copy-start | bytes 9220
  15.4 17.1 %copy-start.30 = (s32[1,8]{1,0:T(1,128)S(1)}, s32[1,8]{1,0:T(1,128)}, u32[]{:S(2)}) copy-start(s32[1,8]{1,0:T(1,128)} %param.21) | copy-start | bytes 100
  15.4 17.1 %copy-start.1 = (s32[1,4]{1,0:T(1,128)S(1)}, s32[1,4]{1,0:T(1,128)}, u32[]{:S(2)}) copy-start(s32[1,4]{1,0:T(1,128)} %param.22) | copy-start | bytes 52
  15.4 18.8 %copy-start.28 = (s32[1,2]{1,0:T(1,128)S(1)}, s32[1,2]{1,0:T(1,128)}, u32[]{:S(2)}) copy-start(s32[1,2]{1,0:T(1,128)} %param.19) | copy-start | bytes 28
  15.4 18.9 %copy-start.31 = (u32[32]{0:T(128)S(1)}, u32[32]{0:T(128)}, u32[]{:S(2)}) copy-start(u32[32]{0:T(128)} %constant.60) | copy-start | bytes 388
  15.4 22.2 %copy-start.4 = (bf16[1,256,768]{2,1,0:T(8,128)(2,1)S(1)}, bf16[1,256,768]{2,1,0:T(8,128)(2,1)}, u32[]{:S(2)}) copy-start(bf16[1,256,768]{2,1,0:T(8,128)(2,1)} %param.23) | copy-start | bytes 1179652
  15.5 22.2 %copy-start.29 = (f32[1536]{0:T(1024)S(1)}, f32[1536]{0:T(1024)}, u32[]{:S(2)}) copy-start(f32[1536]{0:T(1024)} %param.27) | copy-start | bytes 18436
  15.5 343.9 %all-reduce.4.cloned.1.call-start = ((), (), s32[]{:S(2)}) async-start(), calls=%async_computation.4 | async-start | bytes 524288 | tf_op jit(solution)/shard_map/psum | solution.py:66
  16.4 23.2 %copy-start.17 = (f32[256]{0:T(256)}, f32[256]{0:T(256)S(1)}, u32[]{:S(2)}) copy-start(f32[256]{0:T(256)S(1)} %compare_convert_fusion) | copy-start | bytes 3076
  16.6 23.1 %copy-start.7 = (f32[256]{0:T(256)}, f32[256]{0:T(256)S(1)}, u32[]{:S(2)}) copy-start(f32[256]{0:T(256)S(1)} %broadcast_multiply_fusion.3) | copy-start | bytes 3076
  16.8 22.8 %copy-start.10 = (f32[256]{0:T(256)}, f32[256]{0:T(256)S(1)}, u32[]{:S(2)}) copy-start(f32[256]{0:T(256)S(1)} %add_rsqrt_fusion) | copy-start | bytes 3076
  34.3 167.3 %copy-start.14 = (pred[512]{0:T(512)(128)(4,1)}, pred[512]{0:T(512)(128)(4,1)S(1)}, u32[]{:S(2)}) copy-start(pred[512]{0:T(512)(128)(4,1)S(1)} %lt.61) | copy-start | bytes 1540
  173.1 43.5 %copy-start.25 = (f32[8]{0:T(128)S(1)}, f32[8]{0:T(128)}, u32[]{:S(2)}) copy-start(f32[8]{0:T(128)} %copy-done.24) | copy-start | bytes 100
  173.1 43.5 %copy-start.27 = (s32[8]{0:T(128)S(1)}, s32[8]{0:T(128)}, u32[]{:S(2)}) copy-start(s32[8]{0:T(128)} %copy-done.26) | copy-start | bytes 100
  173.1 45.4 %copy-start.13 = (f32[768]{0:T(1024)S(1)}, f32[768]{0:T(1024)}, u32[]{:S(2)}) copy-start(f32[768]{0:T(1024)} %reduce.20) | copy-start | bytes 9220
  173.1 46.0 %copy-start.8 = (f32[256]{0:T(256)S(1)}, f32[256]{0:T(256)}, u32[]{:S(2)}) copy-start(f32[256]{0:T(256)} %copy-done.7) | copy-start | bytes 3076
  173.1 46.0 %copy-start.11 = (f32[256]{0:T(256)S(1)}, f32[256]{0:T(256)}, u32[]{:S(2)}) copy-start(f32[256]{0:T(256)} %copy-done.10) | copy-start | bytes 3076
  173.1 46.0 %copy-start.18 = (f32[256]{0:T(256)S(1)}, f32[256]{0:T(256)}, u32[]{:S(2)}) copy-start(f32[256]{0:T(256)} %copy-done.17) | copy-start | bytes 3076
  314.5 8.2 %copy-start.15 = (pred[512]{0:T(512)(128)(4,1)S(1)}, pred[512]{0:T(512)(128)(4,1)}, u32[]{:S(2)}) copy-start(pred[512]{0:T(512)(128)(4,1)} %copy-done.14) | copy-start | bytes 1540
  325.6 55.1 %all-reduce.6.cloned.1.call-start = ((), (), s32[]{:S(2)}) async-start(), calls=%async_computation.5 | async-start | bytes 1572864 | tf_op jit(solution)/shard_map/psum | solution.py:116
  325.8 3.4 copy-start.20
  331.0 194.2 %reduce-scatter.5.cloned.1.call-start = ((), (), s32[]{:S(2)}) async-start(), calls=%async_computation.6 | async-start | bytes 5013504 | tf_op jit(solution)/shard_map/reduce_scatter | solution.py:120
  335.8 331.6 %reduce-scatter.7.cloned.1.call-start = ((), (), s32[]{:S(2)}) async-start(), calls=%async_computation.7 | async-start | bytes 5013504
  346.0 34.6 %copy-start.9 = (f32[256]{0:T(256)S(1)}, f32[256]{0:T(256)}, u32[]{:S(2)}) copy-start(f32[256]{0:T(256)} %copy-done.7) | copy-start | bytes 3076
  346.0 34.6 %copy-start.12 = (f32[256]{0:T(256)S(1)}, f32[256]{0:T(256)}, u32[]{:S(2)}) copy-start(f32[256]{0:T(256)} %copy-done.10) | copy-start | bytes 3076
  346.0 34.6 %copy-start.19 = (f32[256]{0:T(256)S(1)}, f32[256]{0:T(256)}, u32[]{:S(2)}) copy-start(f32[256]{0:T(256)} %copy-done.17) | copy-start | bytes 3076
  346.0 34.6 %copy-start.21 = (f32[256]{0:T(256)S(1)}, f32[256]{0:T(256)}, u32[]{:S(2)}) copy-start(f32[256]{0:T(256)} %copy-done.20) | copy-start | bytes 3076
  346.0 34.6 %copy-start.23 = (f32[256]{0:T(256)S(1)}, f32[256]{0:T(256)}, u32[]{:S(2)}) copy-start(f32[256]{0:T(256)} %copy-done.22) | copy-start | bytes 3076
  (6 other events, 11.4 us)
Sparse Core Ops, SparseCore 0:
  11.5 152.3 all-gather.7
  165.5 148.9 all-gather.5
  325.7 33.6 all-reduce.3
  361.7 18.9 all-reduce.5
  386.2 138.8 reduce-scatter.4
  531.6 135.7 reduce-scatter.6
where the time goes:
time: 675 us; the launch traced here: 674 us
  waiting for transfers between devices  535 us (79%)
  blocking collectives  56.8 us (8%)
  matrix products  36.8 us (5%)
  local copies, waits for them, and re-layouts  18 us (3%)
  between operations  16.1 us (2%)
  other arithmetic  10.7 us (2%)
    unnamed x7, waiting for transfers between devices  142 us
    reduce_scatter x1, waiting for transfers between devices, local(): lax.psum_scatter(grad_down, ('pb', 'pa'), scatter_dimension=0, tiled=True)  142 us
    all_gather x1, waiting for transfers between devices, local(): keys = add_one(lax.all_gather(key_weight, 'pa', axis=0, tiled=True))  124 us
    all_gather x1, waiting for transfers between devices, local(): values = add_one(lax.all_gather(value_weight, 'pa', axis=0, tiled=True))  93.9 us
    psum x1, waiting for transfers between devices, local(): back = lax.psum(partial_back, 'ma')  19.4 us
    psum x1, blocking collectives, local(): totals, summed = lax.psum((local_total, local_summed), 'pa')  18.9 us
    dot_general x2, matrix products, add_one(): return jnp.dot(token_rows, piece, preferred_element_type=jnp.float32)  16.5 us
    unnamed x72, local copies, waits for them, and re-layouts  15.5 us
  transfers between devices with their start and end apart: 6, of which 6 were waited for; matrix products, arithmetic and copies ran while one was open for 7% of the time, Pallas kernels for 0%

commit v1 on v0

v1 whole, which is shorter than its diff:
```python
import jax
import jax.numpy as jnp
from jax import lax
from jax.experimental import pallas as pl
from jax.experimental.pallas import tpu as pltpu
from jax.sharding import PartitionSpec as P

HEADS = 32
HDIM = 64
ANS = 32
DR = 768


RING_MOST = 4


loss_scale = 16384.0
highest = lax.Precision.HIGHEST


def gelu_exact(upper):
    return 0.5 * upper * (1.0 + lax.erf(upper * 0.7071067811865476))


def gelu_slope(upper):
    return (
        0.5 * (1.0 + lax.erf(upper * 0.7071067811865476))
        + upper * jnp.exp(-0.5 * upper * upper) * 0.3989422804014327
    )


def ring_order(count):
    return list(range(0, count, 2)) + [i for i in range(count - 1, 0, -1) if i % 2]


def ring_next(count):
    order = ring_order(count)
    return [(order[i], order[(i + 1) % count]) for i in range(count)]


def flip(values, bit):
    count = lax.axis_size("pb")
    return lax.ppermute(values, "pb", [(i, i ^ bit) for i in range(count)])


def after(value, *others):
    return lax.optimization_barrier((value,) + others)[0]


def plane_gather(piece, through):
    from_x = flip(piece, 1)
    from_y = flip(piece, 2)
    far = flip(from_y, 1) if through == 1 else flip(from_x, 2)
    return [piece, from_x, from_y, far]


COLUMNS = 256


def accumulate(refs, has_total, counts):
    at = 0
    total = None
    if has_total:
        total = refs[0][...]
        at = 1
    for count in counts:
        rows, parts = refs[at], refs[at + 1 : at + 1 + count]
        at += 1 + count
        start = 0
        for part in parts:
            stop = start + part.shape[0]
            term = jnp.dot(rows[:, start:stop], part[...], preferred_element_type=jnp.float32)
            total = term if total is None else total + term
            start = stop
    return total, refs[at:]


def two_terms(values):
    high = values.astype(jnp.bfloat16)
    return high, (values - high.astype(jnp.float32)).astype(jnp.bfloat16)


def projection(total, groups, finish, extra, extra_specs, out_shape, out_specs):
    arrays = [] if total is None else [total]
    wide = lambda count: pl.BlockSpec((count, COLUMNS), lambda i: (0, i))
    specs = [] if total is None else [wide(total.shape[0])]
    flops = 0
    for rows, parts in groups:
        arrays += [rows] + list(parts)
        specs += [pl.BlockSpec(rows.shape, lambda i: (0, 0))] + [wide(part.shape[0]) for part in parts]
        flops += 2 * rows.shape[0] * rows.shape[1] * parts[0].shape[1]
    counts = [len(parts) for _, parts in groups]

    def kernel(*refs):
        value, rest = accumulate(refs, total is not None, counts)
        finish(value, *rest)

    return pl.pallas_call(
        kernel,
        grid=(groups[0][1][0].shape[1] // COLUMNS,),
        in_specs=specs + list(extra_specs),
        out_specs=out_specs,
        out_shape=out_shape,
        compiler_params=pltpu.CompilerParams(vmem_limit_bytes=32 << 20),
        cost_estimate=pl.CostEstimate(flops=flops, bytes_accessed=8 << 20, transcendentals=0),
    )(*arrays, *extra)


def store(value, out_ref):
    out_ref[...] = value


def running(total, groups):
    tokens, columns = groups[0][0].shape[0], groups[0][1][0].shape[1]
    return projection(
        total,
        groups,
        store,
        (),
        (),
        jax.ShapeDtypeStruct((tokens, columns), jnp.float32),
        pl.BlockSpec((tokens, COLUMNS), lambda i: (0, i)),
    )


def scores_of(total, groups, query_blocks, valid, p_here):
    tokens = groups[0][0].shape[0]
    pairs = query_blocks.shape[1]
    blocks = groups[0][1][0].shape[1] // COLUMNS
    each = tokens // p_here

    def finish(keys, query_ref, valid_ref, weight_ref, stat_ref):
        high, low = two_terms(keys)
        query = query_ref[...]
        scores = jnp.dot(high, query, preferred_element_type=jnp.float32)
        scores = scores + jnp.dot(low, query, preferred_element_type=jnp.float32)
        alive = valid_ref[...] > 0.0
        scores = jnp.where(alive, scores, -1e30)
        top = jnp.max(scores, axis=0, keepdims=True)
        weights = jnp.where(alive, jnp.exp(scores - top), 0.0)
        weight_ref[...] = weights
        rows = [top] + [
            jnp.sum(weights[p * each : (p + 1) * each], axis=0, keepdims=True) for p in range(p_here)
        ]
        for i, row in enumerate(rows):
            stat_ref[i : i + 1, :] = row

    wide = pairs // blocks
    return projection(
        total,
        groups,
        finish,
        (query_blocks, valid),
        (
            pl.BlockSpec((COLUMNS, wide), lambda i: (0, i)),
            pl.BlockSpec((tokens, wide), lambda i: (0, 0)),
        ),
        (
            jax.ShapeDtypeStruct((tokens, pairs), jnp.float32),
            jax.ShapeDtypeStruct((1 + p_here, pairs), jnp.float32),
        ),
        (
            pl.BlockSpec((tokens, wide), lambda i: (0, i)),
            pl.BlockSpec((1 + p_here, wide), lambda i: (0, i)),
        ),
    )


def summed_of(total, groups, weights, ratio):
    tokens, pairs = weights.shape
    columns = groups[0][1][0].shape[1]
    blocks = columns // COLUMNS
    wide = pairs // blocks

    def finish(values, weight_ref, ratio_ref, out_ref):
        high, low = two_terms(values)
        w_high, w_low = two_terms(weight_ref[...] * ratio_ref[...])
        over = (((0,), (0,)), ((), ()))
        full = lax.dot_general(w_high, high, over, preferred_element_type=jnp.float32)
        full = full + lax.dot_general(w_high, low, over, preferred_element_type=jnp.float32)
        full = full + lax.dot_general(w_low, high, over, preferred_element_type=jnp.float32)
        head = lax.broadcasted_iota(jnp.int32, (ANS, COLUMNS), 1) // HDIM
        out = jnp.zeros((ANS, COLUMNS), jnp.float32)
        for h in range(COLUMNS // HDIM):
            out = jnp.where(head == h, full[h * ANS : (h + 1) * ANS], out)
        out_ref[...] = out

    return projection(
        total,
        groups,
        finish,
        (weights, ratio),
        (
            pl.BlockSpec((tokens, wide), lambda i: (0, i)),
            pl.BlockSpec((1, wide), lambda i: (0, i)),
        ),
        jax.ShapeDtypeStruct((ANS, columns), jnp.float32),
        pl.BlockSpec((ANS, COLUMNS), lambda i: (0, i)),
    )


def quarter_of(weight):
    quarter = weight.shape[0] // lax.axis_size("pb")
    return lax.dynamic_slice_in_dim(weight, lax.axis_index("pb") * quarter, quarter, 0)


def ring_step(piece):
    return lax.ppermute(piece, "pa", ring_next(lax.axis_size("pa")))


def local(
    encoded,
    key_weight,
    value_weight,
    queries,
    key_len,
    retr_query,
    passage_ids,
    placement_perm,
    pool_in,
    pool_pre,
    pool_len,
    up_weight,
    up_bias,
    down_weight,
    norm_gain,
):
    q_here, p_here, tokens, width = encoded.shape
    pb_count = lax.axis_size("pb")
    pa_count = lax.axis_size("pa")
    ma_count = lax.axis_size("ma")
    pb_at = lax.axis_index("pb")
    pa_at = lax.axis_index("pa")
    ma_at = lax.axis_index("ma")
    heads_here = HEADS // ma_count
    cols_here = key_weight.shape[1]
    depth = key_weight.shape[0]
    token_rows = encoded.reshape(p_here * tokens, width)

    order = jnp.array(ring_order(pa_count), jnp.int32)
    place = jnp.argmax(order == pa_at).astype(jnp.int32)

    def columns_of(step, quarter):
        owner = order[(place - step + pa_count) % pa_count]
        if quarter is None:
            return lax.dynamic_slice_in_dim(token_rows, owner * depth, depth, 1)
        return jnp.concatenate(
            [
                lax.dynamic_slice_in_dim(token_rows, owner * depth + (pb_at ^ q) * quarter, quarter, 1)
                for q in range(pb_count)
            ],
            axis=1,
        )

    positions = jnp.arange(tokens, dtype=jnp.int32)
    grouped = pa_count <= RING_MOST
    rows = DR // (pb_count * pa_count)
    ff_here = up_weight.shape[1]
    ma_flip = [(i, ma_count - 1 - i) for i in range(ma_count)]
    blocks = cols_here // COLUMNS
    in_block = COLUMNS // HDIM
    pairs = ANS * heads_here
    same = jnp.eye(in_block, dtype=jnp.bfloat16)
    query_blocks = jnp.einsum(
        "abgj,gh->gjbha", queries[0].reshape(ANS, blocks, in_block, HDIM), same
    ).reshape(COLUMNS, pairs)
    valid = (positions[None, :] < key_len[0][:, None]).astype(jnp.float32).reshape(-1, 1)
    valid = jnp.broadcast_to(valid, (p_here * tokens, pairs // blocks))
    if grouped:
        quarter = depth // pb_count
        own_rows = columns_of(0, None)
        other_rows = [columns_of(step, quarter) for step in range(1, pa_count)]
        first = ma_at == 0
        mine = jnp.where(first, pool_in[0], pool_pre[0])
        mine = jnp.concatenate([mine, jnp.full((16, DR), pool_len[0], jnp.bfloat16)], axis=0)

        key_slices, value_slices = [], []
        piece = quarter_of(key_weight)
        for step in range(1, pa_count):
            piece = ring_step(piece)
            key_slices.append(plane_gather(piece, 1 + step % 2))
        piece = ring_step(after(quarter_of(value_weight), piece))
        mine = after(mine, piece)
        mine = [mine] + [
            lax.ppermute(mine, "pa", [((i + s) % pa_count, i) for i in range(pa_count)])
            for s in range(1, pa_count)
        ]
        plane_ready = after(piece, key_slices[-1][1], key_slices[-1][2])
        value_slices.append(plane_gather(plane_ready, 2))
        piece = after(piece, *mine)
        for step in range(2, pa_count):
            piece = ring_step(piece)
            value_slices.append(plane_gather(piece, 2 - step % 2))

        keys = running(None, [(own_rows, [key_weight]), (other_rows[0], key_slices[0])])
        for rows_in, slices in list(zip(other_rows, key_slices))[1:-1]:
            keys = running(keys, [(rows_in, slices)])
        last_keys = (keys, [(other_rows[-1], key_slices[-1])])
    else:
        whole = lax.all_gather(key_weight, "pa", axis=0, tiled=True)
        last_keys = (None, [(token_rows, [whole])])
    weights, stats = scores_of(*last_keys, query_blocks, valid, p_here)
    own_stats = stats
    if grouped:
        mine = jnp.stack(mine)
        mine = after(mine, own_stats)
        other = lax.ppermute(mine, "ma", ma_flip)
        inputs = jnp.where(first, mine, other)[:, :tokens]
        pre = jnp.where(first, other, mine)[:, :tokens]
        lengths = mine[:, tokens, 0].astype(jnp.float32)
    else:
        inputs, pre, lengths = pool_in, pool_pre, pool_len.astype(jnp.float32)
    count = inputs.shape[0]

    if grouped:
        stats = jnp.stack(
            [stats]
            + [
                lax.ppermute(stats, "pa", [((i + s) % pa_count, i) for i in range(pa_count)])
                for s in range(1, pa_count)
            ]
        )
    else:
        stats = jnp.roll(lax.all_gather(stats, "pa", axis=0, tiled=False), -pa_at, axis=0)

    query_r = retr_query[0]
    pre_f = pre.astype(jnp.float32)
    centre = pre_f - jnp.mean(pre_f, axis=-1, keepdims=True)
    spread = jnp.mean(centre * centre, axis=-1, keepdims=True)
    inverse = 1.0 / jnp.sqrt(spread + 1e-05)
    normed = centre * inverse
    live = (positions[None, :] < lengths[:, None]).astype(jnp.float32)[..., None]
    embed = jnp.sum(normed * norm_gain * live, axis=1) / lengths[:, None]
    sims = jnp.sum(embed * query_r, axis=-1)
    dnorm = query_r * live * norm_gain / lengths[:, None, None]
    dpre = (
        dnorm
        - jnp.mean(dnorm, axis=-1, keepdims=True)
        - normed * jnp.mean(dnorm * normed, axis=-1, keepdims=True)
    ) * inverse
    dpre_b = dpre.astype(jnp.bfloat16)
    upper = jnp.einsum("krd,df->krf", inputs, up_weight, preferred_element_type=jnp.float32) + up_bias
    act_b = gelu_exact(upper).astype(jnp.bfloat16)
    dact = jnp.einsum("krd,df->krf", dpre_b, down_weight, preferred_element_type=jnp.float32)
    dup_b = (dact * gelu_slope(upper)).astype(jnp.bfloat16)
    dup_own = dup_b[0]
    dpre_own = dpre[0]
    partial_back = jnp.einsum("rf,df->rd", dup_own, up_weight, preferred_element_type=jnp.float32)
    grad_in = dpre_own + partial_back + lax.ppermute(partial_back, "ma", ma_flip)

    def own_columns(values):
        if not grouped:
            return values
        parts = values.reshape(count, tokens, pb_count, pa_count, rows)
        return lax.dynamic_index_in_dim(parts, pa_at, 3, keepdims=False).reshape(count, tokens, pb_count * rows)

    grad_up = jnp.einsum("krd,krf->kdf", own_columns(inputs), dup_b, preferred_element_type=jnp.float32)
    grad_down = jnp.einsum("krd,krf->kdf", own_columns(dpre_b), act_b, preferred_element_type=jnp.float32)

    best = jnp.max(stats[:, 0], axis=0)
    factor = jnp.exp(stats[:, 0] - best[None])
    sums_all = stats[:, 1:] * factor[:, None]
    totals = jnp.sum(sums_all, axis=(0, 1))
    mass = jnp.sum(sums_all / totals, axis=-1) / (ANS * HEADS)
    mass = mass + lax.ppermute(mass, "ma", ma_flip)
    mass = jnp.roll(mass, pa_at, axis=0).reshape(pa_count * p_here)
    if grouped:
        sims = jnp.roll(sims, pa_at)
    else:
        sims = lax.all_gather(sims, "pa", axis=0, tiled=True)
    where_at = placement_perm[0][passage_ids[0]]
    p_ret = jax.nn.softmax(sims[where_at])
    coef = loss_scale * (p_ret - mass)
    held = (jnp.arange(count, dtype=jnp.int32) + pa_at) % pa_count
    scalars = jnp.sum(jnp.where(where_at[None, :] == held[:, None], coef[None, :], 0.0), axis=1)

    pool_grad = (grad_in * scalars[0]).astype(jnp.bfloat16)[None]

    def scatter_sum(grads, bits):
        total = grads[0] * scalars[0]
        for k in range(1, count):
            total = total + grads[k] * scalars[k]
        if not grouped:
            total = jnp.transpose(total.reshape(pb_count, pa_count, rows, ff_here), (1, 0, 2, 3))
            total = lax.psum_scatter(total, "pa", scatter_dimension=0, tiled=False)
        parts = total.reshape(pb_count, rows, ff_here)
        for bit in bits:
            split = parts.reshape((-1, 2, bit if parts.shape[0] == pb_count else 1) + parts.shape[1:])
            side = (pb_at // bit) % 2
            keep = lax.dynamic_index_in_dim(split, side, 1, keepdims=False)
            give = lax.dynamic_index_in_dim(split, 1 - side, 1, keepdims=False)
            got = flip(give.astype(jnp.bfloat16), bit)
            parts = (keep + got.astype(jnp.float32)).reshape((-1,) + parts.shape[1:])
        return parts[0]

    up_grad = scatter_sum(grad_up, (1, 2))
    down_grad = scatter_sum(grad_down, (2, 1))

    if grouped:
        values_own = after(own_rows, grad_up, grad_down)
        values = running(None, [(values_own, [value_weight]), (other_rows[0], value_slices[0])])
        for rows_in, slices in list(zip(other_rows, value_slices))[1:-1]:
            values = running(values, [(rows_in, slices)])
        last_values = (values, [(other_rows[-1], value_slices[-1])])
    else:
        whole = lax.all_gather(value_weight, "pa", axis=0, tiled=True)
        last_values = (None, [(token_rows, [whole])])
    summed = summed_of(*last_values, weights, (factor[0] / totals)[None])
    if grouped:
        step = 1
        while step < pa_count:
            summed = summed + lax.ppermute(summed, "pa", [(i, i ^ step) for i in range(pa_count)])
            step *= 2
    else:
        summed = lax.psum(summed, "pa")
    attn_out = summed.astype(jnp.bfloat16).reshape(q_here, ANS, cols_here)
    return (attn_out, pool_grad, up_grad, down_grad)


def solution(mesh):
    return jax.shard_map(
        local,
        mesh=mesh,
        in_specs=(
            P("pb", "pa", None, None),
            P("pa", "ma"),
            P("pa", "ma"),
            P("pb", None, "ma"),
            P("pb", "pa"),
            P("pb", None),
            P("pb", None),
            P("pb", None),
            P(("pb", "pa"), None, None),
            P(("pb", "pa"), None, None),
            P(("pb", "pa")),
            P(None, "ma"),
            P("ma"),
            P(None, "ma"),
            P(),
        ),
        out_specs=(
            P("pb", None, "ma"),
            P(("pb", "pa"), None, None),
            P(("pb", "pa"), "ma"),
            P(("pb", "pa"), "ma"),
        ),
        check_vma=False,
    )
```

time: 675 us -> 250 us (0.37)
  waiting for transfers between devices: 535 us -> 78.2 us
  blocking collectives: 56.8 us -> 0 us
  starting transfers between devices: 0.43 us -> 49 us
  other arithmetic: 10.7 us -> 39.3 us
  Pallas kernels: 0 us -> 26.5 us
  matrix products: 36.8 us -> 13.7 us
  local copies, waits for them, and re-layouts: 18 us -> 34.1 us
  between operations: 16.1 us -> 7.26 us
    all_gather x2 -> x0, waiting for transfers between devices: 218 us -> none  [the longest x1 124 us: local(): keys = add_one(lax.all_gather(key_weight, 'pa', axis=0, tiled=True))]
    unnamed x7 -> x0, waiting for transfers between devices: 142 us -> none
    reduce_scatter x1 -> x0, waiting for transfers between devices: 142 us -> none  [local(): lax.psum_scatter(grad_down, ('pb', 'pa'), scatter_dimension=0, tiled=True)]
    ppermute x0 -> x39, waiting for transfers between devices: none -> 78.2 us  [the longest x22 38.9 us: flip(): return lax.ppermute(values, 'pb', [(i, i ^ bit) for i in range(count)])]
    ppermute x0 -> x39, starting transfers between devices: none -> 49 us  [the longest x22 24.2 us: flip(): return lax.ppermute(values, 'pb', [(i, i ^ bit) for i in range(count)])]
    psum x2 -> x0, waiting for transfers between devices: 32.7 us -> none  [the longest x1 19.4 us: local(): back = lax.psum(partial_back, 'ma')]
    pallas_call x0 -> x6, Pallas kernels: none -> 26.5 us  [projection(): pl.pallas_call(kernel, grid=(groups[0][1][0].shape[1] // COLUMNS,), in_sp...]
    dot_general x10 -> x5, matrix products: 36.8 us -> 13.7 us  [the longest x1 5.39 us: local(): jnp.einsum('krd,df->krf', dpre_b, down_weight, preferred_element_type=jnp...]
  transfers between devices with their start and end apart: 6 -> 39, of which waited for: 6 -> 14; matrix products, arithmetic and copies ran while one was open for 7% -> 31% of each run, Pallas kernels for 0% -> 11%
where the time goes in v1:
time: 250 us; the launch traced here: 248 us
  waiting for transfers between devices  78.2 us (31%)
  starting transfers between devices  49 us (20%)
  other arithmetic  39.3 us (16%)
  local copies, waits for them, and re-layouts  34.1 us (14%)
  Pallas kernels  26.5 us (11%)
  matrix products  13.7 us (5%)
  between operations  7.26 us (3%)
    ppermute x22, waiting for transfers between devices, flip(): return lax.ppermute(values, 'pb', [(i, i ^ bit) for i in range(count)])  38.9 us
    pallas_call x6, Pallas kernels, projection(): pl.pallas_call(kernel, grid=(groups[0][1][0].shape[1] // COLUMNS,), in_sp...  26.5 us
    ppermute x22, starting transfers between devices, flip(): return lax.ppermute(values, 'pb', [(i, i ^ bit) for i in range(count)])  24.2 us
    ppermute x6, waiting for transfers between devices, ring_step(): return lax.ppermute(piece, 'pa', ring_next(lax.axis_size('pa')))  21.4 us
    ppermute x6, starting transfers between devices, ring_step(): return lax.ppermute(piece, 'pa', ring_next(lax.axis_size('pa')))  15.6 us
    ppermute x2, waiting for transfers between devices, local(): lax.ppermute(summed, 'pa', [(i, i ^ step) for i in range(pa_count)])  8.55 us
    ppermute x3, waiting for transfers between devices, local(): lax.ppermute(mine, 'pa', [((i + s) % pa_count, i) for i in range(pa_count)])  7.97 us
    unnamed x59, local copies, waits for them, and re-layouts  6.99 us
  transfers between devices with their start and end apart: 39, of which 14 were waited for; matrix products, arithmetic and copies ran while one was open for 31% of the time, Pallas kernels for 11%

profile of v1, /device:TPU:0, one launch (start us, length us, event | category | flops | bytes accessed | tf_op | source)
XLA Modules:
  0.0 248.1 jit_solution(16693214329887137299)
XLA Ops:
  1.9 4.1 %collective-permute-start = (bf16[256,1024]{1,0:T(8,128)(2,1)S(1)}, bf16[256,1024]{1,0:T(8,128)(2,1)}, u32[]{:S(2)}, u32[]{:S(2)}) collective-permute-start(bf16[256,1024]{1,0:T(8,128)(2,1)S(1)} %constant_dynamic-slice_fusion.15), channel_id=1, source_target_pairs={{0,4},{4,6},{6,2},{2,0},{1,5},{5,7},{7,3},{3,1},{8,12},{12,14},{14... | collective-permute-start | bytes 1572872 | tf_op jit(solution)/shard_map/ppermute | solution.py:208
  22.5 3.2 %constant_dynamic-slice_fusion.6 = (bf16[512,256]{1,0:T(8,128)(2,1)}, bf16[512,256]{1,0:T(8,128)(2,1)}, bf16[512,256]{1,0:T(8,128)(2,1)}, bf16[512,256]{1,0:T(8,...) fusion(bf16[512,4096]{1,0:T(8,128)(2,1)} %bitcast.96, ...), kind=kLoop, calls=%fused_computation.88 | loop fusion | bytes 6291504 | tf_op jit(solution)/shard_map/dynamic_slice | solution.py:249
  25.7 6.3 %collective-permute-done.1.refs_2_ = bf16[256,1024]{1,0:T(8,128)(2,1)} collective-permute-done((bf16[256,1024]{1,0:T(8,128)(2,1)}, bf16[256,1024]{1,0:T(8,128)(2,1)}, u32[]{:S(2)}, u32[]{:S(2)}) %collective-permute-start.1) | collective-permute-done | bytes 524320 | tf_op jit(solution)/shard_map/ppermute | solution.py:208
  32.0 2.7 %collective-permute-start.2 = (bf16[256,1024]{1,0:T(8,128)(2,1)}, bf16[256,1024]{1,0:T(8,128)(2,1)}, u32[]{:S(2)}, u32[]{:S(2)}) collective-permute-start(bf16[256,1024]{1,0:T(8,128)(2,1)} %collective-permute-done.1.refs_2_), channel_id=1, source_target_pairs={{0,4},{4,6},{6,2},{2,0},{1,5},{5,7},{7,3},{3,1},{8,12},{12,14},{14... | collective-permute-start | bytes 1572872 | tf_op jit(solution)/shard_map/ppermute | solution.py:208
  41.2 3.6 %collective-permute-done.2.refs_2_ = bf16[256,1024]{1,0:T(8,128)(2,1)} collective-permute-done((bf16[256,1024]{1,0:T(8,128)(2,1)}, bf16[256,1024]{1,0:T(8,128)(2,1)}, u32[]{:S(2)}, u32[]{:S(2)}) %collective-permute-start.2) | collective-permute-done | bytes 524320 | tf_op jit(solution)/shard_map/ppermute | solution.py:208
  44.8 3.0 %collective-permute-start.3 = (bf16[256,1024]{1,0:T(8,128)(2,1)}, bf16[256,1024]{1,0:T(8,128)(2,1)}, u32[]{:S(2)}, u32[]{:S(2)}) collective-permute-start(bf16[256,1024]{1,0:T(8,128)(2,1)} %constant_dynamic-slice_fusion.16), channel_id=1, source_target_pairs={{0,4},{4,6},{6,2},{2,0},{1,5},{5,7},{7,3},{3,1},{8,12},{12,14},{14... | collective-permute-start | bytes 1572872 | tf_op jit(solution)/shard_map/ppermute | solution.py:208
  53.8 10.0 %collective-permute-done.11.refs_4_ = bf16[256,1024]{1,0:T(8,128)(2,1)} collective-permute-done((bf16[256,1024]{1,0:T(8,128)(2,1)}, bf16[256,1024]{1,0:T(8,128)(2,1)}, u32[]{:S(2)}, u32[]{:S(2)}) %collective-permute-start.11) | collective-permute-done | bytes 524320 | tf_op jit(solution)/shard_map/ppermute | solution.py:43
  71.7 3.3 %collective-permute-done.9.refs_6_ = bf16[256,1024]{1,0:T(8,128)(2,1)} collective-permute-done((bf16[256,1024]{1,0:T(8,128)(2,1)}, bf16[256,1024]{1,0:T(8,128)(2,1)}, u32[]{:S(2)}, u32[]{:S(2)}) %collective-permute-start.9) | collective-permute-done | bytes 524320 | tf_op jit(solution)/shard_map/ppermute | solution.py:43
  89.8 4.6 %shard_map.183.refs_0_ = f32[512,1024]{1,0:T(8,128)S(1)} custom-call(bf16[512,1024]{1,0:T(8,128)(2,1)S(1)} %copy-done.3, bf16[1024,1024]{1,0:T(8,128)(2,1)S(1)} %copy-done.7, bf16[512,1024]{1,0:T(8,128)(2,1)S(1)} %copy-done.5, bf16[256,1024]{1,0:T(8,128)(2,1)} %collective-permute-done.refs_3_, bf16[256,1024]{1,0:T(8,128)(2,1)} %collective-permute-done.7.refs_4_, ...), custom_call_target="tpu_custom_call" | custom-call | flops 2147483648 | bytes 8388608 | tf_op jit(solution)/shard_map/pallas_call | solution.py:98
  95.0 3.8 %shard_map.184.refs_0_ = f32[512,1024]{1,0:T(8,128)S(1)} custom-call(f32[512,1024]{1,0:T(8,128)S(1)} %shard_map.183.refs_0_, bf16[512,1024]{1,0:T(8,128)(2,1)S(1)} %get-tuple-element.53.refs_1_, bf16[256,1024]{1,0:T(8,128)(2,1)} %collective-permute-done.1.refs_2_, bf16[256,1024]{1,0:T(8,128)(2,1)} %collective-permute-done.10.refs_3_, ...), custom_call_target="tpu_custom_call" | custom-call | flops 1073741824 | bytes 8388608 | tf_op jit(solution)/shard_map/pallas_call | solution.py:98
  98.8 8.0 %collective-permute-done.5 = bf16[272,768]{1,0:T(8,128)(2,1)} collective-permute-done((bf16[272,768]{1,0:T(8,128)(2,1)}, bf16[272,768]{1,0:T(8,128)(2,1)}, u32[]{:S(2)}, u32[]{:S(2)}) %collective-permute-start.5) | collective-permute-done | bytes 417824 | tf_op jit(solution)/shard_map/ppermute | solution.py:285
  106.8 2.8 %pad_maximum_fusion = bf16[4,272,768]{2,1,0:T(8,128)(2,1)} fusion(bf16[1,272,768]{2,1,0:T(8,128)(2,1)} %bitcast.7, bf16[1,272,768]{2,1,0:T(8,128)(2,1)} %bitcast.6, bf16[1,272,768]{2,1,0:T(8,128)(2,1)} %bitcast.5, bf16[1,272,768]{2,1,0:T(8,128)(2,1)} %bitcast.4), kind=kLoop, calls=%fused_computation.32 | loop fusion | flops 2506752 | bytes 3342336 | tf_op jit(solution)/shard_map/stack | solution.py:305
  109.8 5.1 %shard_map.185 = (f32[512,512]{1,0:T(8,128)S(1)}, f32[3,512]{1,0:T(4,128)S(1)}) custom-call(f32[512,1024]{1,0:T(8,128)S(1)} %shard_map.184.refs_0_, bf16[512,1024]{1,0:T(8,128)(2,1)S(1)} %copy-done.1, bf16[256,1024]{1,0:T(8,128)(2,1)} %collective-permute-done.2.refs_2_, bf16[256,1024]{1,0:T(8,128)(2,1)} %collective-permute-done.13.refs_3_, ...), custom_call_target="tpu_custom_call" | custom-call | flops 1073741824 | bytes 8388608 | tf_op jit(solution)/shard_map/pallas_call | solution.py:98
  124.3 11.6 %collective-permute-done.20.refs_2_ = bf16[256,1024]{1,0:T(8,128)(2,1)} collective-permute-done((bf16[256,1024]{1,0:T(8,128)(2,1)}, bf16[256,1024]{1,0:T(8,128)(2,1)}, u32[]{:S(2)}, u32[]{:S(2)}) %collective-permute-start.20) | collective-permute-done | bytes 524320 | tf_op jit(solution)/shard_map/ppermute | solution.py:208
  141.1 7.3 %collective-permute-done.21.refs_3_ = bf16[256,1024]{1,0:T(8,128)(2,1)} collective-permute-done((bf16[256,1024]{1,0:T(8,128)(2,1)}, bf16[256,1024]{1,0:T(8,128)(2,1)}, u32[]{:S(2)}, u32[]{:S(2)}) %collective-permute-start.21) | collective-permute-done | bytes 524320 | tf_op jit(solution)/shard_map/ppermute | solution.py:43
  151.1 2.4 convert_reduce_fusion
  161.1 3.9 %fusion.54 = (bf16[4,256,768]{2,1,0:T(8,128)(2,1)}, f32[4,256,768]{2,1,0:T(8,128)}) fusion(f32[4,256]{1,0:T(4,128)S(1)} %broadcast_multiply_fusion, f32[4,256]{1,0:T(4,128)S(1)} %add_rsqrt_fusion, f32[4,256]{1,0:T(4,128)S(1)} %broadcast_multiply_fusion.1, bf16[4,256,768]{2,1,0:T(8,128)(2,1)} %copy-done.14, f32[4,256]{1,0:T(4,128)S(1)} %broadcast_multiply_fusion.2, ...), kind=kLoop, calls=%fused_computation.137 | loop fusion | flops 8650752 | bytes 6318096 | tf_op jit(solution)/shard_map/convert_element_type | solution.py:341
  165.0 2.6 %copy.38 = bf16[4,256,768]{1,2,0:T(8,128)(2,1)} copy(bf16[4,256,768]{2,1,0:T(8,128)(2,1)} %get-tuple-element.29) | data formatting | bytes 3145728 | tf_op jit(solution)/shard_map/convert_element_type | solution.py:341
  167.6 3.2 %broadcast_select_fusion.1 = bf16[4,256,768]{2,1,0:T(8,128)(2,1)} fusion(pred[]{:T(512)S(6)} %eq.45, bf16[4,272,768]{2,1,0:T(8,128)(2,1)} %collective-permute-done.16, bf16[4,272,768]{2,1,0:T(8,128)(2,1)} %pad_maximum_fusion), kind=kLoop, calls=%fused_computation.34 | loop fusion | flops 786432 | bytes 4718593 | tf_op jit(solution)/shard_map/jit(_where)/select_n | solution.py:308
  170.8 2.6 %copy.37 = bf16[4,256,768]{1,2,0:T(8,128)(2,1)} copy(bf16[4,256,768]{2,1,0:T(8,128)(2,1)} %broadcast_select_fusion.1) | data formatting | bytes 3145728 | tf_op jit(solution)/shard_map/slice | solution.py:308
  173.4 4.0 %fusion.20 = f32[4,256,1536]{2,1,0:T(8,128)S(1)} fusion(bf16[4,256,768]{2,1,0:T(8,128)(2,1)} %broadcast_select_fusion.1, bf16[768,1536]{1,0:T(8,128)(2,1)S(1)} %copy-done), kind=kOutput, calls=%fused_computation.28 | convolution fusion | flops 2415919104 | bytes 10223616 | tf_op jit(solution)/shard_map/krd,df->krf/dot_general | solution.py:342
  178.5 2.7 %fusion.17 = f32[4,192,1536]{2,1,0:T(8,128)S(1)} fusion(bf16[4,256,192]{1,2,0:T(8,128)(2,1)S(1)} %bitcast.104, f32[4,256,1536]{2,1,0:T(8,128)S(1)} %fusion.20, f32[1536]{0:T(1024)S(1)} %copy-done.25), kind=kOutput, calls=%fused_computation.24 | convolution fusion | flops 613416960 | bytes 11409408 | tf_op jit(solution)/shard_map/krd,krf->kdf/dot_general | solution.py:358
  181.2 5.4 %fusion.5 = bf16[4,256,1536]{2,1,0:T(8,128)(2,1)S(1)} fusion(f32[4,256,1536]{2,1,0:T(8,128)S(1)} %fusion.20, bf16[4,256,768]{2,1,0:T(8,128)(2,1)S(1)} %copy-done.15, f32[1536]{0:T(1024)S(1)} %copy-done.25, bf16[768,1536]{1,0:T(8,128)(2,1)S(1)} %copy-done.28), kind=kOutput, calls=%fused_computation.8 | convolution fusion | flops 2433220608 | bytes 13375488 | tf_op jit(solution)/shard_map/krd,df->krf/dot_general | solution.py:344
  188.4 3.0 %fusion.24 = f32[1,192,1536]{2,1,0:T(8,128)S(1)} fusion(f32[4,192,1536]{2,1,0:T(8,128)S(1)} %fusion.17, f32[]{:T(128)} %bitcast.35, f32[]{:T(128)} %bitcast.34, f32[]{:T(128)} %bitcast.33, f32[]{:T(128)} %bitcast.31), kind=kLoop, calls=%fused_computation.36 | loop fusion | flops 2064384 | bytes 5898256 | tf_op jit(solution)/shard_map/add | solution.py:382
  191.4 3.0 %fusion.27 = f32[1,192,1536]{2,1,0:T(8,128)S(1)} fusion(f32[4,192,1536]{2,1,0:T(8,128)S(1)} %fusion.58, f32[]{:T(128)} %bitcast.35, f32[]{:T(128)} %bitcast.34, f32[]{:T(128)} %bitcast.33, f32[]{:T(128)} %bitcast.31), kind=kLoop, calls=%fused_computation.43 | loop fusion | flops 2064384 | bytes 5898256 | tf_op jit(solution)/shard_map/add | solution.py:382
  198.9 4.7 %shard_map.186.refs_0_ = f32[512,1024]{1,0:T(8,128)S(1)} custom-call(bf16[512,1024]{1,0:T(8,128)(2,1)S(1)} %copy-done.4, bf16[1024,1024]{1,0:T(8,128)(2,1)S(1)} %copy-done.8, bf16[512,1024]{1,0:T(8,128)(2,1)S(1)} %copy-done.6, bf16[256,1024]{1,0:T(8,128)(2,1)} %collective-permute-done.3.refs_3_, bf16[256,1024]{1,0:T(8,128)(2,1)} %collective-permute-done.17.refs_4_, ...), custom_call_target="tpu_custom_call" | custom-call | flops 2147483648 | bytes 8388608 | tf_op jit(solution)/shard_map/pallas_call | solution.py:98
  204.4 3.8 %shard_map.187.refs_0_ = f32[512,1024]{1,0:T(8,128)S(1)} custom-call(f32[512,1024]{1,0:T(8,128)S(1)} %shard_map.186.refs_0_, bf16[512,1024]{1,0:T(8,128)(2,1)S(1)} %get-tuple-element.53.refs_1_, bf16[256,1024]{1,0:T(8,128)(2,1)} %collective-permute-done.20.refs_2_, bf16[256,1024]{1,0:T(8,128)(2,1)} %collective-permute-done.21.refs_3_, ...), custom_call_target="tpu_custom_call" | custom-call | flops 1073741824 | bytes 8388608 | tf_op jit(solution)/shard_map/pallas_call | solution.py:98
  209.7 15.8 %collective-permute-done.35 = bf16[2,1,48,1536]{3,2,1,0:T(8,128)(2,1)S(1)} collective-permute-done((bf16[2,1,48,1536]{3,2,1,0:T(8,128)(2,1)S(1)}, bf16[2,1,48,1536]{3,2,1,0:T(8,128)(2,1)S(1)}, u32[]{:S(2)}, u32[]{:S(2)}) %collective-permute-start.35) | collective-permute-done | bytes 294944 | tf_op jit(solution)/shard_map/ppermute | solution.py:43
  226.9 4.7 %shard_map.188 = f32[32,1024]{1,0:T(8,128)S(1)} custom-call(f32[512,1024]{1,0:T(8,128)S(1)} %shard_map.187.refs_0_, bf16[512,1024]{1,0:T(8,128)(2,1)S(1)} %copy-done.2, bf16[256,1024]{1,0:T(8,128)(2,1)} %collective-permute-done.24.refs_2_, bf16[256,1024]{1,0:T(8,128)(2,1)S(1)} %collective-permute-done.25.refs_3_, ...), custom_call_target="tpu_custom_call" | custom-call | flops 1073741824 | bytes 8388608 | tf_op jit(solution)/shard_map/pallas_call | solution.py:98
  234.0 3.5 %collective-permute-done.31 = f32[32,1024]{1,0:T(8,128)S(1)} collective-permute-done((f32[32,1024]{1,0:T(8,128)S(1)}, f32[32,1024]{1,0:T(8,128)S(1)}, u32[]{:S(2)}, u32[]{:S(2)}) %collective-permute-start.31) | collective-permute-done | bytes 131104 | tf_op jit(solution)/shard_map/ppermute | solution.py:412
  239.8 5.1 %collective-permute-done.32 = f32[32,1024]{1,0:T(8,128)S(1)} collective-permute-done((f32[32,1024]{1,0:T(8,128)S(1)}, f32[32,1024]{1,0:T(8,128)S(1)}, u32[]{:S(2)}, u32[]{:S(2)}) %collective-permute-start.32) | collective-permute-done | bytes 131104 | tf_op jit(solution)/shard_map/ppermute | solution.py:412
  245.5 2.6 %fusion.35 = bf16[1,256,768]{2,1,0:T(8,128)(2,1)} fusion(f32[256,768]{1,0:T(8,128)S(1)} %collective-permute-done.33, f32[256,768]{1,0:T(8,128)S(1)} %fusion.30, f32[4,256,768]{2,1,0:T(8,128)} %get-tuple-element.30, f32[]{:T(128)} %bitcast.31), kind=kLoop, calls=%fused_computation.64 | loop fusion | flops 786432 | bytes 2752516 | tf_op jit(solution)/shard_map/broadcast_in_dim | solution.py:377
  (194 shorter events, 88.8 us)
Async XLA Ops:
  1.9 16.4 %collective-permute-start = (bf16[256,1024]{1,0:T(8,128)(2,1)S(1)}, bf16[256,1024]{1,0:T(8,128)(2,1)}, u32[]{:S(2)}, u32[]{:S(2)}) collective-permute-start(bf16[256,1024]{1,0:T(8,128)(2,1)S(1)} %constant_dynamic-slice_fusion.15), channel_id=1, source_target_pairs={{0,4},{4,6},{6,2},{2,0},{1,5},{5,7},{7,3},{3,1},{8,12},{12,14},{14... | collective-permute-start | bytes 1572872 | tf_op jit(solution)/shard_map/ppermute | solution.py:208
  18.3 13.7 %collective-permute-start.1 = (bf16[256,1024]{1,0:T(8,128)(2,1)}, bf16[256,1024]{1,0:T(8,128)(2,1)}, u32[]{:S(2)}, u32[]{:S(2)}) collective-permute-start(bf16[256,1024]{1,0:T(8,128)(2,1)} %collective-permute-done.refs_3_), channel_id=1, source_target_pairs={{0,4},{4,6},{6,2},{2,0},{1,5},{5,7},{7,3},{3,1},{8,12},{12,14},{14... | collective-permute-start | bytes 1572872 | tf_op jit(solution)/shard_map/ppermute | solution.py:208
  32.0 12.8 %collective-permute-start.2 = (bf16[256,1024]{1,0:T(8,128)(2,1)}, bf16[256,1024]{1,0:T(8,128)(2,1)}, u32[]{:S(2)}, u32[]{:S(2)}) collective-permute-start(bf16[256,1024]{1,0:T(8,128)(2,1)} %collective-permute-done.1.refs_2_), channel_id=1, source_target_pairs={{0,4},{4,6},{6,2},{2,0},{1,5},{5,7},{7,3},{3,1},{8,12},{12,14},{14... | collective-permute-start | bytes 1572872 | tf_op jit(solution)/shard_map/ppermute | solution.py:208
  35.9 14.7 %collective-permute-start.7 = (bf16[256,1024]{1,0:T(8,128)(2,1)}, bf16[256,1024]{1,0:T(8,128)(2,1)}, u32[]{:S(2)}, u32[]{:S(2)}) collective-permute-start(bf16[256,1024]{1,0:T(8,128)(2,1)} %collective-permute-done.refs_3_), channel_id=1, source_target_pairs={{0,8},{8,0},{16,24},{24,16},{1,9},{9,1},{17,25},{25,17},{2,10},{10... | collective-permute-start | bytes 1572872 | tf_op jit(solution)/shard_map/ppermute | solution.py:43
  37.4 15.1 %collective-permute-start.8 = (bf16[256,1024]{1,0:T(8,128)(2,1)}, bf16[256,1024]{1,0:T(8,128)(2,1)S(1)}, u32[]{:S(2)}, u32[]{:S(2)}) collective-permute-start(bf16[256,1024]{1,0:T(8,128)(2,1)} %collective-permute-done.refs_3_), channel_id=1, source_target_pairs={{0,16},{8,24},{16,0},{24,8},{1,17},{9,25},{17,1},{25,9},{2,18},{10... | collective-permute-start | bytes 1572872 | tf_op jit(solution)/shard_map/ppermute | solution.py:43
  38.9 24.9 %collective-permute-start.11 = (bf16[256,1024]{1,0:T(8,128)(2,1)}, bf16[256,1024]{1,0:T(8,128)(2,1)}, u32[]{:S(2)}, u32[]{:S(2)}) collective-permute-start(bf16[256,1024]{1,0:T(8,128)(2,1)} %collective-permute-done.1.refs_2_), channel_id=1, source_target_pairs={{0,16},{8,24},{16,0},{24,8},{1,17},{9,25},{17,1},{25,9},{2,18},{10... | collective-permute-start | bytes 1572872 | tf_op jit(solution)/shard_map/ppermute | solution.py:43
  44.8 25.7 %collective-permute-start.3 = (bf16[256,1024]{1,0:T(8,128)(2,1)}, bf16[256,1024]{1,0:T(8,128)(2,1)}, u32[]{:S(2)}, u32[]{:S(2)}) collective-permute-start(bf16[256,1024]{1,0:T(8,128)(2,1)} %constant_dynamic-slice_fusion.16), channel_id=1, source_target_pairs={{0,4},{4,6},{6,2},{2,0},{1,5},{5,7},{7,3},{3,1},{8,12},{12,14},{14... | collective-permute-start | bytes 1572872 | tf_op jit(solution)/shard_map/ppermute | solution.py:208
  49.1 27.3 %collective-permute-start.10 = (bf16[256,1024]{1,0:T(8,128)(2,1)}, bf16[256,1024]{1,0:T(8,128)(2,1)}, u32[]{:S(2)}, u32[]{:S(2)}) collective-permute-start(bf16[256,1024]{1,0:T(8,128)(2,1)} %collective-permute-done.1.refs_2_), channel_id=1, source_target_pairs={{0,8},{8,0},{16,24},{24,16},{1,9},{9,1},{17,25},{25,17},{2,10},{10... | collective-permute-start | bytes 1572872 | tf_op jit(solution)/shard_map/ppermute | solution.py:43
  50.6 24.5 %collective-permute-start.9 = (bf16[256,1024]{1,0:T(8,128)(2,1)}, bf16[256,1024]{1,0:T(8,128)(2,1)}, u32[]{:S(2)}, u32[]{:S(2)}) collective-permute-start(bf16[256,1024]{1,0:T(8,128)(2,1)} %collective-permute-done.7.refs_4_), channel_id=1, source_target_pairs={{0,16},{8,24},{16,0},{24,8},{1,17},{9,25},{17,1},{25,9},{2,18},{10... | collective-permute-start | bytes 1572872 | tf_op jit(solution)/shard_map/ppermute | solution.py:43
  53.3 23.1 %collective-permute-start.13 = (bf16[256,1024]{1,0:T(8,128)(2,1)}, bf16[256,1024]{1,0:T(8,128)(2,1)}, u32[]{:S(2)}, u32[]{:S(2)}) collective-permute-start(bf16[256,1024]{1,0:T(8,128)(2,1)} %collective-permute-done.2.refs_2_), channel_id=1, source_target_pairs={{0,8},{8,0},{16,24},{24,16},{1,9},{9,1},{17,25},{25,17},{2,10},{10... | collective-permute-start | bytes 1572872 | tf_op jit(solution)/shard_map/ppermute | solution.py:43
  63.8 19.4 %collective-permute-start.14 = (bf16[256,1024]{1,0:T(8,128)(2,1)}, bf16[256,1024]{1,0:T(8,128)(2,1)}, u32[]{:S(2)}, u32[]{:S(2)}) collective-permute-start(bf16[256,1024]{1,0:T(8,128)(2,1)} %collective-permute-done.2.refs_2_), channel_id=1, source_target_pairs={{0,16},{8,24},{16,0},{24,8},{1,17},{9,25},{17,1},{25,9},{2,18},{10... | collective-permute-start | bytes 1572872 | tf_op jit(solution)/shard_map/ppermute | solution.py:43
  70.5 23.9 %collective-permute-start.12 = (bf16[256,1024]{1,0:T(8,128)(2,1)}, bf16[256,1024]{1,0:T(8,128)(2,1)}, u32[]{:S(2)}, u32[]{:S(2)}) collective-permute-start(bf16[256,1024]{1,0:T(8,128)(2,1)} %collective-permute-done.11.refs_4_), channel_id=1, source_target_pairs={{0,8},{8,0},{16,24},{24,16},{1,9},{9,1},{17,25},{25,17},{2,10},{10... | collective-permute-start | bytes 1572872 | tf_op jit(solution)/shard_map/ppermute | solution.py:43
  75.0 23.8 %collective-permute-start.4 = (bf16[272,768]{1,0:T(8,128)(2,1)}, bf16[272,768]{1,0:T(8,128)(2,1)}, u32[]{:S(2)}, u32[]{:S(2)}) collective-permute-start(bf16[272,768]{1,0:T(8,128)(2,1)} %concatenate.20), channel_id=1, source_target_pairs={{2,0},{4,2},{6,4},{0,6},{3,1},{5,3},{7,5},{1,7},{10,8},{12,10},{14... | collective-permute-start | bytes 1253384 | tf_op jit(solution)/shard_map/ppermute | solution.py:285
  76.4 30.4 %collective-permute-start.5 = (bf16[272,768]{1,0:T(8,128)(2,1)}, bf16[272,768]{1,0:T(8,128)(2,1)}, u32[]{:S(2)}, u32[]{:S(2)}) collective-permute-start(bf16[272,768]{1,0:T(8,128)(2,1)} %concatenate.20), channel_id=1, source_target_pairs={{4,0},{6,2},{0,4},{2,6},{5,1},{7,3},{1,5},{3,7},{12,8},{14,10},{8,... | collective-permute-start | bytes 1253384 | tf_op jit(solution)/shard_map/ppermute | solution.py:285
  76.4 30.4 %collective-permute-start.6 = (bf16[272,768]{1,0:T(8,128)(2,1)}, bf16[272,768]{1,0:T(8,128)(2,1)}, u32[]{:S(2)}, u32[]{:S(2)}) collective-permute-start(bf16[272,768]{1,0:T(8,128)(2,1)} %concatenate.20), channel_id=1, source_target_pairs={{6,0},{0,2},{2,4},{4,6},{7,1},{1,3},{3,5},{5,7},{14,8},{8,10},{10,... | collective-permute-start | bytes 1253384 | tf_op jit(solution)/shard_map/ppermute | solution.py:285
  83.2 26.4 %collective-permute-start.15 = (bf16[256,1024]{1,0:T(8,128)(2,1)}, bf16[256,1024]{1,0:T(8,128)(2,1)S(1)}, u32[]{:S(2)}, u32[]{:S(2)}) collective-permute-start(bf16[256,1024]{1,0:T(8,128)(2,1)} %collective-permute-done.13.refs_3_), channel_id=1, source_target_pairs={{0,16},{8,24},{16,0},{24,8},{1,17},{9,25},{17,1},{25,9},{2,18},{10... | collective-permute-start | bytes 1572872 | tf_op jit(solution)/shard_map/ppermute | solution.py:43
  94.4 44.0 %collective-permute-start.17 = (bf16[256,1024]{1,0:T(8,128)(2,1)}, bf16[256,1024]{1,0:T(8,128)(2,1)}, u32[]{:S(2)}, u32[]{:S(2)}) collective-permute-start(bf16[256,1024]{1,0:T(8,128)(2,1)} %collective-permute-done.3.refs_3_), channel_id=1, source_target_pairs={{0,8},{8,0},{16,24},{24,16},{1,9},{9,1},{17,25},{25,17},{2,10},{10... | collective-permute-start | bytes 1572872 | tf_op jit(solution)/shard_map/ppermute | solution.py:43
  115.8 34.6 %collective-permute-start.16 = (bf16[4,272,768]{2,1,0:T(8,128)(2,1)}, bf16[4,272,768]{2,1,0:T(8,128)(2,1)}, u32[]{:S(2)}, u32[]{:S(2)}) collective-permute-start(bf16[4,272,768]{2,1,0:T(8,128)(2,1)} %pad_maximum_fusion), channel_id=1, source_target_pairs={{0,1},{1,0},{2,3},{3,2},{4,5},{5,4},{6,7},{7,6},{8,9},{9,8},{10,11... | collective-permute-start | bytes 5013512 | tf_op jit(solution)/shard_map/ppermute | solution.py:307
  120.6 74.8 %collective-permute-start.18 = (bf16[256,1024]{1,0:T(8,128)(2,1)}, bf16[256,1024]{1,0:T(8,128)(2,1)}, u32[]{:S(2)}, u32[]{:S(2)}) collective-permute-start(bf16[256,1024]{1,0:T(8,128)(2,1)} %collective-permute-done.3.refs_3_), channel_id=1, source_target_pairs={{0,16},{8,24},{16,0},{24,8},{1,17},{9,25},{17,1},{25,9},{2,18},{10... | collective-permute-start | bytes 1572872 | tf_op jit(solution)/shard_map/ppermute | solution.py:43
  122.2 13.6 %collective-permute-start.20 = (bf16[256,1024]{1,0:T(8,128)(2,1)}, bf16[256,1024]{1,0:T(8,128)(2,1)}, u32[]{:S(2)}, u32[]{:S(2)}) collective-permute-start(bf16[256,1024]{1,0:T(8,128)(2,1)} %collective-permute-done.3.refs_3_), channel_id=1, source_target_pairs={{0,4},{4,6},{6,2},{2,0},{1,5},{5,7},{7,3},{3,1},{8,12},{12,14},{14... | collective-permute-start | bytes 1572872 | tf_op jit(solution)/shard_map/ppermute | solution.py:208
  135.8 12.6 %collective-permute-start.21 = (bf16[256,1024]{1,0:T(8,128)(2,1)}, bf16[256,1024]{1,0:T(8,128)(2,1)}, u32[]{:S(2)}, u32[]{:S(2)}) collective-permute-start(bf16[256,1024]{1,0:T(8,128)(2,1)} %collective-permute-done.20.refs_2_), channel_id=1, source_target_pairs={{0,8},{8,0},{16,24},{24,16},{1,9},{9,1},{17,25},{25,17},{2,10},{10... | collective-permute-start | bytes 1572872 | tf_op jit(solution)/shard_map/ppermute | solution.py:43
  136.4 12.7 %collective-permute-start.24 = (bf16[256,1024]{1,0:T(8,128)(2,1)}, bf16[256,1024]{1,0:T(8,128)(2,1)}, u32[]{:S(2)}, u32[]{:S(2)}) collective-permute-start(bf16[256,1024]{1,0:T(8,128)(2,1)} %collective-permute-done.20.refs_2_), channel_id=1, source_target_pairs={{0,4},{4,6},{6,2},{2,0},{1,5},{5,7},{7,3},{3,1},{8,12},{12,14},{14... | collective-permute-start | bytes 1572872 | tf_op jit(solution)/shard_map/ppermute | solution.py:208
  139.6 58.0 %collective-permute-start.19 = (bf16[256,1024]{1,0:T(8,128)(2,1)}, bf16[256,1024]{1,0:T(8,128)(2,1)}, u32[]{:S(2)}, u32[]{:S(2)}) collective-permute-start(bf16[256,1024]{1,0:T(8,128)(2,1)} %collective-permute-done.17.refs_4_), channel_id=1, source_target_pairs={{0,16},{8,24},{16,0},{24,8},{1,17},{9,25},{17,1},{25,9},{2,18},{10... | collective-permute-start | bytes 1572872 | tf_op jit(solution)/shard_map/ppermute | solution.py:43
  148.4 55.2 %collective-permute-start.22 = (bf16[256,1024]{1,0:T(8,128)(2,1)}, bf16[256,1024]{1,0:T(8,128)(2,1)}, u32[]{:S(2)}, u32[]{:S(2)}) collective-permute-start(bf16[256,1024]{1,0:T(8,128)(2,1)} %collective-permute-done.20.refs_2_), channel_id=1, source_target_pairs={{0,16},{8,24},{16,0},{24,8},{1,17},{9,25},{17,1},{25,9},{2,18},{10... | collective-permute-start | bytes 1572872 | tf_op jit(solution)/shard_map/ppermute | solution.py:43
  149.1 55.3 %collective-permute-start.23 = (bf16[256,1024]{1,0:T(8,128)(2,1)}, bf16[256,1024]{1,0:T(8,128)(2,1)}, u32[]{:S(2)}, u32[]{:S(2)}) collective-permute-start(bf16[256,1024]{1,0:T(8,128)(2,1)} %collective-permute-done.21.refs_3_), channel_id=1, source_target_pairs={{0,16},{8,24},{16,0},{24,8},{1,17},{9,25},{17,1},{25,9},{2,18},{10... | collective-permute-start | bytes 1572872 | tf_op jit(solution)/shard_map/ppermute | solution.py:43
  150.5 46.1 %collective-permute-start.26 = (bf16[256,1024]{1,0:T(8,128)(2,1)}, bf16[256,1024]{1,0:T(8,128)(2,1)}, u32[]{:S(2)}, u32[]{:S(2)}) collective-permute-start(bf16[256,1024]{1,0:T(8,128)(2,1)} %collective-permute-done.24.refs_2_), channel_id=1, source_target_pairs={{0,16},{8,24},{16,0},{24,8},{1,17},{9,25},{17,1},{25,9},{2,18},{10... | collective-permute-start | bytes 1572872 | tf_op jit(solution)/shard_map/ppermute | solution.py:43
  195.4 31.5 %collective-permute-start.25 = (bf16[256,1024]{1,0:T(8,128)(2,1)}, bf16[256,1024]{1,0:T(8,128)(2,1)S(1)}, u32[]{:S(2)}, u32[]{:S(2)}) collective-permute-start(bf16[256,1024]{1,0:T(8,128)(2,1)} %collective-permute-done.24.refs_2_), channel_id=1, source_target_pairs={{0,8},{8,0},{16,24},{24,16},{1,9},{9,1},{17,25},{25,17},{2,10},{10... | collective-permute-start | bytes 1572872 | tf_op jit(solution)/shard_map/ppermute | solution.py:43
  196.6 30.3 %collective-permute-start.27 = (bf16[256,1024]{1,0:T(8,128)(2,1)}, bf16[256,1024]{1,0:T(8,128)(2,1)S(1)}, u32[]{:S(2)}, u32[]{:S(2)}) collective-permute-start(bf16[256,1024]{1,0:T(8,128)(2,1)} %collective-permute-done.26.refs_4_), channel_id=1, source_target_pairs={{0,8},{8,0},{16,24},{24,16},{1,9},{9,1},{17,25},{25,17},{2,10},{10... | collective-permute-start | bytes 1572872 | tf_op jit(solution)/shard_map/ppermute | solution.py:43
  203.6 21.8 %collective-permute-start.35 = (bf16[2,1,48,1536]{3,2,1,0:T(8,128)(2,1)S(1)}, bf16[2,1,48,1536]{3,2,1,0:T(8,128)(2,1)S(1)}, u32[]{:S(2)}, u32[]{:S(2)}) collective-permute-start(bf16[2,1,48,1536]{3,2,1,0:T(8,128)(2,1)S(1)} %fusion.37), channel_id=1, source_target_pairs={{0,8},{8,0},{16,24},{24,16},{1,9},{9,1},{17,25},{25,17},{2,10},{10... | collective-permute-start | bytes 884744 | tf_op jit(solution)/shard_map/ppermute | solution.py:43
  204.4 41.0 %collective-permute-start.33 = (f32[256,768]{1,0:T(8,128)S(1)}, f32[256,768]{1,0:T(8,128)S(1)}, u32[]{:S(2)}, u32[]{:S(2)}) collective-permute-start(f32[256,768]{1,0:T(8,128)S(1)} %fusion.30), channel_id=1, source_target_pairs={{0,1},{1,0},{2,3},{3,2},{4,5},{5,4},{6,7},{7,6},{8,9},{9,8},{10,11... | collective-permute-start | bytes 2359304 | tf_op jit(solution)/shard_map/ppermute | solution.py:349
  208.4 24.9 %collective-permute-start.38 = (bf16[1,1,48,1536]{3,2,1,0:T(8,128)(2,1)S(1)}, bf16[1,1,48,1536]{3,2,1,0:T(8,128)(2,1)S(1)}, u32[]{:S(2)}, u32[]{:S(2)}) collective-permute-start(bf16[1,1,48,1536]{3,2,1,0:T(8,128)(2,1)S(1)} %dynamic-slice_convert_fusion.1), channel_id=1, source_target_pairs={{0,8},{8,0},{16,24},{24,16},{1,9},{9,1},{17,25},{25,17},{2,10},{10... | collective-permute-start | bytes 442376 | tf_op jit(solution)/shard_map/ppermute | solution.py:43
  225.5 13.5 %collective-permute-start.36 = (bf16[1,1,48,1536]{3,2,1,0:T(8,128)(2,1)S(1)}, bf16[1,1,48,1536]{3,2,1,0:T(8,128)(2,1)S(1)}, u32[]{:S(2)}, u32[]{:S(2)}) collective-permute-start(bf16[1,1,48,1536]{3,2,1,0:T(8,128)(2,1)S(1)} %dynamic-slice_convert_fusion.2), channel_id=1, source_target_pairs={{0,16},{8,24},{16,0},{24,8},{1,17},{9,25},{17,1},{25,9},{2,18},{10... | collective-permute-start | bytes 442376 | tf_op jit(solution)/shard_map/ppermute | solution.py:43
  (36 other events, 465.8 us)

commit v2 on v1

v2 whole, which is shorter than its diff:
```python
import jax
import jax.numpy as jnp
from jax import lax
from jax.experimental import pallas as pl
from jax.experimental.pallas import tpu as pltpu
from jax.sharding import PartitionSpec as P

HEADS = 32
HDIM = 64
ANS = 32
DR = 768


RING_MOST = 4


loss_scale = 16384.0
highest = lax.Precision.HIGHEST


def ring_order(count):
    return list(range(0, count, 2)) + [i for i in range(count - 1, 0, -1) if i % 2]


def ring_next(count):
    order = ring_order(count)
    return [(order[i], order[(i + 1) % count]) for i in range(count)]


def flip(values, bit):
    count = lax.axis_size("pb")
    return lax.ppermute(values, "pb", [(i, i ^ bit) for i in range(count)])


def after(value, *others):
    return lax.optimization_barrier((value,) + others)[0]


def plane_slots(count):
    if count == 6:
        x = ["a0", "a1", "b0", "a2", "b2", "a3", "a4", "a5", "b4"]
        y = ["a0", "a1", "a2", "b1", "a3", "a4", "a5", "b3", "b5"]
    else:
        x, y = [], []
        for r in range(count):
            x.append(f"a{r}")
            y.append(f"a{r}")
            (x, y)[r % 2].append(f"b{r}")
    return [[(slot[0], int(slot[1:])) for slot in link] for link in (x, y)]


class PlaneGathers:
    def __init__(self, ring):
        self.ring = ring
        self.left = plane_slots(len(ring))
        self.got = {}
        self.turns = []

    def turn(self, *others):
        now = []
        for link in (0, 1):
            if not self.left[link]:
                continue
            kind, r = self.left[link][0]
            if kind == "b" and (1 - link, "a", r) not in self.got:
                continue
            self.left[link].pop(0)
            data = self.ring[r] if kind == "a" else self.got[(1 - link, "a", r)]
            before = (self.turns[-2] if len(self.turns) > 1 else []) + list(others)
            if before:
                data = after(data, *before)
            now.append((link, kind, r, flip(data, 1 + link)))
        for link, kind, r, value in now:
            self.got[(link, kind, r)] = value
        self.turns.append([value for _, _, _, value in now])
        return bool(self.left[0] or self.left[1])

    def slice(self, r):
        return [self.ring[r], self.got[(0, "a", r)], self.got[(1, "a", r)], self.got[(r % 2, "b", r)]]


LENGTH_ROWS = 16
COLUMNS = 256


def accumulate(refs, has_total, count):
    total = refs[0][...] if has_total else None
    at = 1 if has_total else 0
    for _ in range(count):
        term = jnp.dot(refs[at][...], refs[at + 1][...], preferred_element_type=jnp.float32)
        total = term if total is None else total + term
        at += 2
    return total, refs[at:]


def two_terms(values):
    high = values.astype(jnp.bfloat16)
    return high, (values - high.astype(jnp.float32)).astype(jnp.bfloat16)


def projection(total, rows, pairs, finish, extra, extra_specs, out_shape, out_specs):
    arrays = [] if total is None else [total]
    specs = [] if total is None else [pl.BlockSpec((total.shape[0], COLUMNS), lambda i, at: (0, i))]
    flops = 0
    for n, (_, part) in enumerate(pairs):
        arrays += [rows, part]
        specs += [
            pl.BlockSpec((rows.shape[0], part.shape[0]), lambda i, at, n=n: (0, at[n])),
            pl.BlockSpec((part.shape[0], COLUMNS), lambda i, at: (0, i)),
        ]
        flops += 2 * rows.shape[0] * part.shape[0] * part.shape[1]
    places = jnp.stack([jnp.asarray(place, jnp.int32) for place, _ in pairs])

    def kernel(places_ref, *refs):
        value, rest = accumulate(refs, total is not None, len(pairs))
        finish(value, *rest)

    return pl.pallas_call(
        kernel,
        grid_spec=pltpu.PrefetchScalarGridSpec(
            num_scalar_prefetch=1,
            grid=(pairs[0][1].shape[1] // COLUMNS,),
            in_specs=specs + list(extra_specs),
            out_specs=out_specs,
        ),
        out_shape=out_shape,
        compiler_params=pltpu.CompilerParams(vmem_limit_bytes=32 << 20),
        cost_estimate=pl.CostEstimate(flops=flops, bytes_accessed=8 << 20, transcendentals=0),
    )(places, *arrays, *extra)


def store(value, out_ref):
    out_ref[...] = value


def running(total, rows, pairs):
    tokens, columns = rows.shape[0], pairs[0][1].shape[1]
    return projection(
        total,
        rows,
        pairs,
        store,
        (),
        (),
        jax.ShapeDtypeStruct((tokens, columns), jnp.float32),
        pl.BlockSpec((tokens, COLUMNS), lambda i, at: (0, i)),
    )


def scores_of(total, rows, pairs, query_blocks, valid, p_here):
    tokens = rows.shape[0]
    queries = query_blocks.shape[1]
    blocks = pairs[0][1].shape[1] // COLUMNS
    each = tokens // p_here

    def finish(keys, query_ref, valid_ref, weight_ref, stat_ref):
        high, low = two_terms(keys)
        query = query_ref[...]
        scores = jnp.dot(high, query, preferred_element_type=jnp.float32)
        scores = scores + jnp.dot(low, query, preferred_element_type=jnp.float32)
        alive = valid_ref[...] > 0.0
        scores = jnp.where(alive, scores, -1e30)
        top = jnp.max(scores, axis=0, keepdims=True)
        weights = jnp.where(alive, jnp.exp(scores - top), 0.0)
        weight_ref[...] = weights
        lines = [top] + [
            jnp.sum(weights[p * each : (p + 1) * each], axis=0, keepdims=True) for p in range(p_here)
        ]
        for i, row in enumerate(lines):
            stat_ref[i : i + 1, :] = row

    wide = queries // blocks
    return projection(
        total,
        rows,
        pairs,
        finish,
        (query_blocks, valid),
        (
            pl.BlockSpec((COLUMNS, wide), lambda i, at: (0, i)),
            pl.BlockSpec((tokens, wide), lambda i, at: (0, 0)),
        ),
        (
            jax.ShapeDtypeStruct((tokens, queries), jnp.float32),
            jax.ShapeDtypeStruct((1 + p_here, queries), jnp.float32),
        ),
        (
            pl.BlockSpec((tokens, wide), lambda i, at: (0, i)),
            pl.BlockSpec((1 + p_here, wide), lambda i, at: (0, i)),
        ),
    )


def summed_of(total, rows, pairs, weights, ratio):
    tokens, queries = weights.shape
    columns = pairs[0][1].shape[1]
    blocks = columns // COLUMNS
    wide = queries // blocks

    def finish(values, weight_ref, ratio_ref, out_ref):
        high, low = two_terms(values)
        w_high, w_low = two_terms(weight_ref[...] * ratio_ref[...])
        over = (((0,), (0,)), ((), ()))
        full = lax.dot_general(w_high, high, over, preferred_element_type=jnp.float32)
        full = full + lax.dot_general(w_high, low, over, preferred_element_type=jnp.float32)
        full = full + lax.dot_general(w_low, high, over, preferred_element_type=jnp.float32)
        head = lax.broadcasted_iota(jnp.int32, (ANS, COLUMNS), 1) // HDIM
        out = jnp.zeros((ANS, COLUMNS), jnp.float32)
        for h in range(COLUMNS // HDIM):
            out = jnp.where(head == h, full[h * ANS : (h + 1) * ANS], out)
        out_ref[...] = out

    return projection(
        total,
        rows,
        pairs,
        finish,
        (weights, ratio),
        (
            pl.BlockSpec((tokens, wide), lambda i, at: (0, i)),
            pl.BlockSpec((1, wide), lambda i, at: (0, i)),
        ),
        jax.ShapeDtypeStruct((ANS, columns), jnp.float32),
        pl.BlockSpec((ANS, COLUMNS), lambda i, at: (0, i)),
    )


def backward_kernel(
    place_ref, mine_ref, other_ref, up_ref, bias_ref, down_ref, gain_ref, query_ref, chosen_ref,
    grad_up_ref, grad_down_ref, sim_ref, dpre_ref, dup_ref,
):
    tokens = mine_ref.shape[1] - LENGTH_ROWS
    mine = mine_ref[0].astype(jnp.float32)
    other = other_ref[0].astype(jnp.float32)
    swap = place_ref[0] != 0
    inputs = jnp.where(swap, other, mine)[:tokens].astype(jnp.bfloat16)
    pre = jnp.where(swap, mine, other)[:tokens]
    length = mine[tokens : tokens + 1, 0:1]
    gain, query = gain_ref[...], query_ref[...]
    centre = pre - jnp.mean(pre, axis=-1, keepdims=True)
    spread = jnp.mean(centre * centre, axis=-1, keepdims=True)
    inverse = 1.0 / jnp.sqrt(spread + 1e-05)
    normed = centre * inverse
    position = lax.broadcasted_iota(jnp.int32, (tokens, 1), 0).astype(jnp.float32)
    live = (position < length).astype(jnp.float32)
    embed = jnp.sum(normed * gain * live, axis=0, keepdims=True) / length
    sim = jnp.sum(embed * query, axis=-1, keepdims=True)
    sim_ref[0] = jnp.broadcast_to(sim, sim_ref.shape[1:])
    dnorm = query * live * gain / length
    dpre = (
        dnorm
        - jnp.mean(dnorm, axis=-1, keepdims=True)
        - normed * jnp.mean(dnorm * normed, axis=-1, keepdims=True)
    ) * inverse
    dpre_b = dpre.astype(jnp.bfloat16)
    chosen = chosen_ref[...]
    inputs_part = jnp.dot(inputs, chosen, preferred_element_type=jnp.float32).astype(jnp.bfloat16)
    dpre_part = jnp.dot(dpre_b, chosen, preferred_element_type=jnp.float32).astype(jnp.bfloat16)
    over = (((0,), (0,)), ((), ()))
    wide = 512
    for start in range(0, up_ref.shape[1], wide):
        cols = slice(start, start + wide)
        upper = jnp.dot(inputs, up_ref[:, cols], preferred_element_type=jnp.float32) + bias_ref[:, cols]
        dact = jnp.dot(dpre_b, down_ref[:, cols], preferred_element_type=jnp.float32)
        below = 0.5 * (1.0 + lax.erf(upper * 0.7071067811865476))
        act_b = (upper * below).astype(jnp.bfloat16)
        slope = below + upper * jnp.exp(-0.5 * upper * upper) * 0.3989422804014327
        dup_b = (dact * slope).astype(jnp.bfloat16)
        grad_up_ref[0, :, cols] = lax.dot_general(inputs_part, dup_b, over, preferred_element_type=jnp.float32)
        grad_down_ref[0, :, cols] = lax.dot_general(dpre_part, act_b, over, preferred_element_type=jnp.float32)

        @pl.when(pl.program_id(0) == 0)
        def _():
            dup_ref[:, cols] = dup_b

    @pl.when(pl.program_id(0) == 0)
    def _():
        dpre_ref[...] = dpre


def backward(place, mine, other, up_weight, up_bias, down_weight, gain, query, chosen):
    count, padded, width = mine.shape
    tokens = padded - LENGTH_ROWS
    hidden, part = up_weight.shape[1], chosen.shape[1]
    whole = lambda array: pl.BlockSpec(array.shape, lambda k, at: (0, 0))
    one = lambda *shape: pl.BlockSpec((1,) + shape, lambda k, at: (k, 0, 0))
    fixed = lambda *shape: pl.BlockSpec(shape, lambda k, at: (0, 0))
    flops = 4 * count * tokens * hidden * (width + part)
    return pl.pallas_call(
        backward_kernel,
        grid_spec=pltpu.PrefetchScalarGridSpec(
            num_scalar_prefetch=1,
            grid=(count,),
            in_specs=[one(padded, width), one(padded, width)]
            + [whole(a) for a in (up_weight, up_bias, down_weight, gain, query, chosen)],
            out_specs=[one(part, hidden), one(part, hidden), one(1, 128), fixed(tokens, width), fixed(tokens, hidden)],
        ),
        out_shape=[
            jax.ShapeDtypeStruct((count, part, hidden), jnp.float32),
            jax.ShapeDtypeStruct((count, part, hidden), jnp.float32),
            jax.ShapeDtypeStruct((count, 1, 128), jnp.float32),
            jax.ShapeDtypeStruct((tokens, width), jnp.float32),
            jax.ShapeDtypeStruct((tokens, hidden), jnp.bfloat16),
        ],
        compiler_params=pltpu.CompilerParams(vmem_limit_bytes=48 << 20),
        cost_estimate=pl.CostEstimate(flops=flops, bytes_accessed=24 << 20, transcendentals=2 * count * tokens * hidden),
    )(place, mine, other, up_weight, up_bias, down_weight, gain, query, chosen)


def quarter_of(weight):
    quarter = weight.shape[0] // lax.axis_size("pb")
    return lax.dynamic_slice_in_dim(weight, lax.axis_index("pb") * quarter, quarter, 0)


def ring_step(piece):
    return lax.ppermute(piece, "pa", ring_next(lax.axis_size("pa")))


def local(
    encoded,
    key_weight,
    value_weight,
    queries,
    key_len,
    retr_query,
    passage_ids,
    placement_perm,
    pool_in,
    pool_pre,
    pool_len,
    up_weight,
    up_bias,
    down_weight,
    norm_gain,
):
    q_here, p_here, tokens, width = encoded.shape
    pb_count = lax.axis_size("pb")
    pa_count = lax.axis_size("pa")
    ma_count = lax.axis_size("ma")
    pb_at = lax.axis_index("pb")
    pa_at = lax.axis_index("pa")
    ma_at = lax.axis_index("ma")
    heads_here = HEADS // ma_count
    cols_here = key_weight.shape[1]
    depth = key_weight.shape[0]
    token_rows = encoded.reshape(p_here * tokens, width)

    order = jnp.array(ring_order(pa_count), jnp.int32)
    place = jnp.argmax(order == pa_at).astype(jnp.int32)

    def owner_of(step):
        return order[(place - step + pa_count) % pa_count]

    def placed(step, parts):
        return [(owner_of(step) * pb_count + (pb_at ^ q), part) for q, part in enumerate(parts)]

    positions = jnp.arange(tokens, dtype=jnp.int32)
    grouped = pa_count <= RING_MOST
    rows = DR // (pb_count * pa_count)
    ff_here = up_weight.shape[1]
    ma_flip = [(i, ma_count - 1 - i) for i in range(ma_count)]
    blocks = cols_here // COLUMNS
    in_block = COLUMNS // HDIM
    pairs = ANS * heads_here
    same = jnp.eye(in_block, dtype=jnp.bfloat16)
    query_blocks = jnp.einsum(
        "abgj,gh->gjbha", queries[0].reshape(ANS, blocks, in_block, HDIM), same
    ).reshape(COLUMNS, pairs)
    valid = (positions[None, :] < key_len[0][:, None]).astype(jnp.float32).reshape(-1, 1)
    valid = jnp.broadcast_to(valid, (p_here * tokens, pairs // blocks))
    if grouped:
        first = ma_at == 0
        mine = jnp.where(first, pool_in[0], pool_pre[0])
        mine = jnp.concatenate([mine, jnp.full((LENGTH_ROWS, DR), pool_len[0], jnp.bfloat16)], axis=0)

        ring = []
        for weight in (key_weight, value_weight):
            piece = quarter_of(weight)
            if ring:
                piece = after(piece, ring[-1])
            for _ in range(pa_count - 1):
                if len(ring) == 2 * pa_count - 3:
                    mine = after(mine, piece)
                    mine = [mine] + [
                        lax.ppermute(mine, "pa", [((i + s) % pa_count, i) for i in range(pa_count)])
                        for s in range(1, pa_count)
                    ]
                piece = ring_step(piece)
                ring.append(piece)
        plane = PlaneGathers(ring)
        while (pa_count % 2, "b", pa_count - 2) not in plane.got:
            plane.turn()
        key_slices = [plane.slice(r) for r in range(pa_count - 1)]
    else:
        whole = lax.all_gather(key_weight, "pa", axis=0, tiled=True)
        weights, stats = scores_of(None, token_rows, [(0, whole)], query_blocks, valid, p_here)
    if grouped:
        keys = running(None, token_rows, [(pa_at, key_weight)] + placed(1, key_slices[0]))
        keys = running(keys, token_rows, placed(2, key_slices[1]))
        rest = [pair for step in range(3, pa_count) for pair in placed(step, key_slices[step - 1])]
        weights, stats = scores_of(keys, token_rows, rest, query_blocks, valid, p_here)
    if grouped:
        mine = after(jnp.stack(mine), stats)
        other = lax.ppermute(mine, "ma", ma_flip)
        inputs_in = ma_at
    else:
        lengths = jnp.full((1, LENGTH_ROWS, DR), pool_len[0], jnp.bfloat16)
        mine = jnp.concatenate([pool_in, lengths], axis=1)
        other = jnp.concatenate([pool_pre, lengths], axis=1)
        inputs_in = 0
    count = mine.shape[0]

    block = jnp.arange(DR, dtype=jnp.int32)
    if grouped:
        kept = jnp.arange(pb_count * rows, dtype=jnp.int32)
        kept = (kept // rows * pa_count + pa_at) * rows + kept % rows
    else:
        kept = block
    chosen = (block[:, None] == kept[None, :]).astype(jnp.bfloat16)
    grad_up, grad_down, sims, dpre, dup_b = backward(
        jnp.asarray(inputs_in, jnp.int32).reshape(1),
        mine,
        other,
        up_weight,
        up_bias[None],
        down_weight,
        norm_gain[None],
        retr_query,
        chosen,
    )
    sims = sims[:, 0, 0]
    if grouped:
        plane.turn()
        plane.turn()
        plane.turn()
        early = set(plane.got)
        while plane.turn(grad_up, grad_down):
            pass
    partial_back = jnp.einsum("rf,df->rd", dup_b, up_weight, preferred_element_type=jnp.float32)
    grad_in = dpre + partial_back + lax.ppermute(partial_back, "ma", ma_flip)

    if grouped:
        stats = jnp.stack(
            [stats]
            + [
                lax.ppermute(stats, "pa", [((i + s) % pa_count, i) for i in range(pa_count)])
                for s in range(1, pa_count)
            ]
        )
    else:
        stats = jnp.roll(lax.all_gather(stats, "pa", axis=0, tiled=False), -pa_at, axis=0)
    best = jnp.max(stats[:, 0], axis=0)
    factor = jnp.exp(stats[:, 0] - best[None])
    sums_all = stats[:, 1:] * factor[:, None]
    totals = jnp.sum(sums_all, axis=(0, 1))
    mass = jnp.sum(sums_all / totals, axis=-1) / (ANS * HEADS)
    mass = mass + lax.ppermute(mass, "ma", ma_flip)
    mass = jnp.roll(mass, pa_at, axis=0).reshape(pa_count * p_here)
    if grouped:
        sims = jnp.roll(sims, pa_at)
    else:
        sims = lax.all_gather(sims, "pa", axis=0, tiled=True)
    where_at = placement_perm[0][passage_ids[0]]
    p_ret = jax.nn.softmax(sims[where_at])
    coef = loss_scale * (p_ret - mass)
    held = (jnp.arange(count, dtype=jnp.int32) + pa_at) % pa_count
    scalars = jnp.sum(jnp.where(where_at[None, :] == held[:, None], coef[None, :], 0.0), axis=1)

    pool_grad = (grad_in * scalars[0]).astype(jnp.bfloat16)[None]

    def scatter_sum(grads, bits):
        total = grads[0] * scalars[0]
        for k in range(1, count):
            total = total + grads[k] * scalars[k]
        if not grouped:
            total = jnp.transpose(total.reshape(pb_count, pa_count, rows, ff_here), (1, 0, 2, 3))
            total = lax.psum_scatter(total, "pa", scatter_dimension=0, tiled=False)
        parts = total.reshape(pb_count, rows, ff_here)
        for bit in bits:
            split = parts.reshape((-1, 2, bit if parts.shape[0] == pb_count else 1) + parts.shape[1:])
            side = (pb_at // bit) % 2
            keep = lax.dynamic_index_in_dim(split, side, 1, keepdims=False)
            give = lax.dynamic_index_in_dim(split, 1 - side, 1, keepdims=False)
            got = flip(give.astype(jnp.bfloat16), bit)
            parts = (keep + got.astype(jnp.float32)).reshape((-1,) + parts.shape[1:])
        return parts[0]

    up_grad = scatter_sum(grad_up, (1, 2))
    down_grad = scatter_sum(grad_down, (2, 1))

    if grouped:
        ready, late = [(pa_at, value_weight)], []
        for r in range(pa_count - 1, 2 * (pa_count - 1)):
            step = r - pa_count + 2
            keys_of = [None, (0, "a", r), (1, "a", r), (r % 2, "b", r)]
            for key, pair in zip(keys_of, placed(step, plane.slice(r))):
                (ready if key is None or key in early else late).append(pair)
        values = running(None, after(token_rows, grad_up, grad_down), ready)
        last_values = (values, token_rows, late)
    else:
        whole = lax.all_gather(value_weight, "pa", axis=0, tiled=True)
        last_values = (None, token_rows, [(0, whole)])
    summed = summed_of(*last_values, weights, (factor[0] / totals)[None])
    if grouped:
        step = 1
        while step < pa_count:
            summed = summed + lax.ppermute(summed, "pa", [(i, i ^ step) for i in range(pa_count)])
            step *= 2
    else:
        summed = lax.psum(summed, "pa")
    attn_out = summed.astype(jnp.bfloat16).reshape(q_here, ANS, cols_here)
    return (attn_out, pool_grad, up_grad, down_grad)


def solution(mesh):
    return jax.shard_map(
        local,
        mesh=mesh,
        in_specs=(
            P("pb", "pa", None, None),
            P("pa", "ma"),
            P("pa", "ma"),
            P("pb", None, "ma"),
            P("pb", "pa"),
            P("pb", None),
            P("pb", None),
            P("pb", None),
            P(("pb", "pa"), None, None),
            P(("pb", "pa"), None, None),
            P(("pb", "pa")),
            P(None, "ma"),
            P("ma"),
            P(None, "ma"),
            P(),
        ),
        out_specs=(
            P("pb", None, "ma"),
            P(("pb", "pa"), None, None),
            P(("pb", "pa"), "ma"),
            P(("pb", "pa"), "ma"),
        ),
        check_vma=False,
    )
```

time: 250 us -> 204 us (0.82)
  Pallas kernels: 26.5 us -> 43.9 us
  local copies, waits for them, and re-layouts: 34.1 us -> 17.3 us
  waiting for transfers between devices: 78.2 us -> 62.2 us
  other arithmetic: 39.3 us -> 25.2 us
  matrix products: 13.7 us -> 1.72 us
    pallas_call x6, Pallas kernels: 26.5 us -> 43.9 us  [the longest x5 26.2 us: projection(): pl.pallas_call(kernel, grid_spec=pltpu.PrefetchScalarGridSpec(num_scalar_...]
    ppermute x22, waiting for transfers between devices: 38.9 us -> 25.6 us  [flip(): return lax.ppermute(values, 'pb', [(i, i ^ bit) for i in range(count)])]
    dot_general x5 -> x1, matrix products: 13.7 us -> 1.72 us  [local(): jnp.einsum('rf,df->rd', dup_b, up_weight, preferred_element_type=jnp.floa...]
    dynamic_slice x5 -> x1, local copies, waits for them, and re-layouts: 8.96 us -> 0.63 us  [owner_of(): return order[(place - step + pa_count) % pa_count]]
    ppermute x3, waiting for transfers between devices: 7.97 us -> 0.01 us  [local(): lax.ppermute(mine, 'pa', [((i + s) % pa_count, i) for i in range(pa_count)])]
    ppermute x6, waiting for transfers between devices: 21.4 us -> 26.7 us  [ring_step(): return lax.ppermute(piece, 'pa', ring_next(lax.axis_size('pa')))]
    reduce_sum x4 -> x0, other arithmetic: 5.13 us -> none  [the longest x1 2.41 us: local(): centre = pre_f - jnp.mean(pre_f, axis=-1, keepdims=True)]
    convert_element_type x4 -> x1, other arithmetic: 5.4 us -> 0.88 us  [local(): chosen = (block[:, None] == kept[None, :]).astype(jnp.bfloat16)]
  transfers between devices with their start and end apart: 39 -> 39, of which waited for: 14 -> 16; matrix products, arithmetic and copies ran while one was open for 31% -> 17% of each run, Pallas kernels for 11% -> 22%
where the time goes in v2:
time: 204 us; the launch traced here: 203 us
  waiting for transfers between devices  62.2 us (30%)
  starting transfers between devices  47.3 us (23%)
  Pallas kernels  43.9 us (22%)
  other arithmetic  25.2 us (12%)
  local copies, waits for them, and re-layouts  17.3 us (8%)
  between operations  5.77 us (3%)
    ppermute x6, waiting for transfers between devices, ring_step(): return lax.ppermute(piece, 'pa', ring_next(lax.axis_size('pa')))  26.7 us
    pallas_call x5, Pallas kernels, projection(): pl.pallas_call(kernel, grid_spec=pltpu.PrefetchScalarGridSpec(num_scalar_...  26.2 us
    ppermute x22, waiting for transfers between devices, flip(): return lax.ppermute(values, 'pb', [(i, i ^ bit) for i in range(count)])  25.6 us
    ppermute x22, starting transfers between devices, flip(): return lax.ppermute(values, 'pb', [(i, i ^ bit) for i in range(count)])  23.2 us
    pallas_call x1, Pallas kernels, backward(): pl.pallas_call(backward_kernel, grid_spec=pltpu.PrefetchScalarGridSpec(nu...  17.7 us
    ppermute x6, starting transfers between devices, ring_step(): return lax.ppermute(piece, 'pa', ring_next(lax.axis_size('pa')))  16.1 us
    add x2, other arithmetic, scatter_sum(): total = total + grads[k] * scalars[k]  9.43 us
    ppermute x2, waiting for transfers between devices, local(): lax.ppermute(summed, 'pa', [(i, i ^ step) for i in range(pa_count)])  8.71 us
  transfers between devices with their start and end apart: 39, of which 16 were waited for; matrix products, arithmetic and copies ran while one was open for 17% of the time, Pallas kernels for 22%

profile of v2, /device:TPU:0, one launch (start us, length us, event | category | flops | bytes accessed | tf_op | source)
XLA Modules:
  0.0 203.3 jit_solution(2725491928824969469)
XLA Ops:
  1.8 4.1 %collective-permute-start = (bf16[256,1024]{1,0:T(8,128)(2,1)S(1)}, bf16[256,1024]{1,0:T(8,128)(2,1)S(1)}, u32[]{:S(2)}, u32[]{:S(2)}) collective-permute-start(bf16[256,1024]{1,0:T(8,128)(2,1)S(1)} %constant_dynamic-slice_fusion.1), channel_id=1, source_target_pairs={{0,4},{4,6},{6,2},{2,0},{1,5},{5,7},{7,3},{3,1},{8,12},{12,14},{14... | collective-permute-start | bytes 1572872 | tf_op jit(solution)/shard_map/ppermute | solution.py:316
  5.9 11.2 %collective-permute-done.refs_3_ = bf16[256,1024]{1,0:T(8,128)(2,1)S(1)} collective-permute-done((bf16[256,1024]{1,0:T(8,128)(2,1)S(1)}, bf16[256,1024]{1,0:T(8,128)(2,1)S(1)}, u32[]{:S(2)}, u32[]{:S(2)}) %collective-permute-start) | collective-permute-done | bytes 524320 | tf_op jit(solution)/shard_map/ppermute | solution.py:316
  17.1 3.4 %collective-permute-start.1 = (bf16[256,1024]{1,0:T(8,128)(2,1)S(1)}, bf16[256,1024]{1,0:T(8,128)(2,1)}, u32[]{:S(2)}, u32[]{:S(2)}) collective-permute-start(bf16[256,1024]{1,0:T(8,128)(2,1)S(1)} %collective-permute-done.refs_3_), channel_id=1, source_target_pairs={{0,4},{4,6},{6,2},{2,0},{1,5},{5,7},{7,3},{3,1},{8,12},{12,14},{14... | collective-permute-start | bytes 1572872 | tf_op jit(solution)/shard_map/ppermute | solution.py:316
  22.1 8.7 %collective-permute-done.1.refs_2_ = bf16[256,1024]{1,0:T(8,128)(2,1)} collective-permute-done((bf16[256,1024]{1,0:T(8,128)(2,1)S(1)}, bf16[256,1024]{1,0:T(8,128)(2,1)}, u32[]{:S(2)}, u32[]{:S(2)}) %collective-permute-start.1) | collective-permute-done | bytes 524320 | tf_op jit(solution)/shard_map/ppermute | solution.py:316
  30.7 3.5 %collective-permute-start.2 = (bf16[256,1024]{1,0:T(8,128)(2,1)}, bf16[256,1024]{1,0:T(8,128)(2,1)S(1)}, u32[]{:S(2)}, u32[]{:S(2)}) collective-permute-start(bf16[256,1024]{1,0:T(8,128)(2,1)} %collective-permute-done.1.refs_2_), channel_id=1, source_target_pairs={{0,4},{4,6},{6,2},{2,0},{1,5},{5,7},{7,3},{3,1},{8,12},{12,14},{14... | collective-permute-start | bytes 1572872 | tf_op jit(solution)/shard_map/ppermute | solution.py:316
  37.9 1.9 constant_dynamic-slice_fusion.2
  40.8 3.1 %collective-permute-done.2.refs_2_ = bf16[256,1024]{1,0:T(8,128)(2,1)S(1)} collective-permute-done((bf16[256,1024]{1,0:T(8,128)(2,1)}, bf16[256,1024]{1,0:T(8,128)(2,1)S(1)}, u32[]{:S(2)}, u32[]{:S(2)}) %collective-permute-start.2) | collective-permute-done | bytes 524320 | tf_op jit(solution)/shard_map/ppermute | solution.py:316
  43.9 3.3 %collective-permute-start.3 = (bf16[256,1024]{1,0:T(8,128)(2,1)}, bf16[256,1024]{1,0:T(8,128)(2,1)}, u32[]{:S(2)}, u32[]{:S(2)}) collective-permute-start(bf16[256,1024]{1,0:T(8,128)(2,1)} %constant_dynamic-slice_fusion.2), channel_id=1, source_target_pairs={{0,4},{4,6},{6,2},{2,0},{1,5},{5,7},{7,3},{3,1},{8,12},{12,14},{14... | collective-permute-start | bytes 1572872 | tf_op jit(solution)/shard_map/ppermute | solution.py:316
  48.0 1.8 collective-permute-done.8.refs_5_
  65.3 2.1 %multiply_bitcast_fusion = bf16[4,64,4,4,32]{1,0,4,3,2:T(4,128)(2,1)} fusion(bf16[4,4]{0,1:T(4,128)(2,1)S(1)} %fusion.9, bf16[32,4,4,64]{3,2,1,0:T(4,128)(2,1)} %reshape_squeeze.5), kind=kLoop, calls=%fused_computation.12 | loop fusion | flops 524288 | bytes 327712 | tf_op jit(solution)/shard_map/abgj,gh->gjbha/transpose | solution.py:366
  67.3 5.0 %collective-permute-done.10.refs_9_ = bf16[256,1024]{1,0:T(8,128)(2,1)} collective-permute-done((bf16[256,1024]{1,0:T(8,128)(2,1)}, bf16[256,1024]{1,0:T(8,128)(2,1)}, u32[]{:S(2)}, u32[]{:S(2)}) %collective-permute-start.10) | collective-permute-done | bytes 524320 | tf_op jit(solution)/shard_map/ppermute | solution.py:32
  74.4 3.8 %collective-permute-done.4.refs_11_ = bf16[256,1024]{1,0:T(8,128)(2,1)} collective-permute-done((bf16[256,1024]{1,0:T(8,128)(2,1)}, bf16[256,1024]{1,0:T(8,128)(2,1)}, u32[]{:S(2)}, u32[]{:S(2)}) %collective-permute-start.4) | collective-permute-done | bytes 524320 | tf_op jit(solution)/shard_map/ppermute | solution.py:316
  78.9 2.5 %collective-permute-done.13.refs_8_ = bf16[256,1024]{1,0:T(8,128)(2,1)S(1)} collective-permute-done((bf16[256,1024]{1,0:T(8,128)(2,1)}, bf16[256,1024]{1,0:T(8,128)(2,1)S(1)}, u32[]{:S(2)}, u32[]{:S(2)}) %collective-permute-start.13) | collective-permute-done | bytes 524320 | tf_op jit(solution)/shard_map/ppermute | solution.py:32
  84.3 2.2 %reshape.309 = bf16[256,512]{0,1:T(8,128)(2,1)} reshape(bf16[4,64,4,4,32]{1,0,4,3,2:T(4,128)(2,1)} %multiply_bitcast_fusion) | data formatting | bytes 524288 | tf_op jit(solution)/shard_map/reshape | solution.py:368
  89.1 2.2 %copy-done.1 = bf16[1,2,256,4096]{3,2,1,0:T(8,128)(2,1)S(1)} copy-done((bf16[1,2,256,4096]{3,2,1,0:T(8,128)(2,1)S(1)}, bf16[1,2,256,4096]{3,2,1,0:T(8,128)(2,1)}, u32[]{:S(2)}) %copy-start.1) | copy-done | bytes 4194328
  92.4 5.2 %shard_map.183.refs_0_ = f32[512,1024]{1,0:T(8,128)S(1)} custom-call(s32[5]{0:T(128)S(1)} %stack.119.places_ref, bf16[512,4096]{1,0:T(8,128)(2,1)S(1)} %bitcast.79, bf16[1024,1024]{1,0:T(8,128)(2,1)S(1)} %copy-done.3, bf16[512,4096]{1,0:T(8,128)(2,1)S(1)} %bitcast.80, bf16[256,1024]{1,0:T(8,128)(2,1)S(1)} %collective-permute-done.refs_3_, ...), custom_call_target="tpu_custom_call" | custom-call | flops 2147483648 | bytes 8388608 | tf_op jit(solution)/shard_map/pallas_call | solution.py:118
  97.6 4.3 %shard_map.184.refs_0_ = f32[512,1024]{1,0:T(8,128)S(1)} custom-call(s32[4]{0:T(128)S(1)} %get-tuple-element.68.places_ref, f32[512,1024]{1,0:T(8,128)S(1)} %shard_map.183.refs_0_, bf16[512,4096]{1,0:T(8,128)(2,1)S(1)} %bitcast.84, bf16[256,1024]{1,0:T(8,128)(2,1)} %collective-permute-done.1.refs_2_, bf16[512,4096]{1,0:T(8,128)(2,1)S(1)} %bitcast.85, ...), custom_call_target="tpu_custom_call" | custom-call | flops 1073741824 | bytes 8388608 | tf_op jit(solution)/shard_map/pallas_call | solution.py:118
  102.1 5.7 %shard_map.185 = (f32[512,512]{1,0:T(8,128)S(1)}, f32[3,512]{1,0:T(4,128)S(1)}) custom-call(s32[4]{0:T(128)S(1)} %get-tuple-element.67.places_ref, f32[512,1024]{1,0:T(8,128)S(1)} %shard_map.184.refs_0_, bf16[512,4096]{1,0:T(8,128)(2,1)S(1)} %bitcast.91, bf16[256,1024]{1,0:T(8,128)(2,1)S(1)} %copy-done.10, bf16[512,4096]{1,0:T(8,128)(2,1)S(1)} %bitcast.89, ...), custom_call_target="tpu_custom_call" | custom-call | flops 1073741824 | bytes 8388608 | tf_op jit(solution)/shard_map/pallas_call | solution.py:118
  108.8 2.9 %collective-permute-start.28 = (f32[3,512]{1,0:T(4,128)S(1)}, f32[3,512]{1,0:T(4,128)S(1)}, u32[]{:S(2)}, u32[]{:S(2)}) collective-permute-start(f32[3,512]{1,0:T(4,128)S(1)} %get-tuple-element.38), channel_id=1, source_target_pairs={{2,0},{4,2},{6,4},{0,6},{3,1},{5,3},{7,5},{1,7},{10,8},{12,10},{14... | collective-permute-start | bytes 18440 | tf_op jit(solution)/shard_map/ppermute | solution.py:446
  115.1 1.9 collective-permute-start.23
  120.2 8.6 %collective-permute-done.18.refs_5_ = bf16[256,1024]{1,0:T(8,128)(2,1)} collective-permute-done((bf16[256,1024]{1,0:T(8,128)(2,1)}, bf16[256,1024]{1,0:T(8,128)(2,1)}, u32[]{:S(2)}, u32[]{:S(2)}) %collective-permute-start.18) | collective-permute-done | bytes 524320 | tf_op jit(solution)/shard_map/ppermute | solution.py:32
  133.1 17.7 %shard_map.186 = (f32[4,192,1536]{2,1,0:T(8,128)}, f32[4,192,1536]{2,1,0:T(8,128)}, f32[4,1,128]{2,1,0:T(1,128)S(1)}, f32[256,768]{1,0:T(8,128)S(1)}, bf16[256,1536]{1,0:T(8,128)(2,1)S(1)}) custom-call(s32[1]{0:T(128)} %bitcast.17.place_ref, bf16[4,272,768]{2,1,0:T(8,128)(2,1)S(1)} %pad_maximum_fusion.mine_ref, ...), custom_call_target="tpu_custom_call" | custom-call | flops 6039797760 | bytes 25165824 | tf_op jit(solution)/shard_map/pallas_call | solution.py:289
  150.8 2.6 %collective-permute-done.25.refs_21_ = bf16[256,1024]{1,0:T(8,128)(2,1)S(1)} collective-permute-done((bf16[256,1024]{1,0:T(8,128)(2,1)}, bf16[256,1024]{1,0:T(8,128)(2,1)S(1)}, u32[]{:S(2)}, u32[]{:S(2)}) %collective-permute-start.25) | collective-permute-done | bytes 524320 | tf_op jit(solution)/shard_map/ppermute | solution.py:32
  155.6 1.7 fusion.27
  162.3 5.7 %multiply_add_fusion.1 = f32[1,192,1536]{2,1,0:T(8,128)S(1)} fusion(f32[4,192,1536]{2,1,0:T(8,128)} %get-tuple-element.40, f32[]{:T(128)} %bitcast.40, f32[]{:T(128)} %bitcast.39, f32[]{:T(128)} %bitcast.38, f32[]{:T(128)} %bitcast.36), kind=kLoop, calls=%fused_computation.4 | loop fusion | flops 2064384 | bytes 5898256 | tf_op jit(solution)/shard_map/add | solution.py:474
  168.8 3.7 %multiply_add_fusion = f32[1,192,1536]{2,1,0:T(8,128)S(1)} fusion(f32[4,192,1536]{2,1,0:T(8,128)S(1)} %copy-done.17, f32[]{:T(128)} %bitcast.40, f32[]{:T(128)} %bitcast.39, f32[]{:T(128)} %bitcast.38, f32[]{:T(128)} %bitcast.36), kind=kLoop, calls=%fused_computation.3 | loop fusion | flops 2064384 | bytes 5898256 | tf_op jit(solution)/shard_map/add | solution.py:474
  173.9 7.1 %shard_map.187.refs_0_ = f32[512,1024]{1,0:T(8,128)S(1)} custom-call(s32[11]{0:T(128)S(1)} %stack.111.places_ref, bf16[512,4096]{1,0:T(8,128)(2,1)S(1)} %bitcast.92, bf16[1024,1024]{1,0:T(8,128)(2,1)S(1)} %copy-done.4, bf16[512,4096]{1,0:T(8,128)(2,1)S(1)} %bitcast.93, bf16[256,1024]{1,0:T(8,128)(2,1)} %collective-permute-done.3.refs_3_, ...), custom_call_target="tpu_custom_call" | custom-call | flops 3758096384 | bytes 8388608 | tf_op jit(solution)/shard_map/pallas_call | solution.py:118
  183.5 3.9 %shard_map.188 = f32[32,1024]{1,0:T(8,128)S(1)} custom-call(s32[2]{0:T(128)S(1)} %pad_add_fusion.places_ref, f32[512,1024]{1,0:T(8,128)S(1)} %shard_map.187.refs_0_, bf16[512,4096]{1,0:T(8,128)(2,1)S(1)} %bitcast.103, bf16[256,1024]{1,0:T(8,128)(2,1)S(1)} %collective-permute-done.26.refs_2_, bf16[512,4096]{1,0:T(8,128)(2,1)S(1)} %bitcast.104, ...), custom_call_target="tpu_custom_call" | custom-call | flops 536870912 | bytes 8388608 | tf_op jit(solution)/shard_map/pallas_call | solution.py:118
  188.5 4.0 %collective-permute-done.31 = f32[32,1024]{1,0:T(8,128)S(1)} collective-permute-done((f32[32,1024]{1,0:T(8,128)S(1)}, f32[32,1024]{1,0:T(8,128)S(1)}, u32[]{:S(2)}, u32[]{:S(2)}) %collective-permute-start.31) | collective-permute-done | bytes 131104 | tf_op jit(solution)/shard_map/ppermute | solution.py:507
  192.5 1.7 collective-permute-start.32
  195.0 4.7 %collective-permute-done.32 = f32[32,1024]{1,0:T(8,128)S(1)} collective-permute-done((f32[32,1024]{1,0:T(8,128)S(1)}, f32[32,1024]{1,0:T(8,128)S(1)}, u32[]{:S(2)}, u32[]{:S(2)}) %collective-permute-start.32) | collective-permute-done | bytes 131104 | tf_op jit(solution)/shard_map/ppermute | solution.py:507
  200.3 3.0 %fusion.1 = bf16[1,256,768]{2,1,0:T(8,128)(2,1)} fusion(f32[256,768]{1,0:T(8,128)} %collective-permute-done.33, f32[256,768]{1,0:T(8,128)S(1)} %copy-done.6, f32[256,768]{1,0:T(8,128)} %fusion.27, f32[]{:T(128)} %bitcast.36), kind=kLoop, calls=%fused_computation.13 | loop fusion | flops 786432 | bytes 2752516 | tf_op jit(solution)/shard_map/broadcast_in_dim | solution.py:469
  (175 shorter events, 54.6 us)
Async XLA Ops:
  1.8 15.3 %collective-permute-start = (bf16[256,1024]{1,0:T(8,128)(2,1)S(1)}, bf16[256,1024]{1,0:T(8,128)(2,1)S(1)}, u32[]{:S(2)}, u32[]{:S(2)}) collective-permute-start(bf16[256,1024]{1,0:T(8,128)(2,1)S(1)} %constant_dynamic-slice_fusion.1), channel_id=1, source_target_pairs={{0,4},{4,6},{6,2},{2,0},{1,5},{5,7},{7,3},{3,1},{8,12},{12,14},{14... | collective-permute-start | bytes 1572872 | tf_op jit(solution)/shard_map/ppermute | solution.py:316
  17.1 13.7 %collective-permute-start.1 = (bf16[256,1024]{1,0:T(8,128)(2,1)S(1)}, bf16[256,1024]{1,0:T(8,128)(2,1)}, u32[]{:S(2)}, u32[]{:S(2)}) collective-permute-start(bf16[256,1024]{1,0:T(8,128)(2,1)S(1)} %collective-permute-done.refs_3_), channel_id=1, source_target_pairs={{0,4},{4,6},{6,2},{2,0},{1,5},{5,7},{7,3},{3,1},{8,12},{12,14},{14... | collective-permute-start | bytes 1572872 | tf_op jit(solution)/shard_map/ppermute | solution.py:316
  30.7 13.2 %collective-permute-start.2 = (bf16[256,1024]{1,0:T(8,128)(2,1)}, bf16[256,1024]{1,0:T(8,128)(2,1)S(1)}, u32[]{:S(2)}, u32[]{:S(2)}) collective-permute-start(bf16[256,1024]{1,0:T(8,128)(2,1)} %collective-permute-done.1.refs_2_), channel_id=1, source_target_pairs={{0,4},{4,6},{6,2},{2,0},{1,5},{5,7},{7,3},{3,1},{8,12},{12,14},{14... | collective-permute-start | bytes 1572872 | tf_op jit(solution)/shard_map/ppermute | solution.py:316
  34.9 14.9 %collective-permute-start.8 = (bf16[256,1024]{1,0:T(8,128)(2,1)S(1)}, bf16[256,1024]{1,0:T(8,128)(2,1)S(1)}, u32[]{:S(2)}, u32[]{:S(2)}) collective-permute-start(bf16[256,1024]{1,0:T(8,128)(2,1)S(1)} %collective-permute-done.refs_3_), channel_id=1, source_target_pairs={{0,8},{8,0},{16,24},{24,16},{1,9},{9,1},{17,25},{25,17},{2,10},{10... | collective-permute-start | bytes 1572872 | tf_op jit(solution)/shard_map/ppermute | solution.py:32
  36.4 15.0 %collective-permute-start.9 = (bf16[256,1024]{1,0:T(8,128)(2,1)S(1)}, bf16[256,1024]{1,0:T(8,128)(2,1)}, u32[]{:S(2)}, u32[]{:S(2)}) collective-permute-start(bf16[256,1024]{1,0:T(8,128)(2,1)S(1)} %collective-permute-done.refs_3_), channel_id=1, source_target_pairs={{0,16},{8,24},{16,0},{24,8},{1,17},{9,25},{17,1},{25,9},{2,18},{10... | collective-permute-start | bytes 1572872 | tf_op jit(solution)/shard_map/ppermute | solution.py:32
  39.8 21.3 %collective-permute-start.11 = (bf16[256,1024]{1,0:T(8,128)(2,1)}, bf16[256,1024]{1,0:T(8,128)(2,1)}, u32[]{:S(2)}, u32[]{:S(2)}) collective-permute-start(bf16[256,1024]{1,0:T(8,128)(2,1)} %collective-permute-done.1.refs_2_), channel_id=1, source_target_pairs={{0,8},{8,0},{16,24},{24,16},{1,9},{9,1},{17,25},{25,17},{2,10},{10... | collective-permute-start | bytes 1572872 | tf_op jit(solution)/shard_map/ppermute | solution.py:32
  40.3 22.3 %collective-permute-start.12 = (bf16[256,1024]{1,0:T(8,128)(2,1)}, bf16[256,1024]{1,0:T(8,128)(2,1)}, u32[]{:S(2)}, u32[]{:S(2)}) collective-permute-start(bf16[256,1024]{1,0:T(8,128)(2,1)} %collective-permute-done.1.refs_2_), channel_id=1, source_target_pairs={{0,16},{8,24},{16,0},{24,8},{1,17},{9,25},{17,1},{25,9},{2,18},{10... | collective-permute-start | bytes 1572872 | tf_op jit(solution)/shard_map/ppermute | solution.py:32
  43.9 20.2 %collective-permute-start.3 = (bf16[256,1024]{1,0:T(8,128)(2,1)}, bf16[256,1024]{1,0:T(8,128)(2,1)}, u32[]{:S(2)}, u32[]{:S(2)}) collective-permute-start(bf16[256,1024]{1,0:T(8,128)(2,1)} %constant_dynamic-slice_fusion.2), channel_id=1, source_target_pairs={{0,4},{4,6},{6,2},{2,0},{1,5},{5,7},{7,3},{3,1},{8,12},{12,14},{14... | collective-permute-start | bytes 1572872 | tf_op jit(solution)/shard_map/ppermute | solution.py:316
  51.3 21.0 %collective-permute-start.10 = (bf16[256,1024]{1,0:T(8,128)(2,1)}, bf16[256,1024]{1,0:T(8,128)(2,1)}, u32[]{:S(2)}, u32[]{:S(2)}) collective-permute-start(bf16[256,1024]{1,0:T(8,128)(2,1)} %collective-permute-done.9.refs_7_), channel_id=1, source_target_pairs={{0,8},{8,0},{16,24},{24,16},{1,9},{9,1},{17,25},{25,17},{2,10},{10... | collective-permute-start | bytes 1572872 | tf_op jit(solution)/shard_map/ppermute | solution.py:32
  52.1 21.8 %collective-permute-start.15 = (bf16[256,1024]{1,0:T(8,128)(2,1)S(1)}, bf16[256,1024]{1,0:T(8,128)(2,1)}, u32[]{:S(2)}, u32[]{:S(2)}) collective-permute-start(bf16[256,1024]{1,0:T(8,128)(2,1)S(1)} %collective-permute-done.2.refs_2_), channel_id=1, source_target_pairs={{0,16},{8,24},{16,0},{24,8},{1,17},{9,25},{17,1},{25,9},{2,18},{10... | collective-permute-start | bytes 1572872 | tf_op jit(solution)/shard_map/ppermute | solution.py:32
  62.6 18.8 %collective-permute-start.13 = (bf16[256,1024]{1,0:T(8,128)(2,1)}, bf16[256,1024]{1,0:T(8,128)(2,1)S(1)}, u32[]{:S(2)}, u32[]{:S(2)}) collective-permute-start(bf16[256,1024]{1,0:T(8,128)(2,1)} %collective-permute-done.11.refs_4_), channel_id=1, source_target_pairs={{0,16},{8,24},{16,0},{24,8},{1,17},{9,25},{17,1},{25,9},{2,18},{10... | collective-permute-start | bytes 1572872 | tf_op jit(solution)/shard_map/ppermute | solution.py:32
  64.1 14.1 %collective-permute-start.4 = (bf16[256,1024]{1,0:T(8,128)(2,1)}, bf16[256,1024]{1,0:T(8,128)(2,1)}, u32[]{:S(2)}, u32[]{:S(2)}) collective-permute-start(bf16[256,1024]{1,0:T(8,128)(2,1)} %collective-permute-done.3.refs_3_), channel_id=1, source_target_pairs={{0,4},{4,6},{6,2},{2,0},{1,5},{5,7},{7,3},{3,1},{8,12},{12,14},{14... | collective-permute-start | bytes 1572872 | tf_op jit(solution)/shard_map/ppermute | solution.py:316
  64.7 22.9 %collective-permute-start.14 = (bf16[256,1024]{1,0:T(8,128)(2,1)S(1)}, bf16[256,1024]{1,0:T(8,128)(2,1)}, u32[]{:S(2)}, u32[]{:S(2)}) collective-permute-start(bf16[256,1024]{1,0:T(8,128)(2,1)S(1)} %collective-permute-done.2.refs_2_), channel_id=1, source_target_pairs={{0,8},{8,0},{16,24},{24,16},{1,9},{9,1},{17,25},{25,17},{2,10},{10... | collective-permute-start | bytes 1572872 | tf_op jit(solution)/shard_map/ppermute | solution.py:32
  73.8 28.1 %collective-permute-start.16 = (bf16[256,1024]{1,0:T(8,128)(2,1)}, bf16[256,1024]{1,0:T(8,128)(2,1)}, u32[]{:S(2)}, u32[]{:S(2)}) collective-permute-start(bf16[256,1024]{1,0:T(8,128)(2,1)} %collective-permute-done.15.refs_6_), channel_id=1, source_target_pairs={{0,8},{8,0},{16,24},{24,16},{1,9},{9,1},{17,25},{25,17},{2,10},{10... | collective-permute-start | bytes 1572872 | tf_op jit(solution)/shard_map/ppermute | solution.py:32
  78.2 30.3 %collective-permute-start.7 = (bf16[272,768]{1,0:T(8,128)(2,1)}, bf16[272,768]{1,0:T(8,128)(2,1)}, u32[]{:S(2)}, u32[]{:S(2)}) collective-permute-start(bf16[272,768]{1,0:T(8,128)(2,1)} %concatenate.11), channel_id=1, source_target_pairs={{6,0},{0,2},{2,4},{4,6},{7,1},{1,3},{3,5},{5,7},{14,8},{8,10},{10,... | collective-permute-start | bytes 1253384 | tf_op jit(solution)/shard_map/ppermute | solution.py:385
  78.2 30.6 %collective-permute-start.6 = (bf16[272,768]{1,0:T(8,128)(2,1)}, bf16[272,768]{1,0:T(8,128)(2,1)}, u32[]{:S(2)}, u32[]{:S(2)}) collective-permute-start(bf16[272,768]{1,0:T(8,128)(2,1)} %concatenate.11), channel_id=1, source_target_pairs={{4,0},{6,2},{0,4},{2,6},{5,1},{7,3},{1,5},{3,7},{12,8},{14,10},{8,... | collective-permute-start | bytes 1253384 | tf_op jit(solution)/shard_map/ppermute | solution.py:385
  82.2 29.5 %collective-permute-start.5 = (bf16[272,768]{1,0:T(8,128)(2,1)}, bf16[272,768]{1,0:T(8,128)(2,1)}, u32[]{:S(2)}, u32[]{:S(2)}) collective-permute-start(bf16[272,768]{1,0:T(8,128)(2,1)} %concatenate.11), channel_id=1, source_target_pairs={{2,0},{4,2},{6,4},{0,6},{3,1},{5,3},{7,5},{1,7},{10,8},{12,10},{14... | collective-permute-start | bytes 1253384 | tf_op jit(solution)/shard_map/ppermute | solution.py:385
  87.6 26.0 %collective-permute-start.19 = (bf16[256,1024]{1,0:T(8,128)(2,1)}, bf16[256,1024]{1,0:T(8,128)(2,1)}, u32[]{:S(2)}, u32[]{:S(2)}) collective-permute-start(bf16[256,1024]{1,0:T(8,128)(2,1)} %collective-permute-done.3.refs_3_), channel_id=1, source_target_pairs={{0,16},{8,24},{16,0},{24,8},{1,17},{9,25},{17,1},{25,9},{2,18},{10... | collective-permute-start | bytes 1572872 | tf_op jit(solution)/shard_map/ppermute | solution.py:32
  113.3 18.8 %collective-permute-start.17 = (bf16[4,272,768]{2,1,0:T(8,128)(2,1)S(1)}, bf16[4,272,768]{2,1,0:T(8,128)(2,1)}, u32[]{:S(2)}, u32[]{:S(2)}) collective-permute-start(bf16[4,272,768]{2,1,0:T(8,128)(2,1)S(1)} %pad_maximum_fusion.mine_ref), channel_id=1, source_target_pairs={{0,1},{1,0},{2,3},{3,2},{4,5},{5,4},{6,7},{7,6},{8,9},{9,8},{10,11... | collective-permute-start | bytes 5013512 | tf_op jit(solution)/shard_map/ppermute | solution.py:404
  113.6 15.1 %collective-permute-start.18 = (bf16[256,1024]{1,0:T(8,128)(2,1)}, bf16[256,1024]{1,0:T(8,128)(2,1)}, u32[]{:S(2)}, u32[]{:S(2)}) collective-permute-start(bf16[256,1024]{1,0:T(8,128)(2,1)} %collective-permute-done.3.refs_3_), channel_id=1, source_target_pairs={{0,8},{8,0},{16,24},{24,16},{1,9},{9,1},{17,25},{25,17},{2,10},{10... | collective-permute-start | bytes 1572872 | tf_op jit(solution)/shard_map/ppermute | solution.py:32
  114.4 14.4 %collective-permute-start.20 = (bf16[256,1024]{1,0:T(8,128)(2,1)}, bf16[256,1024]{1,0:T(8,128)(2,1)S(1)}, u32[]{:S(2)}, u32[]{:S(2)}) collective-permute-start(bf16[256,1024]{1,0:T(8,128)(2,1)} %collective-permute-done.4.refs_11_), channel_id=1, source_target_pairs={{0,16},{8,24},{16,0},{24,8},{1,17},{9,25},{17,1},{25,9},{2,18},{10... | collective-permute-start | bytes 1572872 | tf_op jit(solution)/shard_map/ppermute | solution.py:32
  115.1 14.5 %collective-permute-start.23 = (bf16[256,1024]{1,0:T(8,128)(2,1)}, bf16[256,1024]{1,0:T(8,128)(2,1)}, u32[]{:S(2)}, u32[]{:S(2)}) collective-permute-start(bf16[256,1024]{1,0:T(8,128)(2,1)} %collective-permute-done.4.refs_11_), channel_id=1, source_target_pairs={{0,4},{4,6},{6,2},{2,0},{1,5},{5,7},{7,3},{3,1},{8,12},{12,14},{14... | collective-permute-start | bytes 1572872 | tf_op jit(solution)/shard_map/ppermute | solution.py:316
  118.3 32.4 %collective-permute-start.22 = (bf16[256,1024]{1,0:T(8,128)(2,1)}, bf16[256,1024]{1,0:T(8,128)(2,1)}, u32[]{:S(2)}, u32[]{:S(2)}) collective-permute-start(bf16[256,1024]{1,0:T(8,128)(2,1)} %collective-permute-done.4.refs_11_), channel_id=1, source_target_pairs={{0,8},{8,0},{16,24},{24,16},{1,9},{9,1},{17,25},{25,17},{2,10},{10... | collective-permute-start | bytes 1572872 | tf_op jit(solution)/shard_map/ppermute | solution.py:32
  128.7 43.8 %collective-permute-start.21 = (bf16[256,1024]{1,0:T(8,128)(2,1)}, bf16[256,1024]{1,0:T(8,128)(2,1)}, u32[]{:S(2)}, u32[]{:S(2)}) collective-permute-start(bf16[256,1024]{1,0:T(8,128)(2,1)} %collective-permute-done.18.refs_5_), channel_id=1, source_target_pairs={{0,16},{8,24},{16,0},{24,8},{1,17},{9,25},{17,1},{25,9},{2,18},{10... | collective-permute-start | bytes 1572872 | tf_op jit(solution)/shard_map/ppermute | solution.py:32
  129.6 25.2 %collective-permute-start.24 = (bf16[256,1024]{1,0:T(8,128)(2,1)}, bf16[256,1024]{1,0:T(8,128)(2,1)}, u32[]{:S(2)}, u32[]{:S(2)}) collective-permute-start(bf16[256,1024]{1,0:T(8,128)(2,1)} %collective-permute-done.23.refs_17_), channel_id=1, source_target_pairs={{0,8},{8,0},{16,24},{24,16},{1,9},{9,1},{17,25},{25,17},{2,10},{10... | collective-permute-start | bytes 1572872 | tf_op jit(solution)/shard_map/ppermute | solution.py:32
  130.9 22.5 %collective-permute-start.25 = (bf16[256,1024]{1,0:T(8,128)(2,1)}, bf16[256,1024]{1,0:T(8,128)(2,1)S(1)}, u32[]{:S(2)}, u32[]{:S(2)}) collective-permute-start(bf16[256,1024]{1,0:T(8,128)(2,1)} %collective-permute-done.23.refs_17_), channel_id=1, source_target_pairs={{0,16},{8,24},{16,0},{24,8},{1,17},{9,25},{17,1},{25,9},{2,18},{10... | collective-permute-start | bytes 1572872 | tf_op jit(solution)/shard_map/ppermute | solution.py:32
  153.4 30.1 %collective-permute-start.26 = (bf16[256,1024]{1,0:T(8,128)(2,1)S(1)}, bf16[256,1024]{1,0:T(8,128)(2,1)S(1)}, u32[]{:S(2)}, u32[]{:S(2)}) collective-permute-start(bf16[256,1024]{1,0:T(8,128)(2,1)S(1)} %collective-permute-done.20.refs_15_), channel_id=1, source_target_pairs={{0,8},{8,0},{16,24},{24,16},{1,9},{9,1},{17,25},{25,17},{2,10},{10... | collective-permute-start | bytes 1572872 | tf_op jit(solution)/shard_map/ppermute | solution.py:32
  154.7 28.8 %collective-permute-start.27 = (bf16[256,1024]{1,0:T(8,128)(2,1)}, bf16[256,1024]{1,0:T(8,128)(2,1)S(1)}, u32[]{:S(2)}, u32[]{:S(2)}) collective-permute-start(bf16[256,1024]{1,0:T(8,128)(2,1)} %collective-permute-done.24.refs_19_), channel_id=1, source_target_pairs={{0,16},{8,24},{16,0},{24,8},{1,17},{9,25},{17,1},{25,9},{2,18},{10... | collective-permute-start | bytes 1572872 | tf_op jit(solution)/shard_map/ppermute | solution.py:32
  157.3 43.0 %collective-permute-start.33 = (f32[256,768]{1,0:T(8,128)}, f32[256,768]{1,0:T(8,128)}, u32[]{:S(2)}, u32[]{:S(2)}) collective-permute-start(f32[256,768]{1,0:T(8,128)} %fusion.27), channel_id=1, source_target_pairs={{0,1},{1,0},{2,3},{3,2},{4,5},{5,4},{6,7},{7,6},{8,9},{9,8},{10,11... | collective-permute-start | bytes 2359304 | tf_op jit(solution)/shard_map/ppermute | solution.py:440
  168.1 12.9 %collective-permute-start.35 = (bf16[2,1,48,1536]{3,2,1,0:T(8,128)(2,1)S(1)}, bf16[2,1,48,1536]{3,2,1,0:T(8,128)(2,1)S(1)}, u32[]{:S(2)}, u32[]{:S(2)}) collective-permute-start(bf16[2,1,48,1536]{3,2,1,0:T(8,128)(2,1)S(1)} %fusion.3), channel_id=1, source_target_pairs={{0,8},{8,0},{16,24},{24,16},{1,9},{9,1},{17,25},{25,17},{2,10},{10... | collective-permute-start | bytes 884744 | tf_op jit(solution)/shard_map/ppermute | solution.py:32
  172.5 9.4 %collective-permute-start.37 = (bf16[1,2,48,1536]{3,2,1,0:T(8,128)(2,1)S(1)}, bf16[1,2,48,1536]{3,2,1,0:T(8,128)(2,1)S(1)}, u32[]{:S(2)}, u32[]{:S(2)}) collective-permute-start(bf16[1,2,48,1536]{3,2,1,0:T(8,128)(2,1)S(1)} %fusion.2), channel_id=1, source_target_pairs={{0,16},{8,24},{16,0},{24,8},{1,17},{9,25},{17,1},{25,9},{2,18},{10... | collective-permute-start | bytes 884744 | tf_op jit(solution)/shard_map/ppermute | solution.py:32
  182.0 12.2 %collective-permute-start.38 = (bf16[1,1,48,1536]{3,2,1,0:T(8,128)(2,1)S(1)}, bf16[1,1,48,1536]{3,2,1,0:T(8,128)(2,1)S(1)}, u32[]{:S(2)}, u32[]{:S(2)}) collective-permute-start(bf16[1,1,48,1536]{3,2,1,0:T(8,128)(2,1)S(1)} %dynamic-slice_convert_fusion.1), channel_id=1, source_target_pairs={{0,8},{8,0},{16,24},{24,16},{1,9},{9,1},{17,25},{25,17},{2,10},{10... | collective-permute-start | bytes 442376 | tf_op jit(solution)/shard_map/ppermute | solution.py:32
  (35 other events, 445.3 us)

commit v3 on v2

--- a/solution.py
+++ b/solution.py
@@ -496,7 +496,7 @@
             for key, pair in zip(keys_of, placed(step, plane.slice(r))):
                 (ready if key is None or key in early else late).append(pair)
         values = running(None, after(token_rows, grad_up, grad_down), ready)
-        last_values = (values, token_rows, late)
+        last_values = (after(values, pool_grad), token_rows, late)
     else:
         whole = lax.all_gather(value_weight, "pa", axis=0, tiled=True)
         last_values = (None, token_rows, [(0, whole)])
@@ -504,7 +504,9 @@
     if grouped:
         step = 1
         while step < pa_count:
-            summed = summed + lax.ppermute(summed, "pa", [(i, i ^ step) for i in range(pa_count)])
+            sent = summed.astype(jnp.bfloat16)
+            got = lax.ppermute(sent, "pa", [(i, i ^ step) for i in range(pa_count)])
+            summed = sent.astype(jnp.float32) + got.astype(jnp.float32)
             step *= 2
     else:
         summed = lax.psum(summed, "pa")

time: 204 us -> 201 us (0.985)
  waiting for transfers between devices: 62.2 us -> 57.5 us
    ppermute x2, waiting for transfers between devices: 8.71 us -> 6.2 us  [local(): got = lax.ppermute(sent, 'pa', [(i, i ^ step) for i in range(pa_count)])]
    ppermute x22, waiting for transfers between devices: 25.6 us -> 23.5 us  [flip(): return lax.ppermute(values, 'pb', [(i, i ^ bit) for i in range(count)])]
  transfers between devices with their start and end apart: 39 -> 39, of which waited for: 16 -> 16; matrix products, arithmetic and copies ran while one was open for 17% -> 18% of each run, Pallas kernels for 22% -> 22%
where the time goes in v3:
time: 201 us; the launch traced here: 200 us
  waiting for transfers between devices  57.5 us (29%)
  starting transfers between devices  47.8 us (24%)
  Pallas kernels  43.9 us (22%)
  other arithmetic  24.9 us (12%)
  local copies, waits for them, and re-layouts  18.1 us (9%)
  between operations  5.87 us (3%)
    ppermute x6, waiting for transfers between devices, ring_step(): return lax.ppermute(piece, 'pa', ring_next(lax.axis_size('pa')))  26.7 us
    pallas_call x5, Pallas kernels, projection(): pl.pallas_call(kernel, grid_spec=pltpu.PrefetchScalarGridSpec(num_scalar_...  26.2 us
    ppermute x22, waiting for transfers between devices, flip(): return lax.ppermute(values, 'pb', [(i, i ^ bit) for i in range(count)])  23.5 us
    ppermute x22, starting transfers between devices, flip(): return lax.ppermute(values, 'pb', [(i, i ^ bit) for i in range(count)])  23.2 us
    pallas_call x1, Pallas kernels, backward(): pl.pallas_call(backward_kernel, grid_spec=pltpu.PrefetchScalarGridSpec(nu...  17.7 us
    ppermute x6, starting transfers between devices, ring_step(): return lax.ppermute(piece, 'pa', ring_next(lax.axis_size('pa')))  16.1 us
    add x2, other arithmetic, scatter_sum(): total = total + grads[k] * scalars[k]  9.2 us
    unnamed x57, local copies, waits for them, and re-layouts  6.7 us
  transfers between devices with their start and end apart: 39, of which 16 were waited for; matrix products, arithmetic and copies ran while one was open for 18% of the time, Pallas kernels for 22%

profile of v3, /device:TPU:0, one launch (start us, length us, event | category | flops | bytes accessed | tf_op | source)
XLA Modules:
  0.0 199.8 jit_solution(7695492438864598678)
XLA Ops:
  1.8 4.1 %collective-permute-start = (bf16[256,1024]{1,0:T(8,128)(2,1)S(1)}, bf16[256,1024]{1,0:T(8,128)(2,1)S(1)}, u32[]{:S(2)}, u32[]{:S(2)}) collective-permute-start(bf16[256,1024]{1,0:T(8,128)(2,1)S(1)} %constant_dynamic-slice_fusion.1), channel_id=1, source_target_pairs={{0,4},{4,6},{6,2},{2,0},{1,5},{5,7},{7,3},{3,1},{8,12},{12,14},{14... | collective-permute-start | bytes 1572872 | tf_op jit(solution)/shard_map/ppermute | solution.py:316
  5.9 11.2 %collective-permute-done.refs_3_ = bf16[256,1024]{1,0:T(8,128)(2,1)S(1)} collective-permute-done((bf16[256,1024]{1,0:T(8,128)(2,1)S(1)}, bf16[256,1024]{1,0:T(8,128)(2,1)S(1)}, u32[]{:S(2)}, u32[]{:S(2)}) %collective-permute-start) | collective-permute-done | bytes 524320 | tf_op jit(solution)/shard_map/ppermute | solution.py:316
  17.1 3.4 %collective-permute-start.1 = (bf16[256,1024]{1,0:T(8,128)(2,1)S(1)}, bf16[256,1024]{1,0:T(8,128)(2,1)}, u32[]{:S(2)}, u32[]{:S(2)}) collective-permute-start(bf16[256,1024]{1,0:T(8,128)(2,1)S(1)} %collective-permute-done.refs_3_), channel_id=1, source_target_pairs={{0,4},{4,6},{6,2},{2,0},{1,5},{5,7},{7,3},{3,1},{8,12},{12,14},{14... | collective-permute-start | bytes 1572872 | tf_op jit(solution)/shard_map/ppermute | solution.py:316
  22.1 8.7 %collective-permute-done.1.refs_2_ = bf16[256,1024]{1,0:T(8,128)(2,1)} collective-permute-done((bf16[256,1024]{1,0:T(8,128)(2,1)S(1)}, bf16[256,1024]{1,0:T(8,128)(2,1)}, u32[]{:S(2)}, u32[]{:S(2)}) %collective-permute-start.1) | collective-permute-done | bytes 524320 | tf_op jit(solution)/shard_map/ppermute | solution.py:316
  30.8 3.5 %collective-permute-start.2 = (bf16[256,1024]{1,0:T(8,128)(2,1)}, bf16[256,1024]{1,0:T(8,128)(2,1)S(1)}, u32[]{:S(2)}, u32[]{:S(2)}) collective-permute-start(bf16[256,1024]{1,0:T(8,128)(2,1)} %collective-permute-done.1.refs_2_), channel_id=1, source_target_pairs={{0,4},{4,6},{6,2},{2,0},{1,5},{5,7},{7,3},{3,1},{8,12},{12,14},{14... | collective-permute-start | bytes 1572872 | tf_op jit(solution)/shard_map/ppermute | solution.py:316
  37.9 1.9 constant_dynamic-slice_fusion.2
  40.8 3.1 %collective-permute-done.2.refs_2_ = bf16[256,1024]{1,0:T(8,128)(2,1)S(1)} collective-permute-done((bf16[256,1024]{1,0:T(8,128)(2,1)}, bf16[256,1024]{1,0:T(8,128)(2,1)S(1)}, u32[]{:S(2)}, u32[]{:S(2)}) %collective-permute-start.2) | collective-permute-done | bytes 524320 | tf_op jit(solution)/shard_map/ppermute | solution.py:316
  43.9 3.3 %collective-permute-start.3 = (bf16[256,1024]{1,0:T(8,128)(2,1)}, bf16[256,1024]{1,0:T(8,128)(2,1)}, u32[]{:S(2)}, u32[]{:S(2)}) collective-permute-start(bf16[256,1024]{1,0:T(8,128)(2,1)} %constant_dynamic-slice_fusion.2), channel_id=1, source_target_pairs={{0,4},{4,6},{6,2},{2,0},{1,5},{5,7},{7,3},{3,1},{8,12},{12,14},{14... | collective-permute-start | bytes 1572872 | tf_op jit(solution)/shard_map/ppermute | solution.py:316
  48.0 1.8 collective-permute-done.8.refs_5_
  65.3 2.1 %multiply_bitcast_fusion = bf16[4,64,4,4,32]{1,0,4,3,2:T(4,128)(2,1)} fusion(bf16[4,4]{0,1:T(4,128)(2,1)S(1)} %fusion.9, bf16[32,4,4,64]{3,2,1,0:T(4,128)(2,1)} %reshape_squeeze.5), kind=kLoop, calls=%fused_computation.12 | loop fusion | flops 524288 | bytes 327712 | tf_op jit(solution)/shard_map/abgj,gh->gjbha/transpose | solution.py:366
  67.3 5.0 %collective-permute-done.10.refs_9_ = bf16[256,1024]{1,0:T(8,128)(2,1)} collective-permute-done((bf16[256,1024]{1,0:T(8,128)(2,1)}, bf16[256,1024]{1,0:T(8,128)(2,1)}, u32[]{:S(2)}, u32[]{:S(2)}) %collective-permute-start.10) | collective-permute-done | bytes 524320 | tf_op jit(solution)/shard_map/ppermute | solution.py:32
  74.4 3.7 %collective-permute-done.4.refs_11_ = bf16[256,1024]{1,0:T(8,128)(2,1)} collective-permute-done((bf16[256,1024]{1,0:T(8,128)(2,1)}, bf16[256,1024]{1,0:T(8,128)(2,1)}, u32[]{:S(2)}, u32[]{:S(2)}) %collective-permute-start.4) | collective-permute-done | bytes 524320 | tf_op jit(solution)/shard_map/ppermute | solution.py:316
  78.9 2.5 %collective-permute-done.13.refs_8_ = bf16[256,1024]{1,0:T(8,128)(2,1)S(1)} collective-permute-done((bf16[256,1024]{1,0:T(8,128)(2,1)}, bf16[256,1024]{1,0:T(8,128)(2,1)S(1)}, u32[]{:S(2)}, u32[]{:S(2)}) %collective-permute-start.13) | collective-permute-done | bytes 524320 | tf_op jit(solution)/shard_map/ppermute | solution.py:32
  84.3 2.2 %reshape.310 = bf16[256,512]{0,1:T(8,128)(2,1)} reshape(bf16[4,64,4,4,32]{1,0,4,3,2:T(4,128)(2,1)} %multiply_bitcast_fusion) | data formatting | bytes 524288 | tf_op jit(solution)/shard_map/reshape | solution.py:368
  89.2 2.2 %copy-done.1 = bf16[1,2,256,4096]{3,2,1,0:T(8,128)(2,1)S(1)} copy-done((bf16[1,2,256,4096]{3,2,1,0:T(8,128)(2,1)S(1)}, bf16[1,2,256,4096]{3,2,1,0:T(8,128)(2,1)}, u32[]{:S(2)}) %copy-start.1) | copy-done | bytes 4194328
  92.4 5.2 %shard_map.183.refs_0_ = f32[512,1024]{1,0:T(8,128)S(1)} custom-call(s32[5]{0:T(128)S(1)} %stack.119.places_ref, bf16[512,4096]{1,0:T(8,128)(2,1)S(1)} %bitcast.79, bf16[1024,1024]{1,0:T(8,128)(2,1)S(1)} %copy-done.3, bf16[512,4096]{1,0:T(8,128)(2,1)S(1)} %bitcast.80, bf16[256,1024]{1,0:T(8,128)(2,1)S(1)} %collective-permute-done.refs_3_, ...), custom_call_target="tpu_custom_call" | custom-call | flops 2147483648 | bytes 8388608 | tf_op jit(solution)/shard_map/pallas_call | solution.py:118
  97.6 4.3 %shard_map.184.refs_0_ = f32[512,1024]{1,0:T(8,128)S(1)} custom-call(s32[4]{0:T(128)S(1)} %get-tuple-element.68.places_ref, f32[512,1024]{1,0:T(8,128)S(1)} %shard_map.183.refs_0_, bf16[512,4096]{1,0:T(8,128)(2,1)S(1)} %bitcast.84, bf16[256,1024]{1,0:T(8,128)(2,1)} %collective-permute-done.1.refs_2_, bf16[512,4096]{1,0:T(8,128)(2,1)S(1)} %bitcast.85, ...), custom_call_target="tpu_custom_call" | custom-call | flops 1073741824 | bytes 8388608 | tf_op jit(solution)/shard_map/pallas_call | solution.py:118
  102.1 5.7 %shard_map.185 = (f32[512,512]{1,0:T(8,128)S(1)}, f32[3,512]{1,0:T(4,128)S(1)}) custom-call(s32[4]{0:T(128)S(1)} %get-tuple-element.67.places_ref, f32[512,1024]{1,0:T(8,128)S(1)} %shard_map.184.refs_0_, bf16[512,4096]{1,0:T(8,128)(2,1)S(1)} %bitcast.91, bf16[256,1024]{1,0:T(8,128)(2,1)S(1)} %copy-done.10, bf16[512,4096]{1,0:T(8,128)(2,1)S(1)} %bitcast.89, ...), custom_call_target="tpu_custom_call" | custom-call | flops 1073741824 | bytes 8388608 | tf_op jit(solution)/shard_map/pallas_call | solution.py:118
  108.8 2.9 %collective-permute-start.27 = (f32[3,512]{1,0:T(4,128)S(1)}, f32[3,512]{1,0:T(4,128)S(1)}, u32[]{:S(2)}, u32[]{:S(2)}) collective-permute-start(f32[3,512]{1,0:T(4,128)S(1)} %get-tuple-element.39), channel_id=1, source_target_pairs={{2,0},{4,2},{6,4},{0,6},{3,1},{5,3},{7,5},{1,7},{10,8},{12,10},{14... | collective-permute-start | bytes 18440 | tf_op jit(solution)/shard_map/ppermute | solution.py:446
  111.8 1.6 pad_maximum_fusion.mine_ref
  115.2 1.9 collective-permute-start.23
  120.2 8.6 %collective-permute-done.18.refs_5_ = bf16[256,1024]{1,0:T(8,128)(2,1)} collective-permute-done((bf16[256,1024]{1,0:T(8,128)(2,1)}, bf16[256,1024]{1,0:T(8,128)(2,1)}, u32[]{:S(2)}, u32[]{:S(2)}) %collective-permute-start.18) | collective-permute-done | bytes 524320 | tf_op jit(solution)/shard_map/ppermute | solution.py:32
  133.1 17.7 %shard_map.186 = (f32[4,192,1536]{2,1,0:T(8,128)}, f32[4,192,1536]{2,1,0:T(8,128)}, f32[4,1,128]{2,1,0:T(1,128)S(1)}, f32[256,768]{1,0:T(8,128)S(1)}, bf16[256,1536]{1,0:T(8,128)(2,1)S(1)}) custom-call(s32[1]{0:T(128)} %bitcast.17.place_ref, bf16[4,272,768]{2,1,0:T(8,128)(2,1)S(1)} %pad_maximum_fusion.mine_ref, ...), custom_call_target="tpu_custom_call" | custom-call | flops 6039797760 | bytes 25165824 | tf_op jit(solution)/shard_map/pallas_call | solution.py:289
  150.8 1.7 fusion.25
  161.2 5.6 %multiply_add_fusion.1 = f32[1,192,1536]{2,1,0:T(8,128)S(1)} fusion(f32[4,192,1536]{2,1,0:T(8,128)} %get-tuple-element.41, f32[]{:T(128)} %bitcast.40, f32[]{:T(128)} %bitcast.39, f32[]{:T(128)} %bitcast.38, f32[]{:T(128)} %bitcast.33), kind=kLoop, calls=%fused_computation.4 | loop fusion | flops 2064384 | bytes 5898256 | tf_op jit(solution)/shard_map/add | solution.py:474
  167.5 3.6 %multiply_add_fusion = f32[1,192,1536]{2,1,0:T(8,128)S(1)} fusion(f32[4,192,1536]{2,1,0:T(8,128)S(1)} %copy-done.17, f32[]{:T(128)} %bitcast.40, f32[]{:T(128)} %bitcast.39, f32[]{:T(128)} %bitcast.38, f32[]{:T(128)} %bitcast.33), kind=kLoop, calls=%fused_computation.3 | loop fusion | flops 2064384 | bytes 5898256 | tf_op jit(solution)/shard_map/add | solution.py:474
  172.5 7.1 %shard_map.187.refs_0_ = f32[512,1024]{1,0:T(8,128)S(1)} custom-call(s32[11]{0:T(128)S(1)} %stack.111.places_ref, bf16[512,4096]{1,0:T(8,128)(2,1)S(1)} %bitcast.92, bf16[1024,1024]{1,0:T(8,128)(2,1)S(1)} %copy-done.4, bf16[512,4096]{1,0:T(8,128)(2,1)S(1)} %bitcast.93, bf16[256,1024]{1,0:T(8,128)(2,1)} %collective-permute-done.3.refs_3_, ...), custom_call_target="tpu_custom_call" | custom-call | flops 3758096384 | bytes 8388608 | tf_op jit(solution)/shard_map/pallas_call | solution.py:118
  182.1 2.9 %fusion.1 = bf16[1,256,768]{2,1,0:T(8,128)(2,1)} fusion(f32[256,768]{1,0:T(8,128)} %collective-permute-done.26, f32[256,768]{1,0:T(8,128)S(1)} %copy-done.6, f32[256,768]{1,0:T(8,128)} %fusion.25, f32[]{:T(128)} %bitcast.33), kind=kLoop, calls=%fused_computation.13 | loop fusion | flops 786432 | bytes 2752516 | tf_op jit(solution)/shard_map/broadcast_in_dim | solution.py:469
  185.0 3.9 %shard_map.188 = f32[32,1024]{1,0:T(8,128)S(1)} custom-call(s32[2]{0:T(128)S(1)} %pad_add_fusion.places_ref, f32[512,1024]{1,0:T(8,128)S(1)} %shard_map.187.refs_0_, bf16[512,4096]{1,0:T(8,128)(2,1)S(1)} %bitcast.103, bf16[256,1024]{1,0:T(8,128)(2,1)S(1)} %collective-permute-done.31.refs_2_, bf16[512,4096]{1,0:T(8,128)(2,1)S(1)} %bitcast.104, ...), custom_call_target="tpu_custom_call" | custom-call | flops 536870912 | bytes 8388608 | tf_op jit(solution)/shard_map/pallas_call | solution.py:118
  190.2 3.1 %collective-permute-done.33 = bf16[32,1024]{1,0:T(8,128)(2,1)S(1)} collective-permute-done((bf16[32,1024]{1,0:T(8,128)(2,1)S(1)}, bf16[32,1024]{1,0:T(8,128)(2,1)S(1)}, u32[]{:S(2)}, u32[]{:S(2)}) %collective-permute-start.33) | collective-permute-done | bytes 65568 | tf_op jit(solution)/shard_map/ppermute | solution.py:508
  193.3 1.9 collective-permute-start.34
  196.0 3.1 %collective-permute-done.34 = bf16[32,1024]{1,0:T(8,128)(2,1)S(1)} collective-permute-done((bf16[32,1024]{1,0:T(8,128)(2,1)S(1)}, bf16[32,1024]{1,0:T(8,128)(2,1)S(1)}, u32[]{:S(2)}, u32[]{:S(2)}) %collective-permute-start.34) | collective-permute-done | bytes 65568 | tf_op jit(solution)/shard_map/ppermute | solution.py:508
  (177 shorter events, 54.6 us)
Async XLA Ops:
  1.8 15.3 %collective-permute-start = (bf16[256,1024]{1,0:T(8,128)(2,1)S(1)}, bf16[256,1024]{1,0:T(8,128)(2,1)S(1)}, u32[]{:S(2)}, u32[]{:S(2)}) collective-permute-start(bf16[256,1024]{1,0:T(8,128)(2,1)S(1)} %constant_dynamic-slice_fusion.1), channel_id=1, source_target_pairs={{0,4},{4,6},{6,2},{2,0},{1,5},{5,7},{7,3},{3,1},{8,12},{12,14},{14... | collective-permute-start | bytes 1572872 | tf_op jit(solution)/shard_map/ppermute | solution.py:316
  17.1 13.7 %collective-permute-start.1 = (bf16[256,1024]{1,0:T(8,128)(2,1)S(1)}, bf16[256,1024]{1,0:T(8,128)(2,1)}, u32[]{:S(2)}, u32[]{:S(2)}) collective-permute-start(bf16[256,1024]{1,0:T(8,128)(2,1)S(1)} %collective-permute-done.refs_3_), channel_id=1, source_target_pairs={{0,4},{4,6},{6,2},{2,0},{1,5},{5,7},{7,3},{3,1},{8,12},{12,14},{14... | collective-permute-start | bytes 1572872 | tf_op jit(solution)/shard_map/ppermute | solution.py:316
  30.8 13.2 %collective-permute-start.2 = (bf16[256,1024]{1,0:T(8,128)(2,1)}, bf16[256,1024]{1,0:T(8,128)(2,1)S(1)}, u32[]{:S(2)}, u32[]{:S(2)}) collective-permute-start(bf16[256,1024]{1,0:T(8,128)(2,1)} %collective-permute-done.1.refs_2_), channel_id=1, source_target_pairs={{0,4},{4,6},{6,2},{2,0},{1,5},{5,7},{7,3},{3,1},{8,12},{12,14},{14... | collective-permute-start | bytes 1572872 | tf_op jit(solution)/shard_map/ppermute | solution.py:316
  34.9 14.9 %collective-permute-start.8 = (bf16[256,1024]{1,0:T(8,128)(2,1)S(1)}, bf16[256,1024]{1,0:T(8,128)(2,1)S(1)}, u32[]{:S(2)}, u32[]{:S(2)}) collective-permute-start(bf16[256,1024]{1,0:T(8,128)(2,1)S(1)} %collective-permute-done.refs_3_), channel_id=1, source_target_pairs={{0,8},{8,0},{16,24},{24,16},{1,9},{9,1},{17,25},{25,17},{2,10},{10... | collective-permute-start | bytes 1572872 | tf_op jit(solution)/shard_map/ppermute | solution.py:32
  36.4 15.0 %collective-permute-start.9 = (bf16[256,1024]{1,0:T(8,128)(2,1)S(1)}, bf16[256,1024]{1,0:T(8,128)(2,1)}, u32[]{:S(2)}, u32[]{:S(2)}) collective-permute-start(bf16[256,1024]{1,0:T(8,128)(2,1)S(1)} %collective-permute-done.refs_3_), channel_id=1, source_target_pairs={{0,16},{8,24},{16,0},{24,8},{1,17},{9,25},{17,1},{25,9},{2,18},{10... | collective-permute-start | bytes 1572872 | tf_op jit(solution)/shard_map/ppermute | solution.py:32
  39.8 21.3 %collective-permute-start.11 = (bf16[256,1024]{1,0:T(8,128)(2,1)}, bf16[256,1024]{1,0:T(8,128)(2,1)}, u32[]{:S(2)}, u32[]{:S(2)}) collective-permute-start(bf16[256,1024]{1,0:T(8,128)(2,1)} %collective-permute-done.1.refs_2_), channel_id=1, source_target_pairs={{0,8},{8,0},{16,24},{24,16},{1,9},{9,1},{17,25},{25,17},{2,10},{10... | collective-permute-start | bytes 1572872 | tf_op jit(solution)/shard_map/ppermute | solution.py:32
  40.3 22.3 %collective-permute-start.12 = (bf16[256,1024]{1,0:T(8,128)(2,1)}, bf16[256,1024]{1,0:T(8,128)(2,1)}, u32[]{:S(2)}, u32[]{:S(2)}) collective-permute-start(bf16[256,1024]{1,0:T(8,128)(2,1)} %collective-permute-done.1.refs_2_), channel_id=1, source_target_pairs={{0,16},{8,24},{16,0},{24,8},{1,17},{9,25},{17,1},{25,9},{2,18},{10... | collective-permute-start | bytes 1572872 | tf_op jit(solution)/shard_map/ppermute | solution.py:32
  43.9 20.2 %collective-permute-start.3 = (bf16[256,1024]{1,0:T(8,128)(2,1)}, bf16[256,1024]{1,0:T(8,128)(2,1)}, u32[]{:S(2)}, u32[]{:S(2)}) collective-permute-start(bf16[256,1024]{1,0:T(8,128)(2,1)} %constant_dynamic-slice_fusion.2), channel_id=1, source_target_pairs={{0,4},{4,6},{6,2},{2,0},{1,5},{5,7},{7,3},{3,1},{8,12},{12,14},{14... | collective-permute-start | bytes 1572872 | tf_op jit(solution)/shard_map/ppermute | solution.py:316
  51.3 21.0 %collective-permute-start.10 = (bf16[256,1024]{1,0:T(8,128)(2,1)}, bf16[256,1024]{1,0:T(8,128)(2,1)}, u32[]{:S(2)}, u32[]{:S(2)}) collective-permute-start(bf16[256,1024]{1,0:T(8,128)(2,1)} %collective-permute-done.9.refs_7_), channel_id=1, source_target_pairs={{0,8},{8,0},{16,24},{24,16},{1,9},{9,1},{17,25},{25,17},{2,10},{10... | collective-permute-start | bytes 1572872 | tf_op jit(solution)/shard_map/ppermute | solution.py:32
  52.1 21.8 %collective-permute-start.15 = (bf16[256,1024]{1,0:T(8,128)(2,1)S(1)}, bf16[256,1024]{1,0:T(8,128)(2,1)}, u32[]{:S(2)}, u32[]{:S(2)}) collective-permute-start(bf16[256,1024]{1,0:T(8,128)(2,1)S(1)} %collective-permute-done.2.refs_2_), channel_id=1, source_target_pairs={{0,16},{8,24},{16,0},{24,8},{1,17},{9,25},{17,1},{25,9},{2,18},{10... | collective-permute-start | bytes 1572872 | tf_op jit(solution)/shard_map/ppermute | solution.py:32
  62.6 18.8 %collective-permute-start.13 = (bf16[256,1024]{1,0:T(8,128)(2,1)}, bf16[256,1024]{1,0:T(8,128)(2,1)S(1)}, u32[]{:S(2)}, u32[]{:S(2)}) collective-permute-start(bf16[256,1024]{1,0:T(8,128)(2,1)} %collective-permute-done.11.refs_4_), channel_id=1, source_target_pairs={{0,16},{8,24},{16,0},{24,8},{1,17},{9,25},{17,1},{25,9},{2,18},{10... | collective-permute-start | bytes 1572872 | tf_op jit(solution)/shard_map/ppermute | solution.py:32
  64.1 14.1 %collective-permute-start.4 = (bf16[256,1024]{1,0:T(8,128)(2,1)}, bf16[256,1024]{1,0:T(8,128)(2,1)}, u32[]{:S(2)}, u32[]{:S(2)}) collective-permute-start(bf16[256,1024]{1,0:T(8,128)(2,1)} %collective-permute-done.3.refs_3_), channel_id=1, source_target_pairs={{0,4},{4,6},{6,2},{2,0},{1,5},{5,7},{7,3},{3,1},{8,12},{12,14},{14... | collective-permute-start | bytes 1572872 | tf_op jit(solution)/shard_map/ppermute | solution.py:316
  64.7 23.0 %collective-permute-start.14 = (bf16[256,1024]{1,0:T(8,128)(2,1)S(1)}, bf16[256,1024]{1,0:T(8,128)(2,1)}, u32[]{:S(2)}, u32[]{:S(2)}) collective-permute-start(bf16[256,1024]{1,0:T(8,128)(2,1)S(1)} %collective-permute-done.2.refs_2_), channel_id=1, source_target_pairs={{0,8},{8,0},{16,24},{24,16},{1,9},{9,1},{17,25},{25,17},{2,10},{10... | collective-permute-start | bytes 1572872 | tf_op jit(solution)/shard_map/ppermute | solution.py:32
  73.8 28.2 %collective-permute-start.16 = (bf16[256,1024]{1,0:T(8,128)(2,1)}, bf16[256,1024]{1,0:T(8,128)(2,1)}, u32[]{:S(2)}, u32[]{:S(2)}) collective-permute-start(bf16[256,1024]{1,0:T(8,128)(2,1)} %collective-permute-done.15.refs_6_), channel_id=1, source_target_pairs={{0,8},{8,0},{16,24},{24,16},{1,9},{9,1},{17,25},{25,17},{2,10},{10... | collective-permute-start | bytes 1572872 | tf_op jit(solution)/shard_map/ppermute | solution.py:32
  78.2 30.4 %collective-permute-start.7 = (bf16[272,768]{1,0:T(8,128)(2,1)}, bf16[272,768]{1,0:T(8,128)(2,1)}, u32[]{:S(2)}, u32[]{:S(2)}) collective-permute-start(bf16[272,768]{1,0:T(8,128)(2,1)} %concatenate.11), channel_id=1, source_target_pairs={{6,0},{0,2},{2,4},{4,6},{7,1},{1,3},{3,5},{5,7},{14,8},{8,10},{10,... | collective-permute-start | bytes 1253384 | tf_op jit(solution)/shard_map/ppermute | solution.py:385
  78.2 30.6 %collective-permute-start.6 = (bf16[272,768]{1,0:T(8,128)(2,1)}, bf16[272,768]{1,0:T(8,128)(2,1)}, u32[]{:S(2)}, u32[]{:S(2)}) collective-permute-start(bf16[272,768]{1,0:T(8,128)(2,1)} %concatenate.11), channel_id=1, source_target_pairs={{4,0},{6,2},{0,4},{2,6},{5,1},{7,3},{1,5},{3,7},{12,8},{14,10},{8,... | collective-permute-start | bytes 1253384 | tf_op jit(solution)/shard_map/ppermute | solution.py:385
  82.2 29.6 %collective-permute-start.5 = (bf16[272,768]{1,0:T(8,128)(2,1)}, bf16[272,768]{1,0:T(8,128)(2,1)}, u32[]{:S(2)}, u32[]{:S(2)}) collective-permute-start(bf16[272,768]{1,0:T(8,128)(2,1)} %concatenate.11), channel_id=1, source_target_pairs={{2,0},{4,2},{6,4},{0,6},{3,1},{5,3},{7,5},{1,7},{10,8},{12,10},{14... | collective-permute-start | bytes 1253384 | tf_op jit(solution)/shard_map/ppermute | solution.py:385
  87.7 26.0 %collective-permute-start.19 = (bf16[256,1024]{1,0:T(8,128)(2,1)}, bf16[256,1024]{1,0:T(8,128)(2,1)}, u32[]{:S(2)}, u32[]{:S(2)}) collective-permute-start(bf16[256,1024]{1,0:T(8,128)(2,1)} %collective-permute-done.3.refs_3_), channel_id=1, source_target_pairs={{0,16},{8,24},{16,0},{24,8},{1,17},{9,25},{17,1},{25,9},{2,18},{10... | collective-permute-start | bytes 1572872 | tf_op jit(solution)/shard_map/ppermute | solution.py:32
  113.4 18.8 %collective-permute-start.17 = (bf16[4,272,768]{2,1,0:T(8,128)(2,1)S(1)}, bf16[4,272,768]{2,1,0:T(8,128)(2,1)}, u32[]{:S(2)}, u32[]{:S(2)}) collective-permute-start(bf16[4,272,768]{2,1,0:T(8,128)(2,1)S(1)} %pad_maximum_fusion.mine_ref), channel_id=1, source_target_pairs={{0,1},{1,0},{2,3},{3,2},{4,5},{5,4},{6,7},{7,6},{8,9},{9,8},{10,11... | collective-permute-start | bytes 5013512 | tf_op jit(solution)/shard_map/ppermute | solution.py:404
  113.7 15.1 %collective-permute-start.18 = (bf16[256,1024]{1,0:T(8,128)(2,1)}, bf16[256,1024]{1,0:T(8,128)(2,1)}, u32[]{:S(2)}, u32[]{:S(2)}) collective-permute-start(bf16[256,1024]{1,0:T(8,128)(2,1)} %collective-permute-done.3.refs_3_), channel_id=1, source_target_pairs={{0,8},{8,0},{16,24},{24,16},{1,9},{9,1},{17,25},{25,17},{2,10},{10... | collective-permute-start | bytes 1572872 | tf_op jit(solution)/shard_map/ppermute | solution.py:32
  114.4 14.4 %collective-permute-start.20 = (bf16[256,1024]{1,0:T(8,128)(2,1)}, bf16[256,1024]{1,0:T(8,128)(2,1)S(1)}, u32[]{:S(2)}, u32[]{:S(2)}) collective-permute-start(bf16[256,1024]{1,0:T(8,128)(2,1)} %collective-permute-done.4.refs_11_), channel_id=1, source_target_pairs={{0,16},{8,24},{16,0},{24,8},{1,17},{9,25},{17,1},{25,9},{2,18},{10... | collective-permute-start | bytes 1572872 | tf_op jit(solution)/shard_map/ppermute | solution.py:32
  115.2 14.5 %collective-permute-start.23 = (bf16[256,1024]{1,0:T(8,128)(2,1)}, bf16[256,1024]{1,0:T(8,128)(2,1)}, u32[]{:S(2)}, u32[]{:S(2)}) collective-permute-start(bf16[256,1024]{1,0:T(8,128)(2,1)} %collective-permute-done.4.refs_11_), channel_id=1, source_target_pairs={{0,4},{4,6},{6,2},{2,0},{1,5},{5,7},{7,3},{3,1},{8,12},{12,14},{14... | collective-permute-start | bytes 1572872 | tf_op jit(solution)/shard_map/ppermute | solution.py:316
  118.4 34.4 %collective-permute-start.22 = (bf16[256,1024]{1,0:T(8,128)(2,1)}, bf16[256,1024]{1,0:T(8,128)(2,1)}, u32[]{:S(2)}, u32[]{:S(2)}) collective-permute-start(bf16[256,1024]{1,0:T(8,128)(2,1)} %collective-permute-done.4.refs_11_), channel_id=1, source_target_pairs={{0,8},{8,0},{16,24},{24,16},{1,9},{9,1},{17,25},{25,17},{2,10},{10... | collective-permute-start | bytes 1572872 | tf_op jit(solution)/shard_map/ppermute | solution.py:32
  128.8 42.3 %collective-permute-start.21 = (bf16[256,1024]{1,0:T(8,128)(2,1)}, bf16[256,1024]{1,0:T(8,128)(2,1)}, u32[]{:S(2)}, u32[]{:S(2)}) collective-permute-start(bf16[256,1024]{1,0:T(8,128)(2,1)} %collective-permute-done.18.refs_5_), channel_id=1, source_target_pairs={{0,16},{8,24},{16,0},{24,8},{1,17},{9,25},{17,1},{25,9},{2,18},{10... | collective-permute-start | bytes 1572872 | tf_op jit(solution)/shard_map/ppermute | solution.py:32
  129.6 30.7 %collective-permute-start.24 = (bf16[256,1024]{1,0:T(8,128)(2,1)}, bf16[256,1024]{1,0:T(8,128)(2,1)}, u32[]{:S(2)}, u32[]{:S(2)}) collective-permute-start(bf16[256,1024]{1,0:T(8,128)(2,1)} %collective-permute-done.23.refs_17_), channel_id=1, source_target_pairs={{0,8},{8,0},{16,24},{24,16},{1,9},{9,1},{17,25},{25,17},{2,10},{10... | collective-permute-start | bytes 1572872 | tf_op jit(solution)/shard_map/ppermute | solution.py:32
  130.9 22.5 %collective-permute-start.25 = (bf16[256,1024]{1,0:T(8,128)(2,1)}, bf16[256,1024]{1,0:T(8,128)(2,1)S(1)}, u32[]{:S(2)}, u32[]{:S(2)}) collective-permute-start(bf16[256,1024]{1,0:T(8,128)(2,1)} %collective-permute-done.23.refs_17_), channel_id=1, source_target_pairs={{0,16},{8,24},{16,0},{24,8},{1,17},{9,25},{17,1},{25,9},{2,18},{10... | collective-permute-start | bytes 1572872 | tf_op jit(solution)/shard_map/ppermute | solution.py:32
  152.6 29.6 %collective-permute-start.26 = (f32[256,768]{1,0:T(8,128)}, f32[256,768]{1,0:T(8,128)}, u32[]{:S(2)}, u32[]{:S(2)}) collective-permute-start(f32[256,768]{1,0:T(8,128)} %fusion.25), channel_id=1, source_target_pairs={{0,1},{1,0},{2,3},{3,2},{4,5},{5,4},{6,7},{7,6},{8,9},{9,8},{10,11... | collective-permute-start | bytes 2359304 | tf_op jit(solution)/shard_map/ppermute | solution.py:440
  154.2 30.8 %collective-permute-start.31 = (bf16[256,1024]{1,0:T(8,128)(2,1)S(1)}, bf16[256,1024]{1,0:T(8,128)(2,1)S(1)}, u32[]{:S(2)}, u32[]{:S(2)}) collective-permute-start(bf16[256,1024]{1,0:T(8,128)(2,1)S(1)} %collective-permute-done.20.refs_15_), channel_id=1, source_target_pairs={{0,8},{8,0},{16,24},{24,16},{1,9},{9,1},{17,25},{25,17},{2,10},{10... | collective-permute-start | bytes 1572872 | tf_op jit(solution)/shard_map/ppermute | solution.py:32
  160.3 24.7 %collective-permute-start.32 = (bf16[256,1024]{1,0:T(8,128)(2,1)}, bf16[256,1024]{1,0:T(8,128)(2,1)S(1)}, u32[]{:S(2)}, u32[]{:S(2)}) collective-permute-start(bf16[256,1024]{1,0:T(8,128)(2,1)} %collective-permute-done.24.refs_19_), channel_id=1, source_target_pairs={{0,16},{8,24},{16,0},{24,8},{1,17},{9,25},{17,1},{25,9},{2,18},{10... | collective-permute-start | bytes 1572872 | tf_op jit(solution)/shard_map/ppermute | solution.py:32
  166.8 12.8 %collective-permute-start.35 = (bf16[2,1,48,1536]{3,2,1,0:T(8,128)(2,1)S(1)}, bf16[2,1,48,1536]{3,2,1,0:T(8,128)(2,1)S(1)}, u32[]{:S(2)}, u32[]{:S(2)}) collective-permute-start(bf16[2,1,48,1536]{3,2,1,0:T(8,128)(2,1)S(1)} %fusion.3), channel_id=1, source_target_pairs={{0,8},{8,0},{16,24},{24,16},{1,9},{9,1},{17,25},{25,17},{2,10},{10... | collective-permute-start | bytes 884744 | tf_op jit(solution)/shard_map/ppermute | solution.py:32
  179.7 9.8 %collective-permute-start.36 = (bf16[1,1,48,1536]{3,2,1,0:T(8,128)(2,1)S(1)}, bf16[1,1,48,1536]{3,2,1,0:T(8,128)(2,1)S(1)}, u32[]{:S(2)}, u32[]{:S(2)}) collective-permute-start(bf16[1,1,48,1536]{3,2,1,0:T(8,128)(2,1)S(1)} %dynamic-slice_convert_fusion.2), channel_id=1, source_target_pairs={{0,16},{8,24},{16,0},{24,8},{1,17},{9,25},{17,1},{25,9},{2,18},{10... | collective-permute-start | bytes 442376 | tf_op jit(solution)/shard_map/ppermute | solution.py:32
  180.6 14.6 %collective-permute-start.38 = (bf16[1,1,48,1536]{3,2,1,0:T(8,128)(2,1)S(1)}, bf16[1,1,48,1536]{3,2,1,0:T(8,128)(2,1)S(1)}, u32[]{:S(2)}, u32[]{:S(2)}) collective-permute-start(bf16[1,1,48,1536]{3,2,1,0:T(8,128)(2,1)S(1)} %dynamic-slice_convert_fusion.1), channel_id=1, source_target_pairs={{0,8},{8,0},{16,24},{24,16},{1,9},{9,1},{17,25},{25,17},{2,10},{10... | collective-permute-start | bytes 442376 | tf_op jit(solution)/shard_map/ppermute | solution.py:32
  (35 other events, 425.2 us)

commit v4 on v3

--- a/solution.py
+++ b/solution.py
@@ -302,7 +302,7 @@
             jax.ShapeDtypeStruct((tokens, width), jnp.float32),
             jax.ShapeDtypeStruct((tokens, hidden), jnp.bfloat16),
         ],
-        compiler_params=pltpu.CompilerParams(vmem_limit_bytes=48 << 20),
+        compiler_params=pltpu.CompilerParams(vmem_limit_bytes=32 << 20),
         cost_estimate=pl.CostEstimate(flops=flops, bytes_accessed=24 << 20, transcendentals=2 * count * tokens * hidden),
     )(place, mine, other, up_weight, up_bias, down_weight, gain, query, chosen)
 

time: 201 us -> 204 us (1.015)
  local copies, waits for them, and re-layouts: 18.1 us -> 25.7 us
  waiting for transfers between devices: 57.5 us -> 54.5 us
  Pallas kernels: 43.9 us -> 41.2 us
    unnamed x57 -> x63, local copies, waits for them, and re-layouts: 6.7 us -> 14.3 us
    pallas_call x1, Pallas kernels: 17.7 us -> 15 us  [backward(): pl.pallas_call(backward_kernel, grid_spec=pltpu.PrefetchScalarGridSpec(nu...]
    ppermute x2, waiting for transfers between devices: 6.2 us -> 3.66 us  [local(): got = lax.ppermute(sent, 'pa', [(i, i ^ step) for i in range(pa_count)])]
  transfers between devices with their start and end apart: 39 -> 39, of which waited for: 16 -> 15; matrix products, arithmetic and copies ran while one was open for 18% -> 18% of each run, Pallas kernels for 22% -> 20%
where the time goes in v4:
time: 204 us; the launch traced here: 203 us
  waiting for transfers between devices  54.5 us (27%)
  starting transfers between devices  49.4 us (24%)
  Pallas kernels  41.2 us (20%)
  local copies, waits for them, and re-layouts  25.7 us (13%)
  other arithmetic  24.8 us (12%)
  between operations  5.81 us (3%)
    ppermute x6, waiting for transfers between devices, ring_step(): return lax.ppermute(piece, 'pa', ring_next(lax.axis_size('pa')))  26.7 us
    pallas_call x5, Pallas kernels, projection(): pl.pallas_call(kernel, grid_spec=pltpu.PrefetchScalarGridSpec(num_scalar_...  26.2 us
    ppermute x22, waiting for transfers between devices, flip(): return lax.ppermute(values, 'pb', [(i, i ^ bit) for i in range(count)])  23 us
    ppermute x22, starting transfers between devices, flip(): return lax.ppermute(values, 'pb', [(i, i ^ bit) for i in range(count)])  22.7 us
    ppermute x6, starting transfers between devices, ring_step(): return lax.ppermute(piece, 'pa', ring_next(lax.axis_size('pa')))  16.1 us
    pallas_call x1, Pallas kernels, backward(): pl.pallas_call(backward_kernel, grid_spec=pltpu.PrefetchScalarGridSpec(nu...  15 us
    unnamed x63, local copies, waits for them, and re-layouts  14.3 us
    add x2, other arithmetic, scatter_sum(): total = total + grads[k] * scalars[k]  9.2 us
  transfers between devices with their start and end apart: 39, of which 15 were waited for; matrix products, arithmetic and copies ran while one was open for 18% of the time, Pallas kernels for 20%

profile of v4, /device:TPU:0, one launch (start us, length us, event | category | flops | bytes accessed | tf_op | source)
XLA Modules:
  0.0 203.1 jit_solution(17360531796456246480)
XLA Ops:
  1.8 4.1 %collective-permute-start = (bf16[256,1024]{1,0:T(8,128)(2,1)S(1)}, bf16[256,1024]{1,0:T(8,128)(2,1)S(1)}, u32[]{:S(2)}, u32[]{:S(2)}) collective-permute-start(bf16[256,1024]{1,0:T(8,128)(2,1)S(1)} %constant_dynamic-slice_fusion.1), channel_id=1, source_target_pairs={{0,4},{4,6},{6,2},{2,0},{1,5},{5,7},{7,3},{3,1},{8,12},{12,14},{14... | collective-permute-start | bytes 1572872 | tf_op jit(solution)/shard_map/ppermute | solution.py:316
  5.9 11.2 %collective-permute-done.refs_3_ = bf16[256,1024]{1,0:T(8,128)(2,1)S(1)} collective-permute-done((bf16[256,1024]{1,0:T(8,128)(2,1)S(1)}, bf16[256,1024]{1,0:T(8,128)(2,1)S(1)}, u32[]{:S(2)}, u32[]{:S(2)}) %collective-permute-start) | collective-permute-done | bytes 524320 | tf_op jit(solution)/shard_map/ppermute | solution.py:316
  17.1 3.4 %collective-permute-start.1 = (bf16[256,1024]{1,0:T(8,128)(2,1)S(1)}, bf16[256,1024]{1,0:T(8,128)(2,1)}, u32[]{:S(2)}, u32[]{:S(2)}) collective-permute-start(bf16[256,1024]{1,0:T(8,128)(2,1)S(1)} %collective-permute-done.refs_3_), channel_id=1, source_target_pairs={{0,4},{4,6},{6,2},{2,0},{1,5},{5,7},{7,3},{3,1},{8,12},{12,14},{14... | collective-permute-start | bytes 1572872 | tf_op jit(solution)/shard_map/ppermute | solution.py:316
  22.1 8.7 %collective-permute-done.1.refs_2_ = bf16[256,1024]{1,0:T(8,128)(2,1)} collective-permute-done((bf16[256,1024]{1,0:T(8,128)(2,1)S(1)}, bf16[256,1024]{1,0:T(8,128)(2,1)}, u32[]{:S(2)}, u32[]{:S(2)}) %collective-permute-start.1) | collective-permute-done | bytes 524320 | tf_op jit(solution)/shard_map/ppermute | solution.py:316
  30.8 3.5 %collective-permute-start.2 = (bf16[256,1024]{1,0:T(8,128)(2,1)}, bf16[256,1024]{1,0:T(8,128)(2,1)S(1)}, u32[]{:S(2)}, u32[]{:S(2)}) collective-permute-start(bf16[256,1024]{1,0:T(8,128)(2,1)} %collective-permute-done.1.refs_2_), channel_id=1, source_target_pairs={{0,4},{4,6},{6,2},{2,0},{1,5},{5,7},{7,3},{3,1},{8,12},{12,14},{14... | collective-permute-start | bytes 1572872 | tf_op jit(solution)/shard_map/ppermute | solution.py:316
  37.9 1.9 constant_dynamic-slice_fusion.2
  40.8 3.1 %collective-permute-done.2.refs_2_ = bf16[256,1024]{1,0:T(8,128)(2,1)S(1)} collective-permute-done((bf16[256,1024]{1,0:T(8,128)(2,1)}, bf16[256,1024]{1,0:T(8,128)(2,1)S(1)}, u32[]{:S(2)}, u32[]{:S(2)}) %collective-permute-start.2) | collective-permute-done | bytes 524320 | tf_op jit(solution)/shard_map/ppermute | solution.py:316
  43.9 3.3 %collective-permute-start.3 = (bf16[256,1024]{1,0:T(8,128)(2,1)}, bf16[256,1024]{1,0:T(8,128)(2,1)}, u32[]{:S(2)}, u32[]{:S(2)}) collective-permute-start(bf16[256,1024]{1,0:T(8,128)(2,1)} %constant_dynamic-slice_fusion.2), channel_id=1, source_target_pairs={{0,4},{4,6},{6,2},{2,0},{1,5},{5,7},{7,3},{3,1},{8,12},{12,14},{14... | collective-permute-start | bytes 1572872 | tf_op jit(solution)/shard_map/ppermute | solution.py:316
  48.0 1.8 collective-permute-done.8.refs_5_
  65.3 2.0 %multiply_bitcast_fusion = bf16[4,64,4,4,32]{1,0,4,3,2:T(4,128)(2,1)} fusion(bf16[4,4]{0,1:T(4,128)(2,1)S(1)} %fusion.9, bf16[32,4,4,64]{3,2,1,0:T(4,128)(2,1)} %reshape_squeeze.5), kind=kLoop, calls=%fused_computation.12 | loop fusion | flops 524288 | bytes 327712 | tf_op jit(solution)/shard_map/abgj,gh->gjbha/transpose | solution.py:366
  67.3 5.0 %collective-permute-done.10.refs_9_ = bf16[256,1024]{1,0:T(8,128)(2,1)} collective-permute-done((bf16[256,1024]{1,0:T(8,128)(2,1)}, bf16[256,1024]{1,0:T(8,128)(2,1)}, u32[]{:S(2)}, u32[]{:S(2)}) %collective-permute-start.10) | collective-permute-done | bytes 524320 | tf_op jit(solution)/shard_map/ppermute | solution.py:32
  74.4 3.7 %collective-permute-done.4.refs_11_ = bf16[256,1024]{1,0:T(8,128)(2,1)} collective-permute-done((bf16[256,1024]{1,0:T(8,128)(2,1)}, bf16[256,1024]{1,0:T(8,128)(2,1)}, u32[]{:S(2)}, u32[]{:S(2)}) %collective-permute-start.4) | collective-permute-done | bytes 524320 | tf_op jit(solution)/shard_map/ppermute | solution.py:316
  78.9 2.5 %collective-permute-done.13.refs_8_ = bf16[256,1024]{1,0:T(8,128)(2,1)S(1)} collective-permute-done((bf16[256,1024]{1,0:T(8,128)(2,1)}, bf16[256,1024]{1,0:T(8,128)(2,1)S(1)}, u32[]{:S(2)}, u32[]{:S(2)}) %collective-permute-start.13) | collective-permute-done | bytes 524320 | tf_op jit(solution)/shard_map/ppermute | solution.py:32
  84.3 2.2 %reshape.310 = bf16[256,512]{0,1:T(8,128)(2,1)} reshape(bf16[4,64,4,4,32]{1,0,4,3,2:T(4,128)(2,1)} %multiply_bitcast_fusion) | data formatting | bytes 524288 | tf_op jit(solution)/shard_map/reshape | solution.py:368
  89.2 2.2 %copy-done.1 = bf16[1,2,256,4096]{3,2,1,0:T(8,128)(2,1)S(1)} copy-done((bf16[1,2,256,4096]{3,2,1,0:T(8,128)(2,1)S(1)}, bf16[1,2,256,4096]{3,2,1,0:T(8,128)(2,1)}, u32[]{:S(2)}) %copy-start.1) | copy-done | bytes 4194328
  92.4 5.2 %shard_map.183.refs_0_ = f32[512,1024]{1,0:T(8,128)S(1)} custom-call(s32[5]{0:T(128)S(1)} %stack.119.places_ref, bf16[512,4096]{1,0:T(8,128)(2,1)S(1)} %bitcast.79, bf16[1024,1024]{1,0:T(8,128)(2,1)S(1)} %copy-done.6, bf16[512,4096]{1,0:T(8,128)(2,1)S(1)} %bitcast.80, bf16[256,1024]{1,0:T(8,128)(2,1)S(1)} %collective-permute-done.refs_3_, ...), custom_call_target="tpu_custom_call" | custom-call | flops 2147483648 | bytes 8388608 | tf_op jit(solution)/shard_map/pallas_call | solution.py:118
  97.6 4.3 %shard_map.184.refs_0_ = f32[512,1024]{1,0:T(8,128)S(1)} custom-call(s32[4]{0:T(128)S(1)} %get-tuple-element.68.places_ref, f32[512,1024]{1,0:T(8,128)S(1)} %shard_map.183.refs_0_, bf16[512,4096]{1,0:T(8,128)(2,1)S(1)} %bitcast.84, bf16[256,1024]{1,0:T(8,128)(2,1)} %collective-permute-done.1.refs_2_, bf16[512,4096]{1,0:T(8,128)(2,1)S(1)} %bitcast.85, ...), custom_call_target="tpu_custom_call" | custom-call | flops 1073741824 | bytes 8388608 | tf_op jit(solution)/shard_map/pallas_call | solution.py:118
  102.1 5.7 %shard_map.185 = (f32[512,512]{1,0:T(8,128)S(1)}, f32[3,512]{1,0:T(4,128)S(1)}) custom-call(s32[4]{0:T(128)S(1)} %get-tuple-element.67.places_ref, f32[512,1024]{1,0:T(8,128)S(1)} %shard_map.184.refs_0_, bf16[512,4096]{1,0:T(8,128)(2,1)S(1)} %bitcast.91, bf16[256,1024]{1,0:T(8,128)(2,1)S(1)} %copy-done.13, bf16[512,4096]{1,0:T(8,128)(2,1)S(1)} %bitcast.89, ...), custom_call_target="tpu_custom_call" | custom-call | flops 1073741824 | bytes 8388608 | tf_op jit(solution)/shard_map/pallas_call | solution.py:118
  108.8 2.9 %collective-permute-start.27 = (f32[3,512]{1,0:T(4,128)S(1)}, f32[3,512]{1,0:T(4,128)S(1)}, u32[]{:S(2)}, u32[]{:S(2)}) collective-permute-start(f32[3,512]{1,0:T(4,128)S(1)} %get-tuple-element.39), channel_id=1, source_target_pairs={{2,0},{4,2},{6,4},{0,6},{3,1},{5,3},{7,5},{1,7},{10,8},{12,10},{14... | collective-permute-start | bytes 18440 | tf_op jit(solution)/shard_map/ppermute | solution.py:446
  115.1 1.9 collective-permute-start.23
  120.2 8.6 %collective-permute-done.18.refs_5_ = bf16[256,1024]{1,0:T(8,128)(2,1)} collective-permute-done((bf16[256,1024]{1,0:T(8,128)(2,1)}, bf16[256,1024]{1,0:T(8,128)(2,1)}, u32[]{:S(2)}, u32[]{:S(2)}) %collective-permute-start.18) | collective-permute-done | bytes 524320 | tf_op jit(solution)/shard_map/ppermute | solution.py:32
  136.4 15.0 %shard_map.186 = (f32[4,192,1536]{2,1,0:T(8,128)S(1)}, f32[4,192,1536]{2,1,0:T(8,128)S(1)}, f32[4,1,128]{2,1,0:T(1,128)S(1)}, f32[256,768]{1,0:T(8,128)S(1)}, bf16[256,1536]{1,0:T(8,128)(2,1)S(1)}) custom-call(s32[1]{0:T(128)} %bitcast.17.place_ref, bf16[4,272,768]{2,1,0:T(8,128)(2,1)S(1)} %pad_maximum_fusion.mine_ref, ...), custom_call_target="tpu_custom_call" | custom-call | flops 6039797760 | bytes 25165824 | tf_op jit(solution)/shard_map/pallas_call | solution.py:289
  151.4 2.1 %copy-done.3 = f32[4,192,1536]{2,1,0:T(8,128)} copy-done((f32[4,192,1536]{2,1,0:T(8,128)}, f32[4,192,1536]{2,1,0:T(8,128)S(1)}, u32[]{:S(2)}) %copy-start.3) | copy-done | bytes 4718616
  153.5 2.1 %copy-done.5 = f32[4,192,1536]{2,1,0:T(8,128)} copy-done((f32[4,192,1536]{2,1,0:T(8,128)}, f32[4,192,1536]{2,1,0:T(8,128)S(1)}, u32[]{:S(2)}) %copy-start.5) | copy-done | bytes 4718616
  155.7 1.7 fusion.25
  164.8 5.6 %multiply_add_fusion.1 = f32[1,192,1536]{2,1,0:T(8,128)S(1)} fusion(f32[4,192,1536]{2,1,0:T(8,128)} %copy-done.5, f32[]{:T(128)} %bitcast.40, f32[]{:T(128)} %bitcast.39, f32[]{:T(128)} %bitcast.38, f32[]{:T(128)} %bitcast.33), kind=kLoop, calls=%fused_computation.4 | loop fusion | flops 2064384 | bytes 5898256 | tf_op jit(solution)/shard_map/add | solution.py:474
  171.8 3.6 %multiply_add_fusion = f32[1,192,1536]{2,1,0:T(8,128)S(1)} fusion(f32[4,192,1536]{2,1,0:T(8,128)S(1)} %copy-done.4, f32[]{:T(128)} %bitcast.40, f32[]{:T(128)} %bitcast.39, f32[]{:T(128)} %bitcast.38, f32[]{:T(128)} %bitcast.33), kind=kLoop, calls=%fused_computation.3 | loop fusion | flops 2064384 | bytes 5898256 | tf_op jit(solution)/shard_map/add | solution.py:474
  176.7 7.1 %shard_map.187.refs_0_ = f32[512,1024]{1,0:T(8,128)S(1)} custom-call(s32[11]{0:T(128)S(1)} %stack.111.places_ref, bf16[512,4096]{1,0:T(8,128)(2,1)S(1)} %bitcast.92, bf16[1024,1024]{1,0:T(8,128)(2,1)S(1)} %copy-done.7, bf16[512,4096]{1,0:T(8,128)(2,1)S(1)} %bitcast.93, bf16[256,1024]{1,0:T(8,128)(2,1)} %collective-permute-done.3.refs_3_, ...), custom_call_target="tpu_custom_call" | custom-call | flops 3758096384 | bytes 8388608 | tf_op jit(solution)/shard_map/pallas_call | solution.py:118
  186.0 2.9 %fusion.1 = bf16[1,256,768]{2,1,0:T(8,128)(2,1)} fusion(f32[256,768]{1,0:T(8,128)} %collective-permute-done.26, f32[256,768]{1,0:T(8,128)S(1)} %copy-done.9, f32[256,768]{1,0:T(8,128)} %fusion.25, f32[]{:T(128)} %bitcast.33), kind=kLoop, calls=%fused_computation.13 | loop fusion | flops 786432 | bytes 2752516 | tf_op jit(solution)/shard_map/broadcast_in_dim | solution.py:469
  188.9 3.9 %shard_map.188 = f32[32,1024]{1,0:T(8,128)S(1)} custom-call(s32[2]{0:T(128)S(1)} %pad_add_fusion.places_ref, f32[512,1024]{1,0:T(8,128)S(1)} %shard_map.187.refs_0_, bf16[512,4096]{1,0:T(8,128)(2,1)S(1)} %bitcast.103, bf16[256,1024]{1,0:T(8,128)(2,1)S(1)} %collective-permute-done.31.refs_2_, bf16[512,4096]{1,0:T(8,128)(2,1)S(1)} %bitcast.104, ...), custom_call_target="tpu_custom_call" | custom-call | flops 536870912 | bytes 8388608 | tf_op jit(solution)/shard_map/pallas_call | solution.py:118
  195.0 2.1 %collective-permute-done.33 = bf16[32,1024]{1,0:T(8,128)(2,1)S(1)} collective-permute-done((bf16[32,1024]{1,0:T(8,128)(2,1)S(1)}, bf16[32,1024]{1,0:T(8,128)(2,1)S(1)}, u32[]{:S(2)}, u32[]{:S(2)}) %collective-permute-start.33) | collective-permute-done | bytes 65568 | tf_op jit(solution)/shard_map/ppermute | solution.py:508
  197.2 2.9 %collective-permute-start.34 = (bf16[32,1024]{1,0:T(8,128)(2,1)S(1)}, bf16[32,1024]{1,0:T(8,128)(2,1)S(1)}, u32[]{:S(2)}, u32[]{:S(2)}) collective-permute-start(bf16[32,1024]{1,0:T(8,128)(2,1)S(1)} %add_convert_fusion.1), channel_id=1, source_target_pairs={{0,4},{2,6},{4,0},{6,2},{1,5},{3,7},{5,1},{7,3},{8,12},{10,14},{12... | collective-permute-start | bytes 196616 | tf_op jit(solution)/shard_map/ppermute | solution.py:508
  (183 shorter events, 61.1 us)
Async XLA Ops:
  1.8 15.3 %collective-permute-start = (bf16[256,1024]{1,0:T(8,128)(2,1)S(1)}, bf16[256,1024]{1,0:T(8,128)(2,1)S(1)}, u32[]{:S(2)}, u32[]{:S(2)}) collective-permute-start(bf16[256,1024]{1,0:T(8,128)(2,1)S(1)} %constant_dynamic-slice_fusion.1), channel_id=1, source_target_pairs={{0,4},{4,6},{6,2},{2,0},{1,5},{5,7},{7,3},{3,1},{8,12},{12,14},{14... | collective-permute-start | bytes 1572872 | tf_op jit(solution)/shard_map/ppermute | solution.py:316
  17.1 13.7 %collective-permute-start.1 = (bf16[256,1024]{1,0:T(8,128)(2,1)S(1)}, bf16[256,1024]{1,0:T(8,128)(2,1)}, u32[]{:S(2)}, u32[]{:S(2)}) collective-permute-start(bf16[256,1024]{1,0:T(8,128)(2,1)S(1)} %collective-permute-done.refs_3_), channel_id=1, source_target_pairs={{0,4},{4,6},{6,2},{2,0},{1,5},{5,7},{7,3},{3,1},{8,12},{12,14},{14... | collective-permute-start | bytes 1572872 | tf_op jit(solution)/shard_map/ppermute | solution.py:316
  30.8 13.2 %collective-permute-start.2 = (bf16[256,1024]{1,0:T(8,128)(2,1)}, bf16[256,1024]{1,0:T(8,128)(2,1)S(1)}, u32[]{:S(2)}, u32[]{:S(2)}) collective-permute-start(bf16[256,1024]{1,0:T(8,128)(2,1)} %collective-permute-done.1.refs_2_), channel_id=1, source_target_pairs={{0,4},{4,6},{6,2},{2,0},{1,5},{5,7},{7,3},{3,1},{8,12},{12,14},{14... | collective-permute-start | bytes 1572872 | tf_op jit(solution)/shard_map/ppermute | solution.py:316
  34.9 14.9 %collective-permute-start.8 = (bf16[256,1024]{1,0:T(8,128)(2,1)S(1)}, bf16[256,1024]{1,0:T(8,128)(2,1)S(1)}, u32[]{:S(2)}, u32[]{:S(2)}) collective-permute-start(bf16[256,1024]{1,0:T(8,128)(2,1)S(1)} %collective-permute-done.refs_3_), channel_id=1, source_target_pairs={{0,8},{8,0},{16,24},{24,16},{1,9},{9,1},{17,25},{25,17},{2,10},{10... | collective-permute-start | bytes 1572872 | tf_op jit(solution)/shard_map/ppermute | solution.py:32
  36.4 15.0 %collective-permute-start.9 = (bf16[256,1024]{1,0:T(8,128)(2,1)S(1)}, bf16[256,1024]{1,0:T(8,128)(2,1)}, u32[]{:S(2)}, u32[]{:S(2)}) collective-permute-start(bf16[256,1024]{1,0:T(8,128)(2,1)S(1)} %collective-permute-done.refs_3_), channel_id=1, source_target_pairs={{0,16},{8,24},{16,0},{24,8},{1,17},{9,25},{17,1},{25,9},{2,18},{10... | collective-permute-start | bytes 1572872 | tf_op jit(solution)/shard_map/ppermute | solution.py:32
  39.8 21.3 %collective-permute-start.11 = (bf16[256,1024]{1,0:T(8,128)(2,1)}, bf16[256,1024]{1,0:T(8,128)(2,1)}, u32[]{:S(2)}, u32[]{:S(2)}) collective-permute-start(bf16[256,1024]{1,0:T(8,128)(2,1)} %collective-permute-done.1.refs_2_), channel_id=1, source_target_pairs={{0,8},{8,0},{16,24},{24,16},{1,9},{9,1},{17,25},{25,17},{2,10},{10... | collective-permute-start | bytes 1572872 | tf_op jit(solution)/shard_map/ppermute | solution.py:32
  40.3 22.3 %collective-permute-start.12 = (bf16[256,1024]{1,0:T(8,128)(2,1)}, bf16[256,1024]{1,0:T(8,128)(2,1)}, u32[]{:S(2)}, u32[]{:S(2)}) collective-permute-start(bf16[256,1024]{1,0:T(8,128)(2,1)} %collective-permute-done.1.refs_2_), channel_id=1, source_target_pairs={{0,16},{8,24},{16,0},{24,8},{1,17},{9,25},{17,1},{25,9},{2,18},{10... | collective-permute-start | bytes 1572872 | tf_op jit(solution)/shard_map/ppermute | solution.py:32
  43.9 20.2 %collective-permute-start.3 = (bf16[256,1024]{1,0:T(8,128)(2,1)}, bf16[256,1024]{1,0:T(8,128)(2,1)}, u32[]{:S(2)}, u32[]{:S(2)}) collective-permute-start(bf16[256,1024]{1,0:T(8,128)(2,1)} %constant_dynamic-slice_fusion.2), channel_id=1, source_target_pairs={{0,4},{4,6},{6,2},{2,0},{1,5},{5,7},{7,3},{3,1},{8,12},{12,14},{14... | collective-permute-start | bytes 1572872 | tf_op jit(solution)/shard_map/ppermute | solution.py:316
  51.3 21.0 %collective-permute-start.10 = (bf16[256,1024]{1,0:T(8,128)(2,1)}, bf16[256,1024]{1,0:T(8,128)(2,1)}, u32[]{:S(2)}, u32[]{:S(2)}) collective-permute-start(bf16[256,1024]{1,0:T(8,128)(2,1)} %collective-permute-done.9.refs_7_), channel_id=1, source_target_pairs={{0,8},{8,0},{16,24},{24,16},{1,9},{9,1},{17,25},{25,17},{2,10},{10... | collective-permute-start | bytes 1572872 | tf_op jit(solution)/shard_map/ppermute | solution.py:32
  52.0 21.8 %collective-permute-start.15 = (bf16[256,1024]{1,0:T(8,128)(2,1)S(1)}, bf16[256,1024]{1,0:T(8,128)(2,1)}, u32[]{:S(2)}, u32[]{:S(2)}) collective-permute-start(bf16[256,1024]{1,0:T(8,128)(2,1)S(1)} %collective-permute-done.2.refs_2_), channel_id=1, source_target_pairs={{0,16},{8,24},{16,0},{24,8},{1,17},{9,25},{17,1},{25,9},{2,18},{10... | collective-permute-start | bytes 1572872 | tf_op jit(solution)/shard_map/ppermute | solution.py:32
  62.6 18.8 %collective-permute-start.13 = (bf16[256,1024]{1,0:T(8,128)(2,1)}, bf16[256,1024]{1,0:T(8,128)(2,1)S(1)}, u32[]{:S(2)}, u32[]{:S(2)}) collective-permute-start(bf16[256,1024]{1,0:T(8,128)(2,1)} %collective-permute-done.11.refs_4_), channel_id=1, source_target_pairs={{0,16},{8,24},{16,0},{24,8},{1,17},{9,25},{17,1},{25,9},{2,18},{10... | collective-permute-start | bytes 1572872 | tf_op jit(solution)/shard_map/ppermute | solution.py:32
  64.1 14.1 %collective-permute-start.4 = (bf16[256,1024]{1,0:T(8,128)(2,1)}, bf16[256,1024]{1,0:T(8,128)(2,1)}, u32[]{:S(2)}, u32[]{:S(2)}) collective-permute-start(bf16[256,1024]{1,0:T(8,128)(2,1)} %collective-permute-done.3.refs_3_), channel_id=1, source_target_pairs={{0,4},{4,6},{6,2},{2,0},{1,5},{5,7},{7,3},{3,1},{8,12},{12,14},{14... | collective-permute-start | bytes 1572872 | tf_op jit(solution)/shard_map/ppermute | solution.py:316
  64.7 22.9 %collective-permute-start.14 = (bf16[256,1024]{1,0:T(8,128)(2,1)S(1)}, bf16[256,1024]{1,0:T(8,128)(2,1)}, u32[]{:S(2)}, u32[]{:S(2)}) collective-permute-start(bf16[256,1024]{1,0:T(8,128)(2,1)S(1)} %collective-permute-done.2.refs_2_), channel_id=1, source_target_pairs={{0,8},{8,0},{16,24},{24,16},{1,9},{9,1},{17,25},{25,17},{2,10},{10... | collective-permute-start | bytes 1572872 | tf_op jit(solution)/shard_map/ppermute | solution.py:32
  73.8 28.1 %collective-permute-start.16 = (bf16[256,1024]{1,0:T(8,128)(2,1)}, bf16[256,1024]{1,0:T(8,128)(2,1)}, u32[]{:S(2)}, u32[]{:S(2)}) collective-permute-start(bf16[256,1024]{1,0:T(8,128)(2,1)} %collective-permute-done.15.refs_6_), channel_id=1, source_target_pairs={{0,8},{8,0},{16,24},{24,16},{1,9},{9,1},{17,25},{25,17},{2,10},{10... | collective-permute-start | bytes 1572872 | tf_op jit(solution)/shard_map/ppermute | solution.py:32
  78.2 30.3 %collective-permute-start.7 = (bf16[272,768]{1,0:T(8,128)(2,1)}, bf16[272,768]{1,0:T(8,128)(2,1)}, u32[]{:S(2)}, u32[]{:S(2)}) collective-permute-start(bf16[272,768]{1,0:T(8,128)(2,1)} %concatenate.11), channel_id=1, source_target_pairs={{6,0},{0,2},{2,4},{4,6},{7,1},{1,3},{3,5},{5,7},{14,8},{8,10},{10,... | collective-permute-start | bytes 1253384 | tf_op jit(solution)/shard_map/ppermute | solution.py:385
  78.2 30.6 %collective-permute-start.6 = (bf16[272,768]{1,0:T(8,128)(2,1)}, bf16[272,768]{1,0:T(8,128)(2,1)}, u32[]{:S(2)}, u32[]{:S(2)}) collective-permute-start(bf16[272,768]{1,0:T(8,128)(2,1)} %concatenate.11), channel_id=1, source_target_pairs={{4,0},{6,2},{0,4},{2,6},{5,1},{7,3},{1,5},{3,7},{12,8},{14,10},{8,... | collective-permute-start | bytes 1253384 | tf_op jit(solution)/shard_map/ppermute | solution.py:385
  82.2 29.5 %collective-permute-start.5 = (bf16[272,768]{1,0:T(8,128)(2,1)}, bf16[272,768]{1,0:T(8,128)(2,1)}, u32[]{:S(2)}, u32[]{:S(2)}) collective-permute-start(bf16[272,768]{1,0:T(8,128)(2,1)} %concatenate.11), channel_id=1, source_target_pairs={{2,0},{4,2},{6,4},{0,6},{3,1},{5,3},{7,5},{1,7},{10,8},{12,10},{14... | collective-permute-start | bytes 1253384 | tf_op jit(solution)/shard_map/ppermute | solution.py:385
  87.6 26.0 %collective-permute-start.19 = (bf16[256,1024]{1,0:T(8,128)(2,1)}, bf16[256,1024]{1,0:T(8,128)(2,1)}, u32[]{:S(2)}, u32[]{:S(2)}) collective-permute-start(bf16[256,1024]{1,0:T(8,128)(2,1)} %collective-permute-done.3.refs_3_), channel_id=1, source_target_pairs={{0,16},{8,24},{16,0},{24,8},{1,17},{9,25},{17,1},{25,9},{2,18},{10... | collective-permute-start | bytes 1572872 | tf_op jit(solution)/shard_map/ppermute | solution.py:32
  113.3 18.8 %collective-permute-start.17 = (bf16[4,272,768]{2,1,0:T(8,128)(2,1)S(1)}, bf16[4,272,768]{2,1,0:T(8,128)(2,1)}, u32[]{:S(2)}, u32[]{:S(2)}) collective-permute-start(bf16[4,272,768]{2,1,0:T(8,128)(2,1)S(1)} %pad_maximum_fusion.mine_ref), channel_id=1, source_target_pairs={{0,1},{1,0},{2,3},{3,2},{4,5},{5,4},{6,7},{7,6},{8,9},{9,8},{10,11... | collective-permute-start | bytes 5013512 | tf_op jit(solution)/shard_map/ppermute | solution.py:404
  113.7 15.1 %collective-permute-start.18 = (bf16[256,1024]{1,0:T(8,128)(2,1)}, bf16[256,1024]{1,0:T(8,128)(2,1)}, u32[]{:S(2)}, u32[]{:S(2)}) collective-permute-start(bf16[256,1024]{1,0:T(8,128)(2,1)} %collective-permute-done.3.refs_3_), channel_id=1, source_target_pairs={{0,8},{8,0},{16,24},{24,16},{1,9},{9,1},{17,25},{25,17},{2,10},{10... | collective-permute-start | bytes 1572872 | tf_op jit(solution)/shard_map/ppermute | solution.py:32
  114.4 14.4 %collective-permute-start.20 = (bf16[256,1024]{1,0:T(8,128)(2,1)}, bf16[256,1024]{1,0:T(8,128)(2,1)S(1)}, u32[]{:S(2)}, u32[]{:S(2)}) collective-permute-start(bf16[256,1024]{1,0:T(8,128)(2,1)} %collective-permute-done.4.refs_11_), channel_id=1, source_target_pairs={{0,16},{8,24},{16,0},{24,8},{1,17},{9,25},{17,1},{25,9},{2,18},{10... | collective-permute-start | bytes 1572872 | tf_op jit(solution)/shard_map/ppermute | solution.py:32
  115.1 14.5 %collective-permute-start.23 = (bf16[256,1024]{1,0:T(8,128)(2,1)}, bf16[256,1024]{1,0:T(8,128)(2,1)}, u32[]{:S(2)}, u32[]{:S(2)}) collective-permute-start(bf16[256,1024]{1,0:T(8,128)(2,1)} %collective-permute-done.4.refs_11_), channel_id=1, source_target_pairs={{0,4},{4,6},{6,2},{2,0},{1,5},{5,7},{7,3},{3,1},{8,12},{12,14},{14... | collective-permute-start | bytes 1572872 | tf_op jit(solution)/shard_map/ppermute | solution.py:316
  118.4 39.3 %collective-permute-start.22 = (bf16[256,1024]{1,0:T(8,128)(2,1)}, bf16[256,1024]{1,0:T(8,128)(2,1)}, u32[]{:S(2)}, u32[]{:S(2)}) collective-permute-start(bf16[256,1024]{1,0:T(8,128)(2,1)} %collective-permute-done.4.refs_11_), channel_id=1, source_target_pairs={{0,8},{8,0},{16,24},{24,16},{1,9},{9,1},{17,25},{25,17},{2,10},{10... | collective-permute-start | bytes 1572872 | tf_op jit(solution)/shard_map/ppermute | solution.py:32
  128.8 46.7 %collective-permute-start.21 = (bf16[256,1024]{1,0:T(8,128)(2,1)}, bf16[256,1024]{1,0:T(8,128)(2,1)}, u32[]{:S(2)}, u32[]{:S(2)}) collective-permute-start(bf16[256,1024]{1,0:T(8,128)(2,1)} %collective-permute-done.18.refs_5_), channel_id=1, source_target_pairs={{0,16},{8,24},{16,0},{24,8},{1,17},{9,25},{17,1},{25,9},{2,18},{10... | collective-permute-start | bytes 1572872 | tf_op jit(solution)/shard_map/ppermute | solution.py:32
  129.6 34.3 %collective-permute-start.24 = (bf16[256,1024]{1,0:T(8,128)(2,1)}, bf16[256,1024]{1,0:T(8,128)(2,1)}, u32[]{:S(2)}, u32[]{:S(2)}) collective-permute-start(bf16[256,1024]{1,0:T(8,128)(2,1)} %collective-permute-done.23.refs_17_), channel_id=1, source_target_pairs={{0,8},{8,0},{16,24},{24,16},{1,9},{9,1},{17,25},{25,17},{2,10},{10... | collective-permute-start | bytes 1572872 | tf_op jit(solution)/shard_map/ppermute | solution.py:32
  130.9 26.8 %collective-permute-start.25 = (bf16[256,1024]{1,0:T(8,128)(2,1)}, bf16[256,1024]{1,0:T(8,128)(2,1)S(1)}, u32[]{:S(2)}, u32[]{:S(2)}) collective-permute-start(bf16[256,1024]{1,0:T(8,128)(2,1)} %collective-permute-done.23.refs_17_), channel_id=1, source_target_pairs={{0,16},{8,24},{16,0},{24,8},{1,17},{9,25},{17,1},{25,9},{2,18},{10... | collective-permute-start | bytes 1572872 | tf_op jit(solution)/shard_map/ppermute | solution.py:32
  157.4 28.6 %collective-permute-start.26 = (f32[256,768]{1,0:T(8,128)}, f32[256,768]{1,0:T(8,128)}, u32[]{:S(2)}, u32[]{:S(2)}) collective-permute-start(f32[256,768]{1,0:T(8,128)} %fusion.25), channel_id=1, source_target_pairs={{0,1},{1,0},{2,3},{3,2},{4,5},{5,4},{6,7},{7,6},{8,9},{9,8},{10,11... | collective-permute-start | bytes 2359304 | tf_op jit(solution)/shard_map/ppermute | solution.py:440
  158.5 30.4 %collective-permute-start.31 = (bf16[256,1024]{1,0:T(8,128)(2,1)S(1)}, bf16[256,1024]{1,0:T(8,128)(2,1)S(1)}, u32[]{:S(2)}, u32[]{:S(2)}) collective-permute-start(bf16[256,1024]{1,0:T(8,128)(2,1)S(1)} %collective-permute-done.20.refs_15_), channel_id=1, source_target_pairs={{0,8},{8,0},{16,24},{24,16},{1,9},{9,1},{17,25},{25,17},{2,10},{10... | collective-permute-start | bytes 1572872 | tf_op jit(solution)/shard_map/ppermute | solution.py:32
  163.9 25.0 %collective-permute-start.32 = (bf16[256,1024]{1,0:T(8,128)(2,1)}, bf16[256,1024]{1,0:T(8,128)(2,1)S(1)}, u32[]{:S(2)}, u32[]{:S(2)}) collective-permute-start(bf16[256,1024]{1,0:T(8,128)(2,1)} %collective-permute-done.24.refs_19_), channel_id=1, source_target_pairs={{0,16},{8,24},{16,0},{24,8},{1,17},{9,25},{17,1},{25,9},{2,18},{10... | collective-permute-start | bytes 1572872 | tf_op jit(solution)/shard_map/ppermute | solution.py:32
  170.5 13.4 %collective-permute-start.35 = (bf16[2,1,48,1536]{3,2,1,0:T(8,128)(2,1)S(1)}, bf16[2,1,48,1536]{3,2,1,0:T(8,128)(2,1)S(1)}, u32[]{:S(2)}, u32[]{:S(2)}) collective-permute-start(bf16[2,1,48,1536]{3,2,1,0:T(8,128)(2,1)S(1)} %fusion.3), channel_id=1, source_target_pairs={{0,8},{8,0},{16,24},{24,16},{1,9},{9,1},{17,25},{25,17},{2,10},{10... | collective-permute-start | bytes 884744 | tf_op jit(solution)/shard_map/ppermute | solution.py:32
  184.0 10.3 %collective-permute-start.36 = (bf16[1,1,48,1536]{3,2,1,0:T(8,128)(2,1)S(1)}, bf16[1,1,48,1536]{3,2,1,0:T(8,128)(2,1)S(1)}, u32[]{:S(2)}, u32[]{:S(2)}) collective-permute-start(bf16[1,1,48,1536]{3,2,1,0:T(8,128)(2,1)S(1)} %dynamic-slice_convert_fusion.2), channel_id=1, source_target_pairs={{0,16},{8,24},{16,0},{24,8},{1,17},{9,25},{17,1},{25,9},{2,18},{10... | collective-permute-start | bytes 442376 | tf_op jit(solution)/shard_map/ppermute | solution.py:32
  185.0 15.2 %collective-permute-start.38 = (bf16[1,1,48,1536]{3,2,1,0:T(8,128)(2,1)S(1)}, bf16[1,1,48,1536]{3,2,1,0:T(8,128)(2,1)S(1)}, u32[]{:S(2)}, u32[]{:S(2)}) collective-permute-start(bf16[1,1,48,1536]{3,2,1,0:T(8,128)(2,1)S(1)} %dynamic-slice_convert_fusion.1), channel_id=1, source_target_pairs={{0,8},{8,0},{16,24},{24,16},{1,9},{9,1},{17,25},{25,17},{2,10},{10... | collective-permute-start | bytes 442376 | tf_op jit(solution)/shard_map/ppermute | solution.py:32
  (38 other events, 414.1 us)
